TPU v7x, 32 devices: a whole 2x2x4 slice. The times are simulated.
32 devices in a mesh: rows: 8 (over z, core), cols: 4 (over y, x).
Axes of the slice: x: 2, y: 2, z: 4, core: 2. Of those that a mesh axis runs over, the one named last changes fastest.
Arguments:
- window_slab: float32 [24576, 4096], P('rows', 'cols'), may hold values from -6 to 6
- first_inverse: float32 [2, 512, 512], replicated, may hold values from -2 to 2, as said below
- first_factor: float32 [2, 512, 24576], P(None, 'cols', 'rows'), may hold values from -0.25 to 0.25
- second_inverse: float32 [2, 512, 512], replicated, may hold values from -2 to 2, as said below
- second_factor: float32 [2, 512, 4096], P(None, 'cols', 'rows'), may hold values from -0.25 to 0.25
Outputs:
- reduced: float32 [24576, 4096], P('cols', 'rows')
Inputs may be any that keep to these rules, and one draw needn't show every extreme that they name: first_inverse[k] is lower triangular with diagonal entries from 0.5 to 2. second_inverse[k] is lower triangular with diagonal entries from 0.5 to 2.
All inputs are finite; a program needn't handle non-finite values.
Results may differ from a plain program's by a relative error of at most 0.0001.
Values sent between devices are 32-bit elements; how exact they have to be, the bound alone decides.
No kernel may reach another device: no remote copies, remote signals or barrier semaphores. Data moves between devices by JAX's collectives and lax.ppermute only.
A program may use at most 128 MiB of HBM per device.

v0:
```python
import jax
import jax.numpy as jnp
from jax import lax
from jax.sharding import PartitionSpec as P

BLOCK = 128


HIGHEST = lax.Precision.HIGHEST
CONTRACT_ROWS = (((0,), (0,)), ((), ()))
CONTRACT_COLS = (((1,), (1,)), ((), ()))


def right_solve(current, first_column, inverses, total_of, update_of):
    height, breadth = current.shape
    panel_count = inverses.shape[0]
    panel_width = inverses.shape[1]
    portion = min(breadth, panel_width)
    columns = first_column + lax.broadcasted_iota(jnp.int32, (1, breadth), 1)
    for panel_index in range(panel_count):
        panel_start = panel_index * panel_width
        panel_end = panel_start + panel_width
        inner_offset = jnp.clip(first_column - panel_start, 0, panel_width - portion)
        member = jnp.logical_and(first_column < panel_end, first_column + breadth > panel_start)
        own_columns = current
        inverse_cols = lax.dynamic_slice_in_dim(inverses[panel_index], inner_offset, portion, 1)
        partial_value = lax.dot_general(
            own_columns,
            inverse_cols,
            CONTRACT_COLS,
            precision=HIGHEST,
            preferred_element_type=jnp.float32,
        )
        solved = total_of(jnp.where(member, partial_value, 0.0))
        update = update_of(panel_index, solved)
        current = jnp.where(columns >= panel_end, current - update, current)
        mine_cols = lax.dynamic_slice_in_dim(solved, inner_offset, portion, 1)
        present = current
        current = jnp.where(member, mine_cols, present)
    return current


def on_device(window_slab, first_inverse, first_factor, second_inverse, second_factor):
    row_count = lax.axis_size("rows")
    row_index = lax.axis_index("rows")
    row_share, breadth = window_slab.shape
    panel_count = first_inverse.shape[0]
    panel_width = first_inverse.shape[1]
    blocks_per_panel = panel_width // BLOCK
    local_rows = lax.broadcasted_iota(jnp.int32, (row_share, 1), 0)
    logical_rows = (local_rows // BLOCK * row_count + row_index) * BLOCK + local_rows % BLOCK
    current = window_slab
    for panel_index in range(panel_count):
        panel_start = panel_index * panel_width
        panel_end = panel_start + panel_width
        local_block = panel_start // (row_count * BLOCK)
        first_group = panel_start // BLOCK % row_count
        member = jnp.logical_and(
            row_index >= first_group, row_index < first_group + blocks_per_panel
        )
        offset = jnp.clip(row_index - first_group, 0, blocks_per_panel - 1) * BLOCK
        own_rows = current[local_block * BLOCK : (local_block + 1) * BLOCK]
        inverse_cols = lax.dynamic_slice_in_dim(first_inverse[panel_index], offset, BLOCK, 1)
        partial_value = jnp.dot(
            inverse_cols, own_rows, precision=HIGHEST, preferred_element_type=jnp.float32
        )
        solved = lax.psum(jnp.where(member, partial_value, 0.0), "rows")
        update = lax.dot_general(
            lax.all_gather(first_factor[panel_index], "cols", axis=0, tiled=True),
            solved,
            CONTRACT_ROWS,
            precision=HIGHEST,
            preferred_element_type=jnp.float32,
        )
        current = jnp.where(logical_rows >= panel_end, current - update, current)
        mine_rows = lax.dynamic_slice_in_dim(solved, offset, BLOCK, 0)
        present = current[local_block * BLOCK : (local_block + 1) * BLOCK]
        current = lax.dynamic_update_slice_in_dim(
            current, jnp.where(member, mine_rows, present), local_block * BLOCK, 0
        )
    turned = lax.all_to_all(
        lax.all_to_all(current, "cols", split_axis=0, concat_axis=1, tiled=True),
        "rows",
        split_axis=1,
        concat_axis=0,
        tiled=True,
    )
    height, narrow = turned.shape

    def total_rows(partial_sum):
        return lax.psum(partial_sum, "rows")

    def update_rows(panel_number, solved_cols):
        return jnp.dot(
            solved_cols,
            lax.all_gather(second_factor[panel_number], "cols", axis=0, tiled=True),
            precision=HIGHEST,
            preferred_element_type=jnp.float32,
        )

    reduced = right_solve(turned, row_index * narrow, second_inverse, total_rows, update_rows)
    return reduced


def solution(mesh):
    return jax.shard_map(
        on_device,
        mesh=mesh,
        in_specs=(P("rows", "cols"), P(), P(None, "cols", "rows"), P(), P(None, "cols", "rows")),
        out_specs=P("cols", "rows"),
        check_vma=False,
    )
```

profile of v0, /device:TPU:0, one launch (start us, length us, event | category | flops | bytes accessed | tf_op | source)
XLA Modules:
  0.0 1294.2 jit_solution(16294437218668161970)
XLA Ops:
  7.4 1.7 fusion.33
  9.1 4.2 convolution_select_fusion.3
  13.3 0.0 all-gather.9.cloned.1.call-start
  13.3 3.9 fusion.32
  17.2 0.0 all-gather.11.cloned.1.call-start
  17.3 0.5 all-gather.11.cloned.1.call-update
  17.9 63.1 %all-reduce.5.cloned.1.call-done = f32[512,1024]{1,0:T(8,128)} async-done(((f32[512,1024]{1,0:T(8,128)}), f32[512,1024]{1,0:T(8,128)}) %all-reduce.5.cloned.1.call-update) | async-done | bytes 2097168 | tf_op jit(solution)/shard_map/psum | solution.py:67
  81.0 9.0 all-gather.9.cloned.1.call-done
  90.0 26.3 %subtract_select_fusion.3 = f32[3072,1024]{1,0:T(8,128)S(1)} fusion(f32[3072,1024]{1,0:T(8,128)} %param.5, f32[512,1024]{1,0:T(8,128)} %all-reduce.5.cloned.1.call-done, f32[1,512,3072]{2,1,0:T(8,128)} %all-gather.9.cloned.1.call-done, pred[3072]{0:T(1024)(128)(4,1)S(1)} %broadcast_compare_fusion), kind=kOutput, calls=%fused_computation.3 | convolution fusion | flops 19333644288 | bytes 33557504 | tf_op jit(solution)/shard_map/dot_general | solution.py:68
  116.3 4.8 copy-done.1
  121.1 3.2 convolution_select_fusion.2
  124.3 1.9 fusion.16
  126.2 35.5 %all-gather.11.cloned.1.call-done = f32[1,512,3072]{2,1,0:T(8,128)} async-done(((f32[1,128,3072]{2,1,0:T(8,128)}), f32[1,512,3072]{2,1,0:T(8,128)}) %all-gather.11.cloned.1.call-update) | async-done | bytes 6291472 | tf_op jit(solution)/shard_map/all_gather | solution.py:69
  161.7 27.6 %all-reduce.7.cloned.1.call-done = f32[512,1024]{1,0:T(8,128)} async-done(((f32[512,1024]{1,0:T(8,128)}), f32[512,1024]{1,0:T(8,128)}) %all-reduce.7.cloned.1.call-update) | async-done | bytes 2097168 | tf_op jit(solution)/shard_map/psum | solution.py:67
  189.3 26.8 %subtract_select_fusion.2 = f32[3072,1024]{1,0:T(8,128)} fusion(f32[3072,1024]{1,0:T(8,128)} %fusion.16, f32[512,1024]{1,0:T(8,128)} %all-reduce.7.cloned.1.call-done, f32[1,512,3072]{2,1,0:T(8,128)} %all-gather.11.cloned.1.call-done, pred[3072]{0:T(1024)(128)(4,1)S(1)} %broadcast_compare_fusion.1), kind=kOutput, calls=%fused_computation.2 | convolution fusion | flops 19333644288 | bytes 33557504 | tf_op jit(solution)/shard_map/dot_general | solution.py:68
  216.1 2.1 fusion.10
  218.1 12.6 copy.10
  230.8 145.9 %all_to_all.35 = f32[4,768,1024]{1,2,0:T(8,128)} all-to-all(f32[4,768,1024]{1,2,0:T(8,128)} %copy.10), channel_id=1, replica_groups=mesh['rows'=8,'cols'=4] {'cols'}, dimensions={0} | all-to-all | bytes 25165824 | tf_op jit(solution)/shard_map/all_to_all | solution.py:82
  376.7 5.5 all-to-all-start.1
  382.2 0.0 all-gather.13.cloned.1.call-start
  382.2 0.8 fusion.34
  383.1 272.8 %all-to-all-done.1 = f32[768,8,512]{0,2,1:T(8,128)} async-done(((f32[768,8,512]{0,2,1:T(8,128)}), f32[768,8,512]{0,2,1:T(8,128)}, u32[]{:S(2)}, u32[]{:S(2)}) %all-to-all-start.1) | async-done | bytes 12582944 | tf_op jit(solution)/shard_map/all_to_all | solution.py:81
  655.9 12.9 copy.11
  668.8 24.3 %convolution_select_fusion.1 = f32[6144,512]{1,0:T(8,128)} fusion(f32[6144,512]{1,0:T(8,128)} %bitcast.40, pred[]{:T(512)S(6)} %and.53, f32[2,512,512]{2,1,0:T(8,128)S(1)} %copy-done.3), kind=kOutput, calls=%fused_computation.7 | convolution fusion | flops 19330498560 | bytes 26214400 | tf_op jit(solution)/shard_map/dot_general | solution.py:27
  693.2 0.0 all-gather.15.cloned.1.call-start
  693.2 0.7 all-gather.15.cloned.1.call-update
  694.0 251.3 %all-reduce.9.cloned.1.call-done = f32[6144,512]{1,0:T(8,128)} async-done(((f32[6144,512]{1,0:T(8,128)}), f32[6144,512]{1,0:T(8,128)}) %all-reduce.9.cloned.1.call-update) | async-done | bytes 12582928 | tf_op jit(solution)/shard_map/psum | solution.py:91
  945.3 28.2 %fusion = f32[6144,512]{1,0:T(8,128)S(1)} fusion(f32[6144,512]{1,0:T(8,128)} %all-reduce.9.cloned.1.call-done, f32[6144,512]{1,0:T(8,128)} %bitcast.41, pred[512]{0:T(512)(128)(4,1)S(1)} %fusion.29, pred[]{:T(512)S(6)} %and.53, f32[1,512,512]{2,1,0:T(8,128)} %all-gather.13.cloned.1.call-done), kind=kOutput, calls=%fused_computation.4 | convolution fusion | flops 19336790016 | bytes 38797824 | tf_op jit(solution)/shard_map/dot_general | solution.py:94
  973.5 4.5 copy-done
  978.0 23.0 %convolution_select_fusion = f32[6144,512]{1,0:T(8,128)} fusion(f32[6144,512]{1,0:T(8,128)S(1)} %fusion, pred[]{:T(512)S(6)} %and.52, f32[2,512,512]{2,1,0:T(8,128)S(1)} %copy-done.3), kind=kOutput, calls=%fused_computation.6 | convolution fusion | flops 19330498560 | bytes 26214400 | tf_op jit(solution)/shard_map/dot_general | solution.py:27
  1001.0 254.9 %all-reduce.11.cloned.1.call-done = f32[6144,512]{1,0:T(8,128)} async-done(((f32[6144,512]{1,0:T(8,128)}), f32[6144,512]{1,0:T(8,128)}) %all-reduce.11.cloned.1.call-update) | async-done | bytes 12582928 | tf_op jit(solution)/shard_map/psum | solution.py:91
  1255.9 30.5 %fusion.1 = f32[6144,512]{1,0:T(8,128)} fusion(f32[6144,512]{1,0:T(8,128)} %all-reduce.11.cloned.1.call-done, f32[6144,512]{1,0:T(8,128)} %copy-done, pred[512]{0:T(512)(128)(4,1)S(1)} %fusion.28, pred[]{:T(512)S(6)} %and.52, f32[1,512,512]{2,1,0:T(8,128)} %all-gather.15.cloned.1.call-done), kind=kOutput, calls=%fused_computation.5 | convolution fusion | flops 19336790016 | bytes 38797824 | tf_op jit(solution)/shard_map/dot_general | solution.py:94
  (24 shorter events, 0.3 us)
Async XLA Ops:
  7.4 73.6 %all-reduce.5.cloned.1.call-start = ((), (), s32[]{:S(2)}) async-start(), calls=%async_computation.2 | async-start | bytes 4194304 | tf_op jit(solution)/shard_map/psum | solution.py:67
  13.3 76.7 %all-gather.9.cloned.1.call-start = ((), (), s32[]{:S(2)}) async-start(), calls=%async_computation.6 | async-start | bytes 7864320 | tf_op jit(solution)/shard_map/all_gather | solution.py:69
  17.2 144.5 %all-gather.11.cloned.1.call-start = ((), (), s32[]{:S(2)}) async-start(), calls=%async_computation.7 | async-start | bytes 7864320 | tf_op jit(solution)/shard_map/all_gather | solution.py:69
  17.8 171.5 %all-reduce.7.cloned.1.call-start = ((), (), s32[]{:S(2)}) async-start(), calls=%async_computation.3 | async-start | bytes 4194304 | tf_op jit(solution)/shard_map/psum | solution.py:67
  81.0 40.1 %copy-start.2 = (f32[512,1024]{1,0:T(8,128)S(1)}, f32[512,1024]{1,0:T(8,128)}, u32[]{:S(2)}) copy-start(f32[512,1024]{1,0:T(8,128)} %all-reduce.5.cloned.1.call-done) | copy-start | bytes 6291460
  116.3 4.8 copy-start.1
  376.7 5.6 copy-start.4
  376.7 279.3 %all-to-all-start.1 = ((f32[768,8,512]{0,2,1:T(8,128)}), f32[768,8,512]{0,2,1:T(8,128)}, u32[]{:S(2)}, u32[]{:S(2)}) async-start(f32[768,8,512]{0,2,1:T(8,128)} %bitcast.42), calls=%async_computation.1 | async-start | bytes 25165824 | tf_op jit(solution)/shard_map/all_to_all | solution.py:81
  382.2 311.8 %all-gather.13.cloned.1.call-start = ((), (), s32[]{:S(2)}) async-start(), calls=%async_computation.8 | async-start | bytes 1310720 | tf_op jit(solution)/shard_map/all_gather | solution.py:96
  383.1 562.2 %all-reduce.9.cloned.1.call-start = ((), (), s32[]{:S(2)}) async-start(), calls=%async_computation.4 | async-start | bytes 25165824 | tf_op jit(solution)/shard_map/psum | solution.py:91
  655.9 12.9 copy-start.3
  693.2 307.9 %all-gather.15.cloned.1.call-start = ((), (), s32[]{:S(2)}) async-start(), calls=%async_computation.9 | async-start | bytes 1310720 | tf_op jit(solution)/shard_map/all_gather | solution.py:96
  693.9 562.0 %all-reduce.11.cloned.1.call-start = ((), (), s32[]{:S(2)}) async-start(), calls=%async_computation.5 | async-start | bytes 25165824 | tf_op jit(solution)/shard_map/psum | solution.py:91
  973.5 4.5 copy-start
Sparse Core Ops, SparseCore 0:
  13.4 67.5 all-reduce.4
  124.4 64.8 all-reduce.6
  693.3 251.9 all-reduce.8
  1001.1 254.7 all-reduce.10
Sparse Core Ops, SparseCore 1:
  17.3 72.7 all-gather.8
  91.7 70.0 all-gather.10
  384.5 26.3 all-gather.12
  695.8 23.8 all-gather.14
where the time goes:
time: 1300 us; the launch traced here: 1290 us
  waiting for transfers between devices  916 us (70%)
  matrix products  166 us (13%)
  blocking collectives  146 us (11%)
  local copies, waits for them, and re-layouts  41.2 us (3%)
  between operations  15.4 us (1%)
    psum x2, waiting for transfers between devices, total_rows(): return lax.psum(partial_sum, 'rows')  506 us
    all_to_all x1, waiting for transfers between devices, on_device(): lax.all_to_all(lax.all_to_all(current, 'cols', split_axis=0, concat_axis=...  273 us
    all_to_all x1, blocking collectives, on_device(): lax.all_to_all(current, 'cols', split_axis=0, concat_axis=1, tiled=True)  146 us
    psum x2, waiting for transfers between devices, on_device(): solved = lax.psum(jnp.where(member, partial_value, 0.0), 'rows')  90.6 us
    dot_general x2, matrix products, update_rows(): jnp.dot(solved_cols, lax.all_gather(second_factor[panel_number], 'cols',...  58.7 us
    dot_general x2, matrix products, on_device(): lax.dot_general(lax.all_gather(first_factor[panel_index], 'cols', axis=0,...  53 us
    dot_general x2, matrix products, right_solve(): lax.dot_general(own_columns, inverse_cols, CONTRACT_COLS, precision=HIGHE...  47.3 us
    all_gather x2, waiting for transfers between devices, on_device(): lax.all_gather(first_factor[panel_index], 'cols', axis=0, tiled=True)  44.6 us
  transfers between devices with their start and end apart: 9, of which 7 were waited for; matrix products, arithmetic and copies ran while one was open for 10% of the time, Pallas kernels for 0%

commit v1 on v0

v1 whole, which is shorter than its diff:
```python
import functools

import jax
import jax.numpy as jnp
from jax import lax
from jax.experimental import pallas as pl
from jax.experimental.pallas import tpu as pltpu
from jax.sharding import PartitionSpec as P

BLOCK = 128
AHEAD = 2
SHARE = 1000
PLAIN = (((1,), (0,)), ((), ()))
CONTRACT_COLS = (((1,), (1,)), ((), ()))
ANY = pl.BlockSpec(memory_space=pl.ANY)


def split(value):
    high = value.astype(jnp.bfloat16)
    low = (value - high.astype(jnp.float32)).astype(jnp.bfloat16)
    return high, low


def product(left, right, contract=PLAIN):
    def one(a, b):
        return lax.dot_general(a, b, contract, preferred_element_type=jnp.float32)

    return one(left[0], right[0]) + (one(left[0], right[1]) + one(left[1], right[0]))


def whole(shape):
    return pl.BlockSpec(shape, lambda *_: (0,) * len(shape))


def cost(flops, read):
    return pl.CostEstimate(flops=flops // SHARE, bytes_accessed=read // SHARE, transcendentals=0)


def compiler_params(mib):
    return pltpu.CompilerParams(vmem_limit_bytes=mib * 2**20)


def solve_kernel(panels, place, own, other, inverse_ref, corner_ref, *refs):
    solved_ref, high_ref, low_ref, head, inv_high, inv_low, cor_high, cor_low = refs
    width = inverse_ref.shape[1]
    blocks = width // BLOCK

    @pl.when(pl.program_id(0) == 0)
    def _():
        for k in range(panels):
            inv_high[k], inv_low[k] = split(inverse_ref[k])
            for p in range(k):
                for b in range(blocks):
                    rows = slice((k * blocks + b) * BLOCK, (k * blocks + b + 1) * BLOCK)
                    for c in range(corner_ref.shape[0]):
                        parts = split(corner_ref[c, (k - 1) * blocks + b, p].T)
                        held = corner_ref.shape[3]
                        columns = slice(c * held, (c + 1) * held)
                        cor_high[p, rows, columns], cor_low[p, rows, columns] = parts

    for b in range(panels * blocks):
        mine = jnp.where(place[0] == b % 2, own[b // 2], other[b // 2])
        head[b * BLOCK : (b + 1) * BLOCK] = mine
    parts = []
    for k in range(panels):
        rows = slice(k * width, (k + 1) * width)
        current = head[rows]
        for p in range(k):
            block = (cor_high[p, rows], cor_low[p, rows])
            current = current - product(block, parts[p])
        answer = product((inv_high[k], inv_low[k]), split(current))
        parts.append(split(answer))
        solved_ref[rows] = answer
        high_ref[rows] = parts[k][0]
        low_ref[rows] = parts[k][1]


def solve_rows(place, own, other, inverse, corner):
    panels, width, _ = inverse.shape
    breadth = own.shape[2]
    depth = panels * width
    tile = min(breadth, 256)
    half = pl.BlockSpec((depth // BLOCK // 2, BLOCK, tile), lambda i, _: (0, 0, i))
    block = pl.BlockSpec((depth, tile), lambda i, _: (0, i))
    corner_shape = (panels - 1, depth, width)
    return pl.pallas_call(
        functools.partial(solve_kernel, panels),
        grid_spec=pltpu.PrefetchScalarGridSpec(
            num_scalar_prefetch=1,
            grid=(breadth // tile,),
            in_specs=[half, half, whole(inverse.shape), whole(corner.shape)],
            out_specs=[block] * 3,
            scratch_shapes=[
                pltpu.VMEM((depth, tile), jnp.float32),
                pltpu.VMEM(inverse.shape, jnp.bfloat16),
                pltpu.VMEM(inverse.shape, jnp.bfloat16),
                pltpu.VMEM(corner_shape, jnp.bfloat16),
                pltpu.VMEM(corner_shape, jnp.bfloat16),
            ],
        ),
        out_shape=[
            jax.ShapeDtypeStruct((depth, breadth), t)
            for t in (jnp.float32, jnp.bfloat16, jnp.bfloat16)
        ],
        compiler_params=compiler_params(60),
        cost_estimate=cost(6 * 3 * width * width * breadth, 16 * depth * breadth),
        name="solve_rows",
    )(place, own, other, inverse, corner)


def update_kernel(tops, slots, offset, count, place, slab, *rest):
    factors = rest[:count]
    high, low, own_top = rest[count : count + 3]
    outs = rest[-slots - 3 : -3]
    factor_high, factor_low, total = rest[-3:]

    @pl.when(pl.program_id(0) == 0)
    def _():
        panels, share, columns = factors[0].shape
        held = columns // slots
        chunk = slab.shape[1]
        for dest in range(slots):
            rows = slice(dest * chunk, (dest + 1) * chunk)
            taken = slice(dest * held + offset, dest * held + offset + chunk)
            for panel in range(panels):
                for slot in range(count):
                    start = pl.multiple_of((place[1] ^ slot) * share, BLOCK)
                    at = pl.ds(panel * share * count + start, share)
                    parts = split(factors[slot][panel, :, taken].T)
                    factor_high[rows, at], factor_low[rows, at] = parts

    answer = product((factor_high[...], factor_low[...]), (high[...], low[...]))
    total[...] = answer.reshape(total.shape)
    for dest, first, count, flag in tops:

        @pl.when(place[2 + flag] > 0)
        def _():
            total[dest, :count] = slab[dest, :count] - own_top[first : first + count]

    for slot in range(slots):
        dest = place[0] ^ slot
        outs[slot][...] = slab[dest] - total[dest]


def update_rows(place, slab, factors, high, low, own_top, begin, chunk, offset, after):
    slots, piece, breadth = slab.shape
    depth = high.shape[0]
    tile = min(breadth, 256)
    assert begin % chunk == 0
    tops = []
    for dest in range(slots):
        first = dest * piece + begin
        for b in range(own_top.shape[0] // BLOCK):
            start, stop = max(first, b * BLOCK), min(first + chunk, (b + 1) * BLOCK)
            if start < stop:
                assert start == first
                tops.append((dest, start, stop - start, b))
    columns = pl.BlockSpec((depth, tile), lambda i, _: (0, i))
    return pl.pallas_call(
        functools.partial(update_kernel, tops, slots, offset, len(factors)),
        grid_spec=pltpu.PrefetchScalarGridSpec(
            num_scalar_prefetch=1,
            grid=(breadth // tile,),
            in_specs=[
                pl.BlockSpec((slots, chunk, tile), lambda i, _: (0, begin // chunk, i)),
                *[whole(f.shape) for f in factors],
                columns,
                columns,
                pl.BlockSpec((own_top.shape[0], tile), lambda i, _: (0, i)),
            ]
            + [ANY] * len(after),
            out_specs=[pl.BlockSpec((chunk, tile), lambda i, _: (0, i))] * slots,
            scratch_shapes=[
                pltpu.VMEM((slots * chunk, depth), jnp.bfloat16),
                pltpu.VMEM((slots * chunk, depth), jnp.bfloat16),
                pltpu.VMEM((slots, chunk, tile), jnp.float32),
            ],
        ),
        out_shape=[jax.ShapeDtypeStruct((chunk, breadth), jnp.float32)] * slots,
        compiler_params=compiler_params(60),
        cost_estimate=cost(12 * slots * chunk * depth * breadth, 12 * depth * breadth),
        name="update_rows",
    )(place, slab, *factors, high, low, own_top, *after)


def reduce_kernel(slots, views, extra, place, *refs):
    pieces = refs[:slots]
    inverse = refs[slots]
    own = refs[slots + 1 : slots + 1 + views]
    other = refs[slots + 1 + views : slots + 1 + 2 * views]
    out, current, high, low, factor_high, factor_low = refs[slots + 1 + 2 * views + extra :]
    step = pl.program_id(0)
    chunk, breadth = pieces[0].shape
    width = inverse.shape[1]
    depth = current.shape[1]
    narrow = out.shape[2]
    span = depth // breadth
    count, _, piece, _ = own[0].shape
    core = place[1]

    for part in range(span):
        for slot in range(slots):

            @pl.when((step * span + part) ^ place[0] == slot)
            def _():
                current[:, part * breadth : (part + 1) * breadth] = pieces[slot][...]

    def load(group, panels):
        for parity in range(2):
            sources = own if parity == group % 2 else other

            @pl.when(core == parity)
            def _():
                for panel in range(panels):
                    for part in range(count):
                        start = panel * width + part * piece
                        rows = slice(start, start + piece)
                        parts = split(sources[group // 2 * 2 + panel][part, 0])
                        factor_high[rows], factor_low[rows] = parts

    def store(value, start):
        for g in range(value.shape[1] // narrow):
            out[start // narrow + g] = value[:, g * narrow : (g + 1) * narrow]

    @pl.when(step == 0)
    def _():
        first = product(split(current[:, :width]), split(inverse[0]), CONTRACT_COLS)
        first_parts = split(first)
        high[:, :width], low[:, :width] = first_parts
        store(first, 0)
        for group in range(width // narrow, depth // narrow):
            load(group, 1)
            columns = slice(group * narrow, (group + 1) * narrow)
            current[:, columns] -= product(first_parts, (factor_high[:width], factor_low[:width]))
        second = product(split(current[:, width:]), split(inverse[1]), CONTRACT_COLS)
        high[:, width:], low[:, width:] = split(second)
        store(second, width)

    @pl.when(step > 0)
    def _():
        for group in range(depth // narrow):
            load(group, 2)
            columns = slice(group * narrow, (group + 1) * narrow)
            part = product((high[...], low[...]), (factor_high[...], factor_low[...]))
            out[group] = current[:, columns] - part


def reduce_columns(place, pieces, inverse, own, other, row_count, after):
    chunk, breadth = pieces[0].shape
    slots = len(pieces)
    panels, width, _ = inverse.shape
    depth = panels * width
    breadth_all = slots * breadth
    narrow = breadth_all // row_count
    span = depth // narrow // 2
    taken = (own.shape[0], 1) + own.shape[2:]

    def view(chip, panel):
        return pl.BlockSpec(
            taken, lambda i, _: (0, jnp.maximum(2 * (span * i + chip) - 1 + panel, 0), 0, 0)
        )

    views = [view(chip, panel) for chip in range(span) for panel in range(2)]
    return pl.pallas_call(
        functools.partial(reduce_kernel, slots, len(views), len(after)),
        grid_spec=pltpu.PrefetchScalarGridSpec(
            num_scalar_prefetch=1,
            grid=(breadth_all // depth,),
            in_specs=[whole(pieces[0].shape)] * slots
            + [whole(inverse.shape)]
            + views * 2
            + [ANY] * len(after),
            out_specs=pl.BlockSpec((depth // narrow, chunk, narrow), lambda i, _: (i, 0, 0)),
            scratch_shapes=[
                pltpu.VMEM((chunk, depth), jnp.float32),
                pltpu.VMEM((chunk, depth), jnp.bfloat16),
                pltpu.VMEM((chunk, depth), jnp.bfloat16),
                pltpu.VMEM((depth, narrow), jnp.bfloat16),
                pltpu.VMEM((depth, narrow), jnp.bfloat16),
            ],
        ),
        out_shape=jax.ShapeDtypeStruct((row_count, chunk, narrow), jnp.float32),
        compiler_params=compiler_params(60),
        cost_estimate=cost(6 * chunk * depth * breadth_all, 4 * depth * breadth_all),
        name="reduce_columns",
    )(place, *pieces, inverse, *[own] * len(views), *[other] * len(views), *after)


def order_kernel(chips, skipped, place, *refs):
    entry = pl.program_id(0)
    for i in range(2 * chips - 1):
        if not skipped:

            @pl.when(entry - place[0] == i - (chips - 1))
            def _():
                refs[-1][0] = refs[i][...]

        else:
            for panel in range(2):
                chip = (entry + 1 - panel) // 2
                held = jnp.logical_and((entry + 1) % 2 == panel, entry > 0)
                first = panel == 0 and entry == 0

                @pl.when(
                    jnp.logical_and(jnp.logical_or(held, first), chip - place[0] == i - (chips - 1))
                )
                def _():
                    refs[-1][0] = refs[i][panel]


def in_order(place, pieces, skipped, after):
    chips = (len(pieces) + 1) // 2
    shape = pieces[0].shape
    entry = shape[1:] if skipped else shape
    count = 2 * chips - 1 if skipped else chips
    return pl.pallas_call(
        functools.partial(order_kernel, chips, skipped),
        grid_spec=pltpu.PrefetchScalarGridSpec(
            num_scalar_prefetch=1,
            grid=(count,),
            in_specs=[whole(shape)] * len(pieces) + [ANY] * len(after),
            out_specs=pl.BlockSpec((1,) + entry, lambda i, _: (i,) + (0,) * len(entry)),
        ),
        out_shape=jax.ShapeDtypeStruct((count,) + entry, jnp.float32),
        compiler_params=compiler_params(60),
        name="in_order",
    )(place, *pieces, *after)


def along_line(block, row_count, skipped, after):
    chips = row_count // 2
    up = [(i, i + 2) for i in range(row_count - 2)]
    down = [(i + 2, i) for i in range(row_count - 2)]
    below, above = [block], [block]
    for _ in range(chips - 1):
        below.append(lax.ppermute(below[-1], "rows", up))
        above.append(lax.ppermute(above[-1], "rows", down))
    place = jnp.stack([lax.axis_index("rows") // 2])
    return in_order(place, below[:0:-1] + above, skipped, after), [below[-1], above[-1]]


def gate_kernel(*refs):
    pass


def gate(value, after):
    return pl.pallas_call(
        gate_kernel,
        in_specs=[ANY] * (1 + len(after)),
        out_specs=ANY,
        out_shape=jax.ShapeDtypeStruct(value.shape, value.dtype),
        input_output_aliases={0: 0},
        compiler_params=compiler_params(60),
        name="gate",
    )(value, *after)


def pick_kernel(axis, count, *refs):
    out = refs[-1]
    extent = out.shape[axis] // count
    for i in range(count):
        at = (slice(None),) * axis + (slice(i * extent, (i + 1) * extent),)
        out[at] = refs[i][...]


def pick_blocks(source, axis, extent, blocks, after):
    ndim = source.ndim

    def sized(size):
        return source.shape[:axis] + (size,) + source.shape[axis + 1 :]

    def spec(place):
        return pl.BlockSpec(sized(extent), lambda _: (0,) * axis + (place,) + (0,) * (ndim - axis - 1))

    result = sized(extent * len(blocks))
    return pl.pallas_call(
        functools.partial(pick_kernel, axis, len(blocks)),
        grid=(1,),
        in_specs=[spec(b) for b in blocks] + [ANY] * len(after),
        out_specs=whole(result),
        out_shape=jax.ShapeDtypeStruct(result, source.dtype),
        compiler_params=compiler_params(60),
        name="pick_blocks",
    )(*[source] * len(blocks), *after)


def on_device(window_slab, first_inverse, first_factor, second_inverse, second_factor):
    row_count = lax.axis_size("rows")
    col_count = lax.axis_size("cols")
    row_index = lax.axis_index("rows")
    col_index = lax.axis_index("cols")
    core = row_index % 2
    row_share, breadth = window_slab.shape
    panels, width, _ = first_inverse.shape
    depth = panels * width
    assert depth <= row_count * BLOCK and panels == 2
    piece = row_share // col_count
    if piece == 6 * BLOCK:
        sizes, groups = [BLOCK] * 6, [[0, 1], [2, 3], [4, 5]]
    else:
        sizes, groups = [piece], [[0]]
    begins = [sum(sizes[:j]) for j in range(len(sizes))]
    chunks = len(sizes)
    narrow = breadth * col_count // row_count
    swap = [(i, i ^ 1) for i in range(row_count)]

    def from_sibling(value):
        return lax.ppermute(value, "rows", swap)

    over_cols = [[(i, i ^ s) for i in range(col_count)] for s in range(col_count)]

    corner = lax.all_gather(first_factor[: panels - 1, :, :BLOCK], "rows")
    corner = lax.all_gather(corner[width // BLOCK : depth // BLOCK], "cols")

    def gather_factor(group, after):
        begin, extent = begins[group[0]], sum(sizes[j] for j in group)
        if piece % BLOCK == 0:
            blocks = [(d * piece + begin) // extent for d in range(col_count)]
            part = pick_blocks(first_factor, 2, extent, blocks, after)
        else:
            columns = [d * piece + begin for d in range(col_count)]
            part = jnp.concatenate([first_factor[:, :, c : c + extent] for c in columns], 2)
        if group[0] == 0 and col_count == 4:
            parts = [lax.ppermute(part, "cols", pairs) for pairs in over_cols[1:]]
            return [part] + parts, col_index
        return [lax.all_gather(part, "cols", axis=1, tiled=True)], 0

    factors = [gather_factor(groups[0], [])]

    line, last = along_line(second_factor, row_count, True, factors[0][0][1:] + [corner])
    own_second = lax.all_gather(line, "cols")

    own_head, _ = along_line(pick_blocks(window_slab, 0, BLOCK, [0], last), row_count, False, [])
    other_head = from_sibling(own_head)
    solved, solved_high, solved_low = solve_rows(
        jnp.stack([core]), own_head, other_head, first_inverse, corner
    )
    start = row_index * BLOCK
    own_top = lax.dynamic_slice_in_dim(solved, jnp.minimum(start, depth - BLOCK), BLOCK, 0)
    is_top = (start < depth).astype(jnp.int32)

    slab = window_slab.reshape(col_count, piece, breadth)
    updated, done, results, ready = [], [], [], []

    def update(j):
        number = next(g for g, group in enumerate(groups) if j in group)
        after = [done[max(j - AHEAD, 1)]] if j >= AHEAD else ready
        arrays, order = factors[number]
        out = update_rows(
            jnp.stack([col_index, jnp.int32(order), is_top]),
            slab,
            arrays,
            solved_high,
            solved_low,
            own_top,
            begins[j],
            sizes[j],
            begins[j] - begins[groups[number][0]],
            after,
        )
        pieces = [out[0]]
        for slot in range(1, col_count):
            pieces.append(lax.ppermute(out[slot], "cols", over_cols[slot]))
        updated.append((out, pieces))

    update(0)

    own_second = gate(own_second, [updated[0][0][0]])
    other_second = from_sibling(own_second)
    place_cores = jnp.stack([col_index, core])
    ready = [own_second]
    if chunks > 1:
        update(1)
    factors += [gather_factor(group, ready) for group in groups[1:]]

    for j in range(chunks):
        pieces = updated[j][1]
        after = [updated[j + 1][0][0]] if j + 1 < len(updated) else []
        after += [results[j - 2]] if j >= 2 else []
        done.append(
            reduce_columns(
                place_cores, pieces, second_inverse, own_second, other_second, row_count, after
            )
        )
        results.append(lax.all_to_all(done[j], "rows", split_axis=0, concat_axis=0, tiled=True))
        for later in range(AHEAD if j == 1 else j + AHEAD, min(j + AHEAD + 1, chunks) if j else 0):
            update(later)
    turned = jnp.concatenate(results, 1)
    return turned.reshape(row_count * piece, narrow)


def solution(mesh):
    return jax.shard_map(
        on_device,
        mesh=mesh,
        in_specs=(P("rows", "cols"), P(), P(None, "cols", "rows"), P(), P(None, "cols", "rows")),
        out_specs=P("cols", "rows"),
        check_vma=False,
    )
```

time: 1300 us -> 597 us (0.46)
  waiting for transfers between devices: 916 us -> 270 us
  Pallas kernels: 0 us -> 170 us
  matrix products: 166 us -> 0 us
  blocking collectives: 146 us -> 25 us
  starting transfers between devices: 5.8 us -> 83.4 us
  local copies, waits for them, and re-layouts: 41.2 us -> 28.2 us
    psum x4 -> x0, waiting for transfers between devices: 597 us -> none  [the longest x2 506 us: total_rows(): return lax.psum(partial_sum, 'rows')]
    all_to_all x1 -> x6, waiting for transfers between devices: 273 us -> 64.8 us  [on_device(): lax.all_to_all(done[j], 'rows', split_axis=0, concat_axis=0, tiled=True)]
    ppermute x0 -> x35, waiting for transfers between devices: none -> 205 us  [the longest x18 127 us: update(): pieces.append(lax.ppermute(out[slot], 'cols', over_cols[slot]))]
    pallas_call x0 -> x20, Pallas kernels: none -> 170 us  [the longest x6 79.8 us: reduce_columns(): pl.pallas_call(functools.partial(reduce_kernel, slots, len(views), len(af...]
    dot_general x8 -> x0, matrix products: 166 us -> none  [the longest x2 58.7 us: update_rows(): jnp.dot(solved_cols, lax.all_gather(second_factor[panel_number], 'cols',...]
    all_to_all x1 -> x0, blocking collectives: 146 us -> none  [on_device(): lax.all_to_all(current, 'cols', split_axis=0, concat_axis=1, tiled=True)]
    ppermute x0 -> x35, starting transfers between devices: none -> 56.9 us  [the longest x6 23 us: along_line(): below.append(lax.ppermute(below[-1], 'rows', up))]
    all_gather x4, waiting for transfers between devices: 44.6 us -> 0.04 us  [the longest x1 0.02 us: on_device(): corner = lax.all_gather(corner[width // BLOCK:depth // BLOCK], 'cols')]
  transfers between devices with their start and end apart: 9 -> 45, of which waited for: 7 -> 27; matrix products, arithmetic and copies ran while one was open for 10% -> 3% of each run, Pallas kernels for 0% -> 28%
where the time goes in v1:
time: 597 us; the launch traced here: 592 us
  waiting for transfers between devices  270 us (45%)
  Pallas kernels  170 us (28%)
  starting transfers between devices  83.4 us (14%)
  local copies, waits for them, and re-layouts  28.2 us (5%)
  blocking collectives  25 us (4%)
  between operations  13.8 us (2%)
    ppermute x18, waiting for transfers between devices, update(): pieces.append(lax.ppermute(out[slot], 'cols', over_cols[slot]))  127 us
    pallas_call x6, Pallas kernels, reduce_columns(): pl.pallas_call(functools.partial(reduce_kernel, slots, len(views), len(af...  79.8 us
    all_to_all x6, waiting for transfers between devices, on_device(): lax.all_to_all(done[j], 'rows', split_axis=0, concat_axis=0, tiled=True)  64.8 us
    pallas_call x6, Pallas kernels, update_rows(): pl.pallas_call(functools.partial(update_kernel, tops, slots, offset, len(...  59.1 us
    ppermute x3, waiting for transfers between devices, gather_factor(): parts = [lax.ppermute(part, 'cols', pairs) for pairs in over_cols[1:]]  35 us
    ppermute x6, waiting for transfers between devices, along_line(): below.append(lax.ppermute(below[-1], 'rows', up))  34.5 us
    all_to_all x6, starting transfers between devices, on_device(): lax.all_to_all(done[j], 'rows', split_axis=0, concat_axis=0, tiled=True)  26.3 us
    all_gather x1, blocking collectives, on_device(): corner = lax.all_gather(first_factor[:panels - 1, :, :BLOCK], 'rows')  25 us
  transfers between devices with their start and end apart: 45, of which 27 were waited for; matrix products, arithmetic and copies ran while one was open for 3% of the time, Pallas kernels for 28%

profile of v1, /device:TPU:0, one launch (start us, length us, event | category | flops | bytes accessed | tf_op | source)
XLA Modules:
  0.0 592.5 jit_solution(8624664645624905073)
XLA Ops:
  14.4 25.0 %all-gather = f32[8,128,128]{2,1,0:T(8,128)S(1)} all-gather(f32[1,128,128]{2,1,0:T(8,128)S(1)} %slice.6), channel_id=2, replica_groups=mesh['rows'=8,'cols'=4] {'rows'}, dimensions={0}, use_global_device_ids=true | all-gather | bytes 589824 | tf_op jit(solution)/shard_map/all_gather | solution.py:412
  49.3 9.3 %collective-permute-done.4.refs_1_ = f32[2,128,512]{2,1,0:T(8,128)} collective-permute-done((f32[2,128,512]{2,1,0:T(8,128)}, f32[2,128,512]{2,1,0:T(8,128)}, u32[]{:S(2)}, u32[]{:S(2)}) %collective-permute-start.4) | collective-permute-done | bytes 524320 | tf_op jit(solution)/shard_map/ppermute | solution.py:336
  65.1 11.9 %collective-permute-done.rest_1_.refs_7_ = f32[2,128,1024]{2,1,0:T(8,128)S(1)} collective-permute-done((f32[2,128,1024]{2,1,0:T(8,128)}, f32[2,128,1024]{2,1,0:T(8,128)S(1)}, u32[]{:S(2)}, u32[]{:S(2)}) %collective-permute-start) | collective-permute-done | bytes 1048608 | tf_op jit(solution)/shard_map/ppermute | solution.py:424
  77.0 23.1 %collective-permute-done.1.rest_2_.refs_8_ = f32[2,128,1024]{2,1,0:T(8,128)S(1)} collective-permute-done((f32[2,128,1024]{2,1,0:T(8,128)}, f32[2,128,1024]{2,1,0:T(8,128)S(1)}, u32[]{:S(2)}, u32[]{:S(2)}) %collective-permute-start.1) | collective-permute-done | bytes 1048608 | tf_op jit(solution)/shard_map/ppermute | solution.py:424
  111.0 9.6 %collective-permute-done.9.refs_2_ = f32[128,1024]{1,0:T(8,128)S(1)} collective-permute-done((f32[128,1024]{1,0:T(8,128)}, f32[128,1024]{1,0:T(8,128)S(1)}, u32[]{:S(2)}, u32[]{:S(2)}) %collective-permute-start.9) | collective-permute-done | bytes 524320 | tf_op jit(solution)/shard_map/ppermute | solution.py:336
  126.2 8.4 %collective-permute-done.10.refs_1_ = f32[128,1024]{1,0:T(8,128)S(1)} collective-permute-done((f32[128,1024]{1,0:T(8,128)S(1)}, f32[128,1024]{1,0:T(8,128)S(1)}, u32[]{:S(2)}, u32[]{:S(2)}) %collective-permute-start.10) | collective-permute-done | bytes 524320 | tf_op jit(solution)/shard_map/ppermute | solution.py:336
  162.6 13.9 %solve_rows.1 = (f32[1024,1024]{1,0:T(8,128)}, bf16[1024,1024]{1,0:T(8,128)(2,1)}, bf16[1024,1024]{1,0:T(8,128)(2,1)}) custom-call(s32[1]{0:T(128)} %bitcast.1.place, f32[4,128,1024]{2,1,0:T(8,128)} %in_order.2.own, f32[4,128,1024]{2,1,0:T(8,128)} %copy-done.7, f32[2,512,512]{2,1,0:T(8,128)} %inverse_ref.1, f32[4,4,1,128,128]{4,3,2,1,0:T(8,128)} %bitcast.16), custom_call_target="tpu_custom_call" | custom-call | flops 4831838 | bytes 16777 | tf_op jit(solution)/shard_map/solve_rows/pallas_call | solution.py:86
  178.4 9.8 %update_rows.6 = (f32[128,1024]{1,0:T(8,128)}, f32[128,1024]{1,0:T(8,128)}, f32[128,1024]{1,0:T(8,128)}, f32[128,1024]{1,0:T(8,128)}) custom-call(s32[3]{0:T(128)} %add_add_fusion.place, f32[4,768,1024]{2,1,0:T(8,128)} %bitcast.9, f32[2,128,1024]{2,1,0:T(8,128)} %pick_blocks.4.rest_0_, f32[2,128,1024]{2,1,0:T(8,128)} %copy-done.4, ...), custom_call_target="tpu_custom_call" | custom-call | flops 6442450 | bytes 12582 | tf_op jit(solution)/shard_map/update_rows/pallas_call | solution.py:159
  195.8 10.3 %update_rows.7 = (f32[128,1024]{1,0:T(8,128)}, f32[128,1024]{1,0:T(8,128)}, f32[128,1024]{1,0:T(8,128)}, f32[128,1024]{1,0:T(8,128)}) custom-call(s32[3]{0:T(128)} %add_add_fusion.place, f32[4,768,1024]{2,1,0:T(8,128)} %bitcast.10, f32[2,128,1024]{2,1,0:T(8,128)} %pick_blocks.4.rest_0_, f32[2,128,1024]{2,1,0:T(8,128)} %copy-done.4, ...), custom_call_target="tpu_custom_call" | custom-call | flops 6442450 | bytes 12582 | tf_op jit(solution)/shard_map/update_rows/pallas_call | solution.py:159
  216.5 13.0 %collective-permute-done.18.refs_3_ = f32[128,1024]{1,0:T(8,128)S(1)} collective-permute-done((f32[128,1024]{1,0:T(8,128)S(1)}, f32[128,1024]{1,0:T(8,128)S(1)}, u32[]{:S(2)}, u32[]{:S(2)}) %collective-permute-start.18) | collective-permute-done | bytes 524320 | tf_op jit(solution)/shard_map/ppermute | solution.py:463
  230.4 13.9 %reduce_columns.6 = f32[8,128,512]{2,1,0:T(8,128)} custom-call(s32[2]{0:T(128)} %pad_add_fusion.place, f32[128,1024]{1,0:T(8,128)} %get-tuple-element.35.refs_1_.refs_0_, f32[128,1024]{1,0:T(8,128)} %copy-done.8, f32[128,1024]{1,0:T(8,128)} %copy-done.9, f32[128,1024]{1,0:T(8,128)} %copy-done.12, f32[2,512,512]{2,1,0:T(8,128)} %refs_4_.11, ...), custom_call_target="tpu_custom_call" | custom-call | flops 3221225 | bytes 16777 | tf_op jit(solution)/shard_map/reduce_columns/pallas_call | solution.py:264
  251.6 17.1 %collective-permute-done.20.refs_1_ = f32[128,1024]{1,0:T(8,128)S(1)} collective-permute-done((f32[128,1024]{1,0:T(8,128)}, f32[128,1024]{1,0:T(8,128)S(1)}, u32[]{:S(2)}, u32[]{:S(2)}) %collective-permute-start.20) | collective-permute-done | bytes 524320 | tf_op jit(solution)/shard_map/ppermute | solution.py:463
  268.6 12.0 %collective-permute-done.22.refs_3_ = f32[128,1024]{1,0:T(8,128)S(1)} collective-permute-done((f32[128,1024]{1,0:T(8,128)}, f32[128,1024]{1,0:T(8,128)S(1)}, u32[]{:S(2)}, u32[]{:S(2)}) %collective-permute-start.22) | collective-permute-done | bytes 524320 | tf_op jit(solution)/shard_map/ppermute | solution.py:463
  281.4 13.2 %reduce_columns.7.rest_4_ = f32[8,128,512]{2,1,0:T(8,128)} custom-call(s32[2]{0:T(128)} %pad_add_fusion.place, f32[128,1024]{1,0:T(8,128)} %get-tuple-element.39.refs_9_.refs_0_, f32[128,1024]{1,0:T(8,128)} %copy-done.19, f32[128,1024]{1,0:T(8,128)} %copy-done.22, f32[128,1024]{1,0:T(8,128)} %copy-done.24, f32[2,512,512]{2,1,0:T(8,128)} %refs_4_.11, ...), custom_call_target="tpu_custom_call" | custom-call | flops 3221225 | bytes 16777 | tf_op jit(solution)/shard_map/reduce_columns/pallas_call | solution.py:264
  304.3 9.9 %update_rows.8 = (f32[128,1024]{1,0:T(8,128)}, f32[128,1024]{1,0:T(8,128)}, f32[128,1024]{1,0:T(8,128)}, f32[128,1024]{1,0:T(8,128)}) custom-call(s32[3]{0:T(128)} %add_add_fusion.1.place, f32[4,768,1024]{2,1,0:T(8,128)} %bitcast.11, f32[2,512,1024]{2,1,0:T(8,128)} %all-gather.9.cloned.1.call-done.rest_0_, ...), custom_call_target="tpu_custom_call" | custom-call | flops 6442450 | bytes 12582 | tf_op jit(solution)/shard_map/update_rows/pallas_call | solution.py:159
  317.8 9.7 %update_rows.9 = (f32[128,1024]{1,0:T(8,128)}, f32[128,1024]{1,0:T(8,128)}, f32[128,1024]{1,0:T(8,128)}, f32[128,1024]{1,0:T(8,128)}) custom-call(s32[3]{0:T(128)} %add_add_fusion.1.place, f32[4,768,1024]{2,1,0:T(8,128)} %bitcast.12, f32[2,512,1024]{2,1,0:T(8,128)} %all-gather.9.cloned.1.call-done.rest_0_, ...), custom_call_target="tpu_custom_call" | custom-call | flops 6442450 | bytes 12582 | tf_op jit(solution)/shard_map/update_rows/pallas_call | solution.py:159
  327.4 9.7 %collective-permute-done.23.refs_1_ = f32[128,1024]{1,0:T(8,128)S(1)} collective-permute-done((f32[128,1024]{1,0:T(8,128)}, f32[128,1024]{1,0:T(8,128)S(1)}, u32[]{:S(2)}, u32[]{:S(2)}) %collective-permute-start.23) | collective-permute-done | bytes 524320 | tf_op jit(solution)/shard_map/ppermute | solution.py:463
  337.5 16.7 %collective-permute-done.25.refs_3_ = f32[128,1024]{1,0:T(8,128)S(1)} collective-permute-done((f32[128,1024]{1,0:T(8,128)}, f32[128,1024]{1,0:T(8,128)S(1)}, u32[]{:S(2)}, u32[]{:S(2)}) %collective-permute-start.25) | collective-permute-done | bytes 524320 | tf_op jit(solution)/shard_map/ppermute | solution.py:463
  355.0 13.2 %reduce_columns.8.rest_4_ = f32[8,128,512]{2,1,0:T(8,128)} custom-call(s32[2]{0:T(128)} %pad_add_fusion.place, f32[128,1024]{1,0:T(8,128)} %get-tuple-element.43.refs_0_, f32[128,1024]{1,0:T(8,128)} %copy-done.14, f32[128,1024]{1,0:T(8,128)} %copy-done.16, f32[128,1024]{1,0:T(8,128)} %copy-done.20, f32[2,512,512]{2,1,0:T(8,128)} %refs_4_.11, ...), custom_call_target="tpu_custom_call" | custom-call | flops 3221225 | bytes 16777 | tf_op jit(solution)/shard_map/reduce_columns/pallas_call | solution.py:264
  376.6 9.6 %update_rows.10 = (f32[128,1024]{1,0:T(8,128)}, f32[128,1024]{1,0:T(8,128)}, f32[128,1024]{1,0:T(8,128)}, f32[128,1024]{1,0:T(8,128)}) custom-call(s32[3]{0:T(128)} %add_add_fusion.1.place, f32[4,768,1024]{2,1,0:T(8,128)} %bitcast.13, f32[2,512,1024]{2,1,0:T(8,128)} %all-gather.11.cloned.1.call-done.rest_0_, ...), custom_call_target="tpu_custom_call" | custom-call | flops 6442450 | bytes 12582 | tf_op jit(solution)/shard_map/update_rows/pallas_call | solution.py:159
  388.1 11.3 %collective-permute-done.27.refs_2_ = f32[128,1024]{1,0:T(8,128)S(1)} collective-permute-done((f32[128,1024]{1,0:T(8,128)}, f32[128,1024]{1,0:T(8,128)S(1)}, u32[]{:S(2)}, u32[]{:S(2)}) %collective-permute-start.27) | collective-permute-done | bytes 524320 | tf_op jit(solution)/shard_map/ppermute | solution.py:463
  400.2 13.2 %reduce_columns.9.rest_4_ = f32[8,128,512]{2,1,0:T(8,128)} custom-call(s32[2]{0:T(128)} %pad_add_fusion.place, f32[128,1024]{1,0:T(8,128)} %get-tuple-element.47.refs_9_.refs_0_, f32[128,1024]{1,0:T(8,128)} %copy-done.11, f32[128,1024]{1,0:T(8,128)} %copy-done.15, f32[128,1024]{1,0:T(8,128)} %collective-permute-done.28.refs_3_, f32[2,512,512]{2,1,0:T(8,128)} %refs_4_.11, ...), custom_call_target="tpu_custom_call" | custom-call | flops 3221225 | bytes 16777 | tf_op jit(solution)/shard_map/reduce_columns/pallas_call | solution.py:264
  413.3 8.8 %all-to-all-done.2.refs_10_ = f32[8,128,512]{2,1,0:T(8,128)S(1)} async-done(((f32[8,128,512]{2,1,0:T(8,128)}), f32[8,128,512]{2,1,0:T(8,128)S(1)}, u32[]{:S(2)}, u32[]{:S(2)}) %all-to-all-start.2) | async-done | bytes 2097184 | tf_op jit(solution)/shard_map/all_to_all | solution.py:485
  430.0 9.7 %update_rows.11 = (f32[128,1024]{1,0:T(8,128)}, f32[128,1024]{1,0:T(8,128)}, f32[128,1024]{1,0:T(8,128)}, f32[128,1024]{1,0:T(8,128)}) custom-call(s32[3]{0:T(128)} %add_add_fusion.1.place, f32[4,768,1024]{2,1,0:T(8,128)} %bitcast.14, f32[2,512,1024]{2,1,0:T(8,128)} %all-gather.11.cloned.1.call-done.rest_0_, ...), custom_call_target="tpu_custom_call" | custom-call | flops 6442450 | bytes 12582 | tf_op jit(solution)/shard_map/update_rows/pallas_call | solution.py:159
  441.5 11.0 %collective-permute-done.30.refs_2_ = f32[128,1024]{1,0:T(8,128)S(1)} collective-permute-done((f32[128,1024]{1,0:T(8,128)}, f32[128,1024]{1,0:T(8,128)S(1)}, u32[]{:S(2)}, u32[]{:S(2)}) %collective-permute-start.30) | collective-permute-done | bytes 524320 | tf_op jit(solution)/shard_map/ppermute | solution.py:463
  453.5 13.2 %reduce_columns.10 = f32[8,128,512]{2,1,0:T(8,128)} custom-call(s32[2]{0:T(128)} %pad_add_fusion.place, f32[128,1024]{1,0:T(8,128)} %get-tuple-element.51.refs_9_.refs_0_, f32[128,1024]{1,0:T(8,128)} %copy-done.10, f32[128,1024]{1,0:T(8,128)} %copy-done.13, f32[128,1024]{1,0:T(8,128)} %copy-done.17, f32[2,512,512]{2,1,0:T(8,128)} %refs_4_.11, ...), custom_call_target="tpu_custom_call" | custom-call | flops 3221225 | bytes 16777 | tf_op jit(solution)/shard_map/reduce_columns/pallas_call | solution.py:264
  466.8 8.8 %all-to-all-done.3.refs_9_ = f32[8,128,512]{2,1,0:T(8,128)} async-done(((f32[8,128,512]{2,1,0:T(8,128)}), f32[8,128,512]{2,1,0:T(8,128)}, u32[]{:S(2)}, u32[]{:S(2)}) %all-to-all-start.3) | async-done | bytes 2097184 | tf_op jit(solution)/shard_map/all_to_all | solution.py:485
  483.7 11.2 %collective-permute-done.32.refs_1_ = f32[128,1024]{1,0:T(8,128)S(1)} collective-permute-done((f32[128,1024]{1,0:T(8,128)S(1)}, f32[128,1024]{1,0:T(8,128)S(1)}, u32[]{:S(2)}, u32[]{:S(2)}) %collective-permute-start.32) | collective-permute-done | bytes 524320 | tf_op jit(solution)/shard_map/ppermute | solution.py:463
  494.9 11.2 %collective-permute-done.33.refs_2_ = f32[128,1024]{1,0:T(8,128)S(1)} collective-permute-done((f32[128,1024]{1,0:T(8,128)S(1)}, f32[128,1024]{1,0:T(8,128)S(1)}, u32[]{:S(2)}, u32[]{:S(2)}) %collective-permute-start.33) | collective-permute-done | bytes 524320 | tf_op jit(solution)/shard_map/ppermute | solution.py:463
  507.7 13.2 %reduce_columns.11 = f32[8,128,512]{2,1,0:T(8,128)} custom-call(s32[2]{0:T(128)} %pad_add_fusion.place, f32[128,1024]{1,0:T(8,128)} %get-tuple-element.55.refs_9_.refs_0_, f32[128,1024]{1,0:T(8,128)} %copy-done.18, f32[128,1024]{1,0:T(8,128)} %copy-done.21, f32[128,1024]{1,0:T(8,128)} %copy-done.23, f32[2,512,512]{2,1,0:T(8,128)} %refs_4_.11, ...), custom_call_target="tpu_custom_call" | custom-call | flops 3221225 | bytes 16777 | tf_op jit(solution)/shard_map/reduce_columns/pallas_call | solution.py:264
  520.9 8.3 %all-to-all-done.4 = f32[8,128,512]{2,1,0:T(8,128)} async-done(((f32[8,128,512]{2,1,0:T(8,128)}), f32[8,128,512]{2,1,0:T(8,128)}, u32[]{:S(2)}, u32[]{:S(2)}) %all-to-all-start.4) | async-done | bytes 2097184 | tf_op jit(solution)/shard_map/all_to_all | solution.py:485
  546.0 36.6 %all-to-all-done.5 = f32[8,128,512]{2,1,0:T(8,128)} async-done(((f32[8,128,512]{2,1,0:T(8,128)}), f32[8,128,512]{2,1,0:T(8,128)}, u32[]{:S(2)}, u32[]{:S(2)}) %all-to-all-start.5) | async-done | bytes 2097184 | tf_op jit(solution)/shard_map/all_to_all | solution.py:485
  (169 shorter events, 162.9 us)
Async XLA Ops:
  6.5 93.6 %all-gather.15.cloned.1.call-start = ((), (), s32[]{:S(2)}) async-start(), calls=%async_computation.9 | async-start | bytes 1310720 | tf_op jit(solution)/shard_map/all_gather | solution.py:413
  6.5 39.4 %collective-permute-start.3 = (f32[2,128,512]{2,1,0:T(8,128)}, f32[2,128,512]{2,1,0:T(8,128)}, u32[]{:S(2)}, u32[]{:S(2)}) collective-permute-start(f32[2,128,512]{2,1,0:T(8,128)} %refs_3_.5), channel_id=1, source_target_pairs={{0,8},{4,12},{8,16},{12,20},{16,24},{20,28},{1,9},{5,13},{9,17},{1... | collective-permute-start | bytes 1572872 | tf_op jit(solution)/shard_map/ppermute | solution.py:336
  12.3 35.7 %collective-permute-start.6 = (f32[2,128,512]{2,1,0:T(8,128)}, f32[2,128,512]{2,1,0:T(8,128)}, u32[]{:S(2)}, u32[]{:S(2)}) collective-permute-start(f32[2,128,512]{2,1,0:T(8,128)} %refs_3_.5), channel_id=1, source_target_pairs={{8,0},{12,4},{16,8},{20,12},{24,16},{28,20},{9,1},{13,5},{17,9},{2... | collective-permute-start | bytes 1572872 | tf_op jit(solution)/shard_map/ppermute | solution.py:337
  40.1 148.1 %all-gather.13.cloned.1.call-start = ((), (), s32[]{:S(2)}) async-start(), calls=%async_computation.8 | async-start | bytes 9175040 | tf_op jit(solution)/shard_map/all_gather | solution.py:431
  42.4 34.6 %collective-permute-start = (f32[2,128,1024]{2,1,0:T(8,128)}, f32[2,128,1024]{2,1,0:T(8,128)S(1)}, u32[]{:S(2)}, u32[]{:S(2)}) collective-permute-start(f32[2,128,1024]{2,1,0:T(8,128)} %pick_blocks.4.rest_0_), channel_id=1, source_target_pairs={{0,1},{1,0},{2,3},{3,2},{4,5},{5,4},{6,7},{7,6},{8,9},{9,8},{10,11... | collective-permute-start | bytes 3145736 | tf_op jit(solution)/shard_map/ppermute | solution.py:424
  43.9 56.2 %collective-permute-start.1 = (f32[2,128,1024]{2,1,0:T(8,128)}, f32[2,128,1024]{2,1,0:T(8,128)S(1)}, u32[]{:S(2)}, u32[]{:S(2)}) collective-permute-start(f32[2,128,1024]{2,1,0:T(8,128)} %pick_blocks.4.rest_0_), channel_id=1, source_target_pairs={{0,2},{1,3},{2,0},{3,1},{4,6},{5,7},{6,4},{7,5},{8,10},{9,11},{10,... | collective-permute-start | bytes 3145736 | tf_op jit(solution)/shard_map/ppermute | solution.py:424
  45.4 54.7 %collective-permute-start.2 = (f32[2,128,1024]{2,1,0:T(8,128)}, f32[2,128,1024]{2,1,0:T(8,128)S(1)}, u32[]{:S(2)}, u32[]{:S(2)}) collective-permute-start(f32[2,128,1024]{2,1,0:T(8,128)} %pick_blocks.4.rest_0_), channel_id=1, source_target_pairs={{0,3},{1,2},{2,1},{3,0},{4,7},{5,6},{6,5},{7,4},{8,11},{9,10},{10,... | collective-permute-start | bytes 3145736 | tf_op jit(solution)/shard_map/ppermute | solution.py:424
  58.6 41.5 %collective-permute-start.5 = (f32[2,128,512]{2,1,0:T(8,128)}, f32[2,128,512]{2,1,0:T(8,128)}, u32[]{:S(2)}, u32[]{:S(2)}) collective-permute-start(f32[2,128,512]{2,1,0:T(8,128)} %collective-permute-done.4.refs_1_), channel_id=1, source_target_pairs={{0,8},{4,12},{8,16},{12,20},{16,24},{20,28},{1,9},{5,13},{9,17},{1... | collective-permute-start | bytes 1572872 | tf_op jit(solution)/shard_map/ppermute | solution.py:336
  63.8 36.3 %collective-permute-start.8 = (f32[2,128,512]{2,1,0:T(8,128)}, f32[2,128,512]{2,1,0:T(8,128)}, u32[]{:S(2)}, u32[]{:S(2)}) collective-permute-start(f32[2,128,512]{2,1,0:T(8,128)} %collective-permute-done.7.refs_5_), channel_id=1, source_target_pairs={{8,0},{12,4},{16,8},{20,12},{24,16},{28,20},{9,1},{13,5},{17,9},{2... | collective-permute-start | bytes 1572872 | tf_op jit(solution)/shard_map/ppermute | solution.py:337
  106.4 197.9 %all-gather.9.cloned.1.call-start = ((), (), s32[]{:S(2)}) async-start(), calls=%async_computation.6 | async-start | bytes 5242880 | tf_op jit(solution)/shard_map/all_gather | solution.py:426
  188.3 41.3 %collective-permute-start.19 = (f32[4,7,128,512]{3,2,1,0:T(8,128)}, f32[4,7,128,512]{3,2,1,0:T(8,128)}, u32[]{:S(2)}, u32[]{:S(2)}) collective-permute-start(f32[4,7,128,512]{3,2,1,0:T(8,128)} %gate.1.rest_7_.refs_5_.refs_6_.refs_4_), channel_id=1, source_target_pairs={{0,4},{4,0},{8,12},{12,8},{16,20},{20,16},{24,28},{28,24},{1,5},{5... | collective-permute-start | bytes 22020104 | tf_op jit(solution)/shard_map/ppermute | solution.py:408
  190.9 22.1 %collective-permute-start.16 = (f32[128,1024]{1,0:T(8,128)S(1)}, f32[128,1024]{1,0:T(8,128)S(1)}, u32[]{:S(2)}, u32[]{:S(2)}) collective-permute-start(f32[128,1024]{1,0:T(8,128)S(1)} %copy-done.36), channel_id=1, source_target_pairs={{0,1},{1,0},{2,3},{3,2},{4,5},{5,4},{6,7},{7,6},{8,9},{9,8},{10,11... | collective-permute-start | bytes 1572872 | tf_op jit(solution)/shard_map/ppermute | solution.py:463
  193.6 22.9 %collective-permute-start.17 = (f32[128,1024]{1,0:T(8,128)S(1)}, f32[128,1024]{1,0:T(8,128)S(1)}, u32[]{:S(2)}, u32[]{:S(2)}) collective-permute-start(f32[128,1024]{1,0:T(8,128)S(1)} %copy-done.34), channel_id=1, source_target_pairs={{0,2},{1,3},{2,0},{3,1},{4,6},{5,7},{6,4},{7,5},{8,10},{9,11},{10,... | collective-permute-start | bytes 1572872 | tf_op jit(solution)/shard_map/ppermute | solution.py:463
  193.6 35.9 %collective-permute-start.18 = (f32[128,1024]{1,0:T(8,128)S(1)}, f32[128,1024]{1,0:T(8,128)S(1)}, u32[]{:S(2)}, u32[]{:S(2)}) collective-permute-start(f32[128,1024]{1,0:T(8,128)S(1)} %copy-done.32), channel_id=1, source_target_pairs={{0,3},{1,2},{2,1},{3,0},{4,7},{5,6},{6,5},{7,4},{8,11},{9,10},{10,... | collective-permute-start | bytes 1572872 | tf_op jit(solution)/shard_map/ppermute | solution.py:463
  244.2 52.8 %all-to-all-start = ((f32[8,128,512]{2,1,0:T(8,128)}), f32[8,128,512]{2,1,0:T(8,128)S(1)}, u32[]{:S(2)}, u32[]{:S(2)}) async-start(f32[8,128,512]{2,1,0:T(8,128)} %reduce_columns.6), calls=%async_computation | async-start | bytes 4194304 | tf_op jit(solution)/shard_map/all_to_all | solution.py:485
  248.0 20.6 %collective-permute-start.20 = (f32[128,1024]{1,0:T(8,128)}, f32[128,1024]{1,0:T(8,128)S(1)}, u32[]{:S(2)}, u32[]{:S(2)}) collective-permute-start(f32[128,1024]{1,0:T(8,128)} %get-tuple-element.40), channel_id=1, source_target_pairs={{0,1},{1,0},{2,3},{3,2},{4,5},{5,4},{6,7},{7,6},{8,9},{9,8},{10,11... | collective-permute-start | bytes 1572872 | tf_op jit(solution)/shard_map/ppermute | solution.py:463
  249.9 30.7 %collective-permute-start.22 = (f32[128,1024]{1,0:T(8,128)}, f32[128,1024]{1,0:T(8,128)S(1)}, u32[]{:S(2)}, u32[]{:S(2)}) collective-permute-start(f32[128,1024]{1,0:T(8,128)} %get-tuple-element.42), channel_id=1, source_target_pairs={{0,3},{1,2},{2,1},{3,0},{4,7},{5,6},{6,5},{7,4},{8,11},{9,10},{10,... | collective-permute-start | bytes 1572872 | tf_op jit(solution)/shard_map/ppermute | solution.py:463
  297.0 71.1 %all-to-all-start.1 = ((f32[8,128,512]{2,1,0:T(8,128)}), f32[8,128,512]{2,1,0:T(8,128)}, u32[]{:S(2)}, u32[]{:S(2)}) async-start(f32[8,128,512]{2,1,0:T(8,128)} %reduce_columns.7.rest_4_), calls=%async_computation.1 | async-start | bytes 4194304 | tf_op jit(solution)/shard_map/all_to_all | solution.py:485
  301.3 75.3 %all-gather.11.cloned.1.call-start = ((), (), s32[]{:S(2)}) async-start(), calls=%async_computation.7 | async-start | bytes 5242880 | tf_op jit(solution)/shard_map/all_gather | solution.py:426
  314.3 22.9 %collective-permute-start.23 = (f32[128,1024]{1,0:T(8,128)}, f32[128,1024]{1,0:T(8,128)S(1)}, u32[]{:S(2)}, u32[]{:S(2)}) collective-permute-start(f32[128,1024]{1,0:T(8,128)} %get-tuple-element.44), channel_id=1, source_target_pairs={{0,1},{1,0},{2,3},{3,2},{4,5},{5,4},{6,7},{7,6},{8,9},{9,8},{10,11... | collective-permute-start | bytes 1572872 | tf_op jit(solution)/shard_map/ppermute | solution.py:463
  314.3 23.2 %collective-permute-start.24 = (f32[128,1024]{1,0:T(8,128)}, f32[128,1024]{1,0:T(8,128)S(1)}, u32[]{:S(2)}, u32[]{:S(2)}) collective-permute-start(f32[128,1024]{1,0:T(8,128)} %get-tuple-element.45), channel_id=1, source_target_pairs={{0,2},{1,3},{2,0},{3,1},{4,6},{5,7},{6,4},{7,5},{8,10},{9,11},{10,... | collective-permute-start | bytes 1572872 | tf_op jit(solution)/shard_map/ppermute | solution.py:463
  316.0 38.1 %collective-permute-start.25 = (f32[128,1024]{1,0:T(8,128)}, f32[128,1024]{1,0:T(8,128)S(1)}, u32[]{:S(2)}, u32[]{:S(2)}) collective-permute-start(f32[128,1024]{1,0:T(8,128)} %get-tuple-element.46), channel_id=1, source_target_pairs={{0,3},{1,2},{2,1},{3,0},{4,7},{5,6},{6,5},{7,4},{8,11},{9,10},{10,... | collective-permute-start | bytes 1572872 | tf_op jit(solution)/shard_map/ppermute | solution.py:463
  368.1 54.0 %all-to-all-start.2 = ((f32[8,128,512]{2,1,0:T(8,128)}), f32[8,128,512]{2,1,0:T(8,128)S(1)}, u32[]{:S(2)}, u32[]{:S(2)}) async-start(f32[8,128,512]{2,1,0:T(8,128)} %reduce_columns.8.rest_4_), calls=%async_computation.2 | async-start | bytes 4194304 | tf_op jit(solution)/shard_map/all_to_all | solution.py:485
  373.9 25.5 %collective-permute-start.27 = (f32[128,1024]{1,0:T(8,128)}, f32[128,1024]{1,0:T(8,128)S(1)}, u32[]{:S(2)}, u32[]{:S(2)}) collective-permute-start(f32[128,1024]{1,0:T(8,128)} %get-tuple-element.49), channel_id=1, source_target_pairs={{0,2},{1,3},{2,0},{3,1},{4,6},{5,7},{6,4},{7,5},{8,10},{9,11},{10,... | collective-permute-start | bytes 1572872 | tf_op jit(solution)/shard_map/ppermute | solution.py:463
  374.3 25.0 %collective-permute-start.28 = (f32[128,1024]{1,0:T(8,128)}, f32[128,1024]{1,0:T(8,128)}, u32[]{:S(2)}, u32[]{:S(2)}) collective-permute-start(f32[128,1024]{1,0:T(8,128)} %get-tuple-element.50), channel_id=1, source_target_pairs={{0,3},{1,2},{2,1},{3,0},{4,7},{5,6},{6,5},{7,4},{8,11},{9,10},{10,... | collective-permute-start | bytes 1572872 | tf_op jit(solution)/shard_map/ppermute | solution.py:463
  422.1 53.4 %all-to-all-start.3 = ((f32[8,128,512]{2,1,0:T(8,128)}), f32[8,128,512]{2,1,0:T(8,128)}, u32[]{:S(2)}, u32[]{:S(2)}) async-start(f32[8,128,512]{2,1,0:T(8,128)} %reduce_columns.9.rest_4_), calls=%async_computation.3 | async-start | bytes 4194304 | tf_op jit(solution)/shard_map/all_to_all | solution.py:485
  427.2 25.3 %collective-permute-start.30 = (f32[128,1024]{1,0:T(8,128)}, f32[128,1024]{1,0:T(8,128)S(1)}, u32[]{:S(2)}, u32[]{:S(2)}) collective-permute-start(f32[128,1024]{1,0:T(8,128)} %get-tuple-element.53), channel_id=1, source_target_pairs={{0,2},{1,3},{2,0},{3,1},{4,6},{5,7},{6,4},{7,5},{8,10},{9,11},{10,... | collective-permute-start | bytes 1572872 | tf_op jit(solution)/shard_map/ppermute | solution.py:463
  427.7 24.8 %collective-permute-start.31 = (f32[128,1024]{1,0:T(8,128)}, f32[128,1024]{1,0:T(8,128)S(1)}, u32[]{:S(2)}, u32[]{:S(2)}) collective-permute-start(f32[128,1024]{1,0:T(8,128)} %get-tuple-element.54), channel_id=1, source_target_pairs={{0,3},{1,2},{2,1},{3,0},{4,7},{5,6},{6,5},{7,4},{8,11},{9,10},{10,... | collective-permute-start | bytes 1572872 | tf_op jit(solution)/shard_map/ppermute | solution.py:463
  475.5 53.7 %all-to-all-start.4 = ((f32[8,128,512]{2,1,0:T(8,128)}), f32[8,128,512]{2,1,0:T(8,128)}, u32[]{:S(2)}, u32[]{:S(2)}) async-start(f32[8,128,512]{2,1,0:T(8,128)} %reduce_columns.10), calls=%async_computation.4 | async-start | bytes 4194304 | tf_op jit(solution)/shard_map/all_to_all | solution.py:485
  480.9 25.2 %collective-permute-start.33 = (f32[128,1024]{1,0:T(8,128)S(1)}, f32[128,1024]{1,0:T(8,128)S(1)}, u32[]{:S(2)}, u32[]{:S(2)}) collective-permute-start(f32[128,1024]{1,0:T(8,128)S(1)} %copy-done.33), channel_id=1, source_target_pairs={{0,2},{1,3},{2,0},{3,1},{4,6},{5,7},{6,4},{7,5},{8,10},{9,11},{10,... | collective-permute-start | bytes 1572872 | tf_op jit(solution)/shard_map/ppermute | solution.py:463
  481.4 24.8 %collective-permute-start.34 = (f32[128,1024]{1,0:T(8,128)S(1)}, f32[128,1024]{1,0:T(8,128)S(1)}, u32[]{:S(2)}, u32[]{:S(2)}) collective-permute-start(f32[128,1024]{1,0:T(8,128)S(1)} %copy-done.31), channel_id=1, source_target_pairs={{0,3},{1,2},{2,1},{3,0},{4,7},{5,6},{6,5},{7,4},{8,11},{9,10},{10,... | collective-permute-start | bytes 1572872 | tf_op jit(solution)/shard_map/ppermute | solution.py:463
  529.2 53.4 %all-to-all-start.5 = ((f32[8,128,512]{2,1,0:T(8,128)}), f32[8,128,512]{2,1,0:T(8,128)}, u32[]{:S(2)}, u32[]{:S(2)}) async-start(f32[8,128,512]{2,1,0:T(8,128)} %reduce_columns.11), calls=%async_computation.5 | async-start | bytes 4194304 | tf_op jit(solution)/shard_map/all_to_all | solution.py:485
  (50 other events, 526.1 us)
Sparse Core Ops, SparseCore 0:
  40.2 33.6 all-gather.14
  106.5 76.3 all-gather.12
  191.0 72.4 all-gather.8
  303.8 68.0 all-gather.10

commit v2 on v1

--- a/solution.py
+++ b/solution.py
@@ -409,9 +409,6 @@
 
     over_cols = [[(i, i ^ s) for i in range(col_count)] for s in range(col_count)]
 
-    corner = lax.all_gather(first_factor[: panels - 1, :, :BLOCK], "rows")
-    corner = lax.all_gather(corner[width // BLOCK : depth // BLOCK], "cols")
-
     def gather_factor(group, after):
         begin, extent = begins[group[0]], sum(sizes[j] for j in group)
         if piece % BLOCK == 0:
@@ -420,17 +417,22 @@
         else:
             columns = [d * piece + begin for d in range(col_count)]
             part = jnp.concatenate([first_factor[:, :, c : c + extent] for c in columns], 2)
-        if group[0] == 0 and col_count == 4:
-            parts = [lax.ppermute(part, "cols", pairs) for pairs in over_cols[1:]]
-            return [part] + parts, col_index
-        return [lax.all_gather(part, "cols", axis=1, tiled=True)], 0
+        return [lax.all_gather(part, "cols", axis=1, tiled=True)]
 
     factors = [gather_factor(groups[0], [])]
 
-    line, last = along_line(second_factor, row_count, True, factors[0][0][1:] + [corner])
+    line, last = along_line(second_factor, row_count, True, factors[0])
     own_second = lax.all_gather(line, "cols")
 
-    own_head, _ = along_line(pick_blocks(window_slab, 0, BLOCK, [0], last), row_count, False, [])
+    corner = pick_blocks(first_factor[: panels - 1, :, :BLOCK], 2, BLOCK, [0], [line])
+    corner = lax.all_gather(corner, "rows")[width // BLOCK : depth // BLOCK]
+    if col_count == 4:
+        corner = jnp.stack([corner] + [lax.ppermute(corner, "cols", p) for p in over_cols[1:]])
+        corner = corner[jnp.arange(col_count) ^ col_index]
+    else:
+        corner = lax.all_gather(corner, "cols")
+
+    own_head, _ = along_line(pick_blocks(window_slab, 0, BLOCK, [0], [line]), row_count, False, [corner])
     other_head = from_sibling(own_head)
     solved, solved_high, solved_low = solve_rows(
         jnp.stack([core]), own_head, other_head, first_inverse, corner
@@ -444,12 +446,11 @@
 
     def update(j):
         number = next(g for g, group in enumerate(groups) if j in group)
-        after = [done[max(j - AHEAD, 1)]] if j >= AHEAD else ready
-        arrays, order = factors[number]
+        after = [done[j - AHEAD]] if j >= AHEAD else ready
         out = update_rows(
-            jnp.stack([col_index, jnp.int32(order), is_top]),
+            jnp.stack([col_index, jnp.int32(0), is_top]),
             slab,
-            arrays,
+            factors[number],
             solved_high,
             solved_low,
             own_top,
@@ -483,8 +484,8 @@
             )
         )
         results.append(lax.all_to_all(done[j], "rows", split_axis=0, concat_axis=0, tiled=True))
-        for later in range(AHEAD if j == 1 else j + AHEAD, min(j + AHEAD + 1, chunks) if j else 0):
-            update(later)
+        if j + AHEAD < chunks:
+            update(j + AHEAD)
     turned = jnp.concatenate(results, 1)
     return turned.reshape(row_count * piece, narrow)
 

time: 597 us -> 582 us (0.975)
  waiting for transfers between devices: 270 us -> 255 us
  blocking collectives: 25 us -> 18.6 us
    all_gather x3, waiting for transfers between devices: 0.02 us -> 37.8 us  [gather_factor(): return [lax.all_gather(part, 'cols', axis=1, tiled=True)]]
    ppermute x18, waiting for transfers between devices: 127 us -> 94.5 us  [update(): pieces.append(lax.ppermute(out[slot], 'cols', over_cols[slot]))]
    ppermute x3, waiting for transfers between devices: 35 us -> 23.5 us  [on_device(): lax.ppermute(corner, 'cols', p)]
    all_to_all x6, waiting for transfers between devices: 64.8 us -> 54.9 us  [on_device(): lax.all_to_all(done[j], 'rows', split_axis=0, concat_axis=0, tiled=True)]
    ppermute x6, waiting for transfers between devices: 4.18 us -> 14.1 us  [along_line(): above.append(lax.ppermute(above[-1], 'rows', down))]
    ppermute x6, waiting for transfers between devices: 34.5 us -> 27 us  [along_line(): below.append(lax.ppermute(below[-1], 'rows', up))]
    all_gather x1, blocking collectives: 25 us -> 18.6 us  [on_device(): corner = lax.all_gather(corner, 'rows')[width // BLOCK:depth // BLOCK]]
    unnamed x79 -> x91, local copies, waits for them, and re-layouts: 21.7 us -> 17.8 us
  transfers between devices with their start and end apart: 45 -> 45, of which waited for: 27 -> 31; matrix products, arithmetic and copies ran while one was open for 3% -> 3% of each run, Pallas kernels for 28% -> 29%
where the time goes in v2:
time: 582 us; the launch traced here: 577 us
  waiting for transfers between devices  255 us (44%)
  Pallas kernels  172 us (30%)
  starting transfers between devices  88.4 us (15%)
  local copies, waits for them, and re-layouts  25.9 us (4%)
  blocking collectives  18.6 us (3%)
  between operations  13.9 us (2%)
    ppermute x18, waiting for transfers between devices, update(): pieces.append(lax.ppermute(out[slot], 'cols', over_cols[slot]))  94.5 us
    pallas_call x6, Pallas kernels, reduce_columns(): pl.pallas_call(functools.partial(reduce_kernel, slots, len(views), len(af...  80 us
    pallas_call x6, Pallas kernels, update_rows(): pl.pallas_call(functools.partial(update_kernel, tops, slots, offset, len(...  59 us
    all_to_all x6, waiting for transfers between devices, on_device(): lax.all_to_all(done[j], 'rows', split_axis=0, concat_axis=0, tiled=True)  54.9 us
    all_gather x3, waiting for transfers between devices, gather_factor(): return [lax.all_gather(part, 'cols', axis=1, tiled=True)]  37.8 us
    ppermute x6, starting transfers between devices, along_line(): below.append(lax.ppermute(below[-1], 'rows', up))  28.8 us
    ppermute x6, waiting for transfers between devices, along_line(): below.append(lax.ppermute(below[-1], 'rows', up))  27 us
    all_to_all x6, starting transfers between devices, on_device(): lax.all_to_all(done[j], 'rows', split_axis=0, concat_axis=0, tiled=True)  26.5 us
  transfers between devices with their start and end apart: 45, of which 31 were waited for; matrix products, arithmetic and copies ran while one was open for 3% of the time, Pallas kernels for 29%

profile of v2, /device:TPU:0, one launch (start us, length us, event | category | flops | bytes accessed | tf_op | source)
XLA Modules:
  0.0 577.2 jit_solution(631109690715673121)
XLA Ops:
  15.2 9.8 %collective-permute-done.refs_2_ = f32[2,128,512]{2,1,0:T(8,128)S(1)} collective-permute-done((f32[2,128,512]{2,1,0:T(8,128)S(1)}, f32[2,128,512]{2,1,0:T(8,128)S(1)}, u32[]{:S(2)}, u32[]{:S(2)}) %collective-permute-start) | collective-permute-done | bytes 524320 | tf_op jit(solution)/shard_map/ppermute | solution.py:336
  30.8 9.0 %collective-permute-done.1.refs_1_ = f32[2,128,512]{2,1,0:T(8,128)S(1)} collective-permute-done((f32[2,128,512]{2,1,0:T(8,128)S(1)}, f32[2,128,512]{2,1,0:T(8,128)S(1)}, u32[]{:S(2)}, u32[]{:S(2)}) %collective-permute-start.1) | collective-permute-done | bytes 524320 | tf_op jit(solution)/shard_map/ppermute | solution.py:336
  45.6 8.1 %collective-permute-done.2.refs_0_ = f32[2,128,512]{2,1,0:T(8,128)S(1)} collective-permute-done((f32[2,128,512]{2,1,0:T(8,128)S(1)}, f32[2,128,512]{2,1,0:T(8,128)S(1)}, u32[]{:S(2)}, u32[]{:S(2)}) %collective-permute-start.2) | collective-permute-done | bytes 524320 | tf_op jit(solution)/shard_map/ppermute | solution.py:336
  57.8 6.8 %all-gather.7.cloned.1.call-done.refs_7_.rest_0_ = f32[2,512,1024]{2,1,0:T(8,128)} async-done(((f32[2,128,1024]{2,1,0:T(8,128)}), f32[2,512,1024]{2,1,0:T(8,128)}) %all-gather.7.cloned.1.call-update) | async-done | bytes 4194320 | tf_op jit(solution)/shard_map/all_gather | solution.py:420
  77.5 9.9 %collective-permute-done.9.refs_4_ = f32[128,1024]{1,0:T(8,128)S(1)} collective-permute-done((f32[128,1024]{1,0:T(8,128)}, f32[128,1024]{1,0:T(8,128)S(1)}, u32[]{:S(2)}, u32[]{:S(2)}) %collective-permute-start.9) | collective-permute-done | bytes 524320 | tf_op jit(solution)/shard_map/ppermute | solution.py:337
  96.3 18.6 %all-gather = f32[8,128,128]{2,1,0:T(8,128)S(1)} all-gather(f32[1,128,128]{2,1,0:T(8,128)} %pick_blocks.7), channel_id=2, replica_groups=mesh['rows'=8,'cols'=4] {'rows'}, dimensions={0}, use_global_device_ids=true | all-gather | bytes 589824 | tf_op jit(solution)/shard_map/all_gather | solution.py:428
  125.7 10.9 %collective-permute-done.13 = f32[4,1,128,128]{3,2,0,1:T(8,128)S(1)} collective-permute-done((f32[4,1,128,128]{3,2,0,1:T(8,128)S(1)}, f32[4,1,128,128]{3,2,0,1:T(8,128)S(1)}, u32[]{:S(2)}, u32[]{:S(2)}) %collective-permute-start.13) | collective-permute-done | bytes 262176 | tf_op jit(solution)/shard_map/ppermute | solution.py:430
  138.4 10.8 %collective-permute-done.14 = f32[4,1,128,128]{3,2,0,1:T(8,128)S(1)} collective-permute-done((f32[4,1,128,128]{3,2,0,1:T(8,128)S(1)}, f32[4,1,128,128]{3,2,0,1:T(8,128)S(1)}, u32[]{:S(2)}, u32[]{:S(2)}) %collective-permute-start.14) | collective-permute-done | bytes 262176 | tf_op jit(solution)/shard_map/ppermute | solution.py:430
  162.4 13.9 %solve_rows.1 = (f32[1024,1024]{1,0:T(8,128)}, bf16[1024,1024]{1,0:T(8,128)(2,1)}, bf16[1024,1024]{1,0:T(8,128)(2,1)}) custom-call(s32[1]{0:T(128)} %bitcast.1.place, f32[4,128,1024]{2,1,0:T(8,128)} %in_order.3.own, f32[4,128,1024]{2,1,0:T(8,128)} %copy-done.4, f32[2,512,512]{2,1,0:T(8,128)} %inverse_ref.1, f32[4,4,1,128,128]{4,3,2,1,0:T(8,128)} %bitcast.27), custom_call_target="tpu_custom_call" | custom-call | flops 4831838 | bytes 16777 | tf_op jit(solution)/shard_map/solve_rows/pallas_call | solution.py:86
  178.2 9.7 %update_rows.6 = (f32[128,1024]{1,0:T(8,128)}, f32[128,1024]{1,0:T(8,128)}, f32[128,1024]{1,0:T(8,128)}, f32[128,1024]{1,0:T(8,128)}) custom-call(s32[3]{0:T(128)} %pad_add_fusion.1.place, f32[4,768,1024]{2,1,0:T(8,128)} %bitcast.20, f32[2,512,1024]{2,1,0:T(8,128)} %all-gather.7.cloned.1.call-done.refs_7_.rest_0_, ...), custom_call_target="tpu_custom_call" | custom-call | flops 6442450 | bytes 12582 | tf_op jit(solution)/shard_map/update_rows/pallas_call | solution.py:159
  194.9 10.3 %update_rows.7 = (f32[128,1024]{1,0:T(8,128)}, f32[128,1024]{1,0:T(8,128)}, f32[128,1024]{1,0:T(8,128)}, f32[128,1024]{1,0:T(8,128)}) custom-call(s32[3]{0:T(128)} %pad_add_fusion.1.place, f32[4,768,1024]{2,1,0:T(8,128)} %bitcast.21, f32[2,512,1024]{2,1,0:T(8,128)} %all-gather.7.cloned.1.call-done.refs_7_.rest_0_, ...), custom_call_target="tpu_custom_call" | custom-call | flops 6442450 | bytes 12582 | tf_op jit(solution)/shard_map/update_rows/pallas_call | solution.py:159
  214.8 13.4 %collective-permute-done.18.refs_3_ = f32[128,1024]{1,0:T(8,128)S(1)} collective-permute-done((f32[128,1024]{1,0:T(8,128)S(1)}, f32[128,1024]{1,0:T(8,128)S(1)}, u32[]{:S(2)}, u32[]{:S(2)}) %collective-permute-start.18) | collective-permute-done | bytes 524320 | tf_op jit(solution)/shard_map/ppermute | solution.py:464
  229.1 13.9 %reduce_columns.6.rest_4_ = f32[8,128,512]{2,1,0:T(8,128)} custom-call(s32[2]{0:T(128)} %pad_add_fusion.place, f32[128,1024]{1,0:T(8,128)} %get-tuple-element.35.refs_1_.refs_0_, f32[128,1024]{1,0:T(8,128)} %copy-done.5, f32[128,1024]{1,0:T(8,128)} %copy-done.7, f32[128,1024]{1,0:T(8,128)} %copy-done.14, f32[2,512,512]{2,1,0:T(8,128)} %refs_4_.11, ...), custom_call_target="tpu_custom_call" | custom-call | flops 3221225 | bytes 16777 | tf_op jit(solution)/shard_map/reduce_columns/pallas_call | solution.py:264
  250.3 13.6 %all-gather.9.cloned.1.call-done.rest_0_ = f32[2,512,1024]{2,1,0:T(8,128)} async-done(((f32[2,128,1024]{2,1,0:T(8,128)}), f32[2,512,1024]{2,1,0:T(8,128)}) %all-gather.9.cloned.1.call-update) | async-done | bytes 4194320 | tf_op jit(solution)/shard_map/all_gather | solution.py:420
  263.9 9.7 %update_rows.8 = (f32[128,1024]{1,0:T(8,128)}, f32[128,1024]{1,0:T(8,128)}, f32[128,1024]{1,0:T(8,128)}, f32[128,1024]{1,0:T(8,128)}) custom-call(s32[3]{0:T(128)} %pad_add_fusion.1.place, f32[4,768,1024]{2,1,0:T(8,128)} %bitcast.22, f32[2,512,1024]{2,1,0:T(8,128)} %all-gather.9.cloned.1.call-done.rest_0_, bf16[1024,1024]{1,0:T(8,128)(2,1)} %get-tuple-element.32.rest_1_, ...), custom_call_target="tpu_custom_call" | custom-call | flops 6442450 | bytes 12582 | tf_op jit(solution)/shard_map/update_rows/pallas_call | solution.py:159
  273.6 6.7 %collective-permute-done.22.refs_3_ = f32[128,1024]{1,0:T(8,128)} collective-permute-done((f32[128,1024]{1,0:T(8,128)}, f32[128,1024]{1,0:T(8,128)}, u32[]{:S(2)}, u32[]{:S(2)}) %collective-permute-start.22) | collective-permute-done | bytes 524320 | tf_op jit(solution)/shard_map/ppermute | solution.py:464
  280.2 13.3 %reduce_columns.7.rest_4_ = f32[8,128,512]{2,1,0:T(8,128)} custom-call(s32[2]{0:T(128)} %pad_add_fusion.place, f32[128,1024]{1,0:T(8,128)} %get-tuple-element.39.refs_9_.refs_0_, f32[128,1024]{1,0:T(8,128)} %copy-done.8, f32[128,1024]{1,0:T(8,128)} %copy-done.11, f32[128,1024]{1,0:T(8,128)} %collective-permute-done.22.refs_3_, f32[2,512,512]{2,1,0:T(8,128)} %refs_4_.11, ...), custom_call_target="tpu_custom_call" | custom-call | flops 3221225 | bytes 16777 | tf_op jit(solution)/shard_map/reduce_columns/pallas_call | solution.py:264
  306.0 10.0 %update_rows.9 = (f32[128,1024]{1,0:T(8,128)}, f32[128,1024]{1,0:T(8,128)}, f32[128,1024]{1,0:T(8,128)}, f32[128,1024]{1,0:T(8,128)}) custom-call(s32[3]{0:T(128)} %pad_add_fusion.1.place, f32[4,768,1024]{2,1,0:T(8,128)} %bitcast.23, f32[2,512,1024]{2,1,0:T(8,128)} %all-gather.9.cloned.1.call-done.rest_0_, bf16[1024,1024]{1,0:T(8,128)(2,1)} %get-tuple-element.32.rest_1_, ...), custom_call_target="tpu_custom_call" | custom-call | flops 6442450 | bytes 12582 | tf_op jit(solution)/shard_map/update_rows/pallas_call | solution.py:159
  322.7 16.0 %collective-permute-done.25.refs_3_ = f32[128,1024]{1,0:T(8,128)S(1)} collective-permute-done((f32[128,1024]{1,0:T(8,128)S(1)}, f32[128,1024]{1,0:T(8,128)S(1)}, u32[]{:S(2)}, u32[]{:S(2)}) %collective-permute-start.25) | collective-permute-done | bytes 524320 | tf_op jit(solution)/shard_map/ppermute | solution.py:464
  339.5 13.2 %reduce_columns.8.rest_4_ = f32[8,128,512]{2,1,0:T(8,128)} custom-call(s32[2]{0:T(128)} %pad_add_fusion.place, f32[128,1024]{1,0:T(8,128)} %get-tuple-element.43.refs_9_.refs_0_, f32[128,1024]{1,0:T(8,128)} %copy-done.12, f32[128,1024]{1,0:T(8,128)} %copy-done.15, f32[128,1024]{1,0:T(8,128)} %copy-done.19, f32[2,512,512]{2,1,0:T(8,128)} %refs_4_.11, ...), custom_call_target="tpu_custom_call" | custom-call | flops 3221225 | bytes 16777 | tf_op jit(solution)/shard_map/reduce_columns/pallas_call | solution.py:264
  361.4 17.3 %all-gather.11.cloned.1.call-done.rest_0_ = f32[2,512,1024]{2,1,0:T(8,128)} async-done(((f32[2,128,1024]{2,1,0:T(8,128)}), f32[2,512,1024]{2,1,0:T(8,128)}) %all-gather.11.cloned.1.call-update) | async-done | bytes 4194320 | tf_op jit(solution)/shard_map/all_gather | solution.py:420
  378.7 9.7 %update_rows.10 = (f32[128,1024]{1,0:T(8,128)}, f32[128,1024]{1,0:T(8,128)}, f32[128,1024]{1,0:T(8,128)}, f32[128,1024]{1,0:T(8,128)}) custom-call(s32[3]{0:T(128)} %pad_add_fusion.1.place, f32[4,768,1024]{2,1,0:T(8,128)} %bitcast.24, f32[2,512,1024]{2,1,0:T(8,128)} %all-gather.11.cloned.1.call-done.rest_0_, bf16[1024,1024]{1,0:T(8,128)(2,1)} %get-tuple-element.32.rest_1_, ...), custom_call_target="tpu_custom_call" | custom-call | flops 6442450 | bytes 12582 | tf_op jit(solution)/shard_map/update_rows/pallas_call | solution.py:159
  393.2 13.2 %reduce_columns.9.rest_4_ = f32[8,128,512]{2,1,0:T(8,128)} custom-call(s32[2]{0:T(128)} %pad_add_fusion.place, f32[128,1024]{1,0:T(8,128)} %get-tuple-element.47.refs_9_.refs_0_, f32[128,1024]{1,0:T(8,128)} %copy-done.9, f32[128,1024]{1,0:T(8,128)} %copy-done.13, f32[128,1024]{1,0:T(8,128)} %collective-permute-done.28.refs_3_, f32[2,512,512]{2,1,0:T(8,128)} %refs_4_.11, ...), custom_call_target="tpu_custom_call" | custom-call | flops 3221225 | bytes 16777 | tf_op jit(solution)/shard_map/reduce_columns/pallas_call | solution.py:264
  414.8 9.7 %update_rows.11 = (f32[128,1024]{1,0:T(8,128)}, f32[128,1024]{1,0:T(8,128)}, f32[128,1024]{1,0:T(8,128)}, f32[128,1024]{1,0:T(8,128)}) custom-call(s32[3]{0:T(128)} %pad_add_fusion.1.place, f32[4,768,1024]{2,1,0:T(8,128)} %bitcast.25, f32[2,512,1024]{2,1,0:T(8,128)} %all-gather.11.cloned.1.call-done.rest_0_, bf16[1024,1024]{1,0:T(8,128)(2,1)} %get-tuple-element.32.rest_1_, ...), custom_call_target="tpu_custom_call" | custom-call | flops 6442450 | bytes 12582 | tf_op jit(solution)/shard_map/update_rows/pallas_call | solution.py:159
  426.2 10.6 %collective-permute-done.30.refs_2_ = f32[128,1024]{1,0:T(8,128)S(1)} collective-permute-done((f32[128,1024]{1,0:T(8,128)}, f32[128,1024]{1,0:T(8,128)S(1)}, u32[]{:S(2)}, u32[]{:S(2)}) %collective-permute-start.30) | collective-permute-done | bytes 524320 | tf_op jit(solution)/shard_map/ppermute | solution.py:464
  439.1 13.4 %reduce_columns.10 = f32[8,128,512]{2,1,0:T(8,128)} custom-call(s32[2]{0:T(128)} %pad_add_fusion.place, f32[128,1024]{1,0:T(8,128)} %get-tuple-element.51.refs_9_.refs_0_, f32[128,1024]{1,0:T(8,128)} %copy-done.6, f32[128,1024]{1,0:T(8,128)} %copy-done.10, f32[128,1024]{1,0:T(8,128)} %copy-done.16, f32[2,512,512]{2,1,0:T(8,128)} %refs_4_.11, ...), custom_call_target="tpu_custom_call" | custom-call | flops 3221225 | bytes 16777 | tf_op jit(solution)/shard_map/reduce_columns/pallas_call | solution.py:264
  452.5 7.7 %all-to-all-done.3.refs_9_ = f32[8,128,512]{2,1,0:T(8,128)} async-done(((f32[8,128,512]{2,1,0:T(8,128)}), f32[8,128,512]{2,1,0:T(8,128)}, u32[]{:S(2)}, u32[]{:S(2)}) %all-to-all-start.3) | async-done | bytes 2097184 | tf_op jit(solution)/shard_map/all_to_all | solution.py:486
  468.5 11.1 %collective-permute-done.32.refs_1_ = f32[128,1024]{1,0:T(8,128)S(1)} collective-permute-done((f32[128,1024]{1,0:T(8,128)S(1)}, f32[128,1024]{1,0:T(8,128)S(1)}, u32[]{:S(2)}, u32[]{:S(2)}) %collective-permute-start.32) | collective-permute-done | bytes 524320 | tf_op jit(solution)/shard_map/ppermute | solution.py:464
  479.7 10.7 %collective-permute-done.33.refs_2_ = f32[128,1024]{1,0:T(8,128)S(1)} collective-permute-done((f32[128,1024]{1,0:T(8,128)S(1)}, f32[128,1024]{1,0:T(8,128)S(1)}, u32[]{:S(2)}, u32[]{:S(2)}) %collective-permute-start.33) | collective-permute-done | bytes 524320 | tf_op jit(solution)/shard_map/ppermute | solution.py:464
  492.7 13.2 %reduce_columns.11 = f32[8,128,512]{2,1,0:T(8,128)} custom-call(s32[2]{0:T(128)} %pad_add_fusion.place, f32[128,1024]{1,0:T(8,128)} %get-tuple-element.55.refs_9_.refs_0_, f32[128,1024]{1,0:T(8,128)} %copy-done.17, f32[128,1024]{1,0:T(8,128)} %copy-done.18, f32[128,1024]{1,0:T(8,128)} %copy-done.20, f32[2,512,512]{2,1,0:T(8,128)} %refs_4_.11, ...), custom_call_target="tpu_custom_call" | custom-call | flops 3221225 | bytes 16777 | tf_op jit(solution)/shard_map/reduce_columns/pallas_call | solution.py:264
  506.0 7.9 %all-to-all-done.4 = f32[8,128,512]{2,1,0:T(8,128)} async-done(((f32[8,128,512]{2,1,0:T(8,128)}), f32[8,128,512]{2,1,0:T(8,128)}, u32[]{:S(2)}, u32[]{:S(2)}) %all-to-all-start.4) | async-done | bytes 2097184 | tf_op jit(solution)/shard_map/all_to_all | solution.py:486
  530.7 36.6 %all-to-all-done.5 = f32[8,128,512]{2,1,0:T(8,128)} async-done(((f32[8,128,512]{2,1,0:T(8,128)}), f32[8,128,512]{2,1,0:T(8,128)}, u32[]{:S(2)}, u32[]{:S(2)}) %all-to-all-start.5) | async-done | bytes 2097184 | tf_op jit(solution)/shard_map/all_to_all | solution.py:486
  (185 shorter events, 174.6 us)
Async XLA Ops:
  6.5 58.1 %all-gather.7.cloned.1.call-start = ((), (), s32[]{:S(2)}) async-start(), calls=%async_computation.6 | async-start | bytes 5242880 | tf_op jit(solution)/shard_map/all_gather | solution.py:420
  8.9 179.1 %all-gather.13.cloned.1.call-start = ((), (), s32[]{:S(2)}) async-start(), calls=%async_computation.9 | async-start | bytes 9175040 | tf_op jit(solution)/shard_map/all_gather | solution.py:425
  69.7 194.1 %all-gather.9.cloned.1.call-start = ((), (), s32[]{:S(2)}) async-start(), calls=%async_computation.7 | async-start | bytes 5242880 | tf_op jit(solution)/shard_map/all_gather | solution.py:420
  87.4 27.4 %collective-permute-start.10 = (f32[128,1024]{1,0:T(8,128)S(1)}, f32[128,1024]{1,0:T(8,128)S(1)}, u32[]{:S(2)}, u32[]{:S(2)}) collective-permute-start(f32[128,1024]{1,0:T(8,128)S(1)} %collective-permute-done.9.refs_4_), channel_id=1, source_target_pairs={{8,0},{12,4},{16,8},{20,12},{24,16},{28,20},{9,1},{13,5},{17,9},{2... | collective-permute-start | bytes 1572872 | tf_op jit(solution)/shard_map/ppermute | solution.py:337
  88.7 27.4 %collective-permute-start.7 = (f32[128,1024]{1,0:T(8,128)S(1)}, f32[128,1024]{1,0:T(8,128)S(1)}, u32[]{:S(2)}, u32[]{:S(2)}) collective-permute-start(f32[128,1024]{1,0:T(8,128)S(1)} %collective-permute-done.6.refs_2_), channel_id=1, source_target_pairs={{0,8},{4,12},{8,16},{12,20},{16,24},{20,28},{1,9},{5,13},{9,17},{1... | collective-permute-start | bytes 1572872 | tf_op jit(solution)/shard_map/ppermute | solution.py:336
  114.9 37.8 %collective-permute-start.11 = (f32[128,1024]{1,0:T(8,128)S(1)}, f32[128,1024]{1,0:T(8,128)}, u32[]{:S(2)}, u32[]{:S(2)}) collective-permute-start(f32[128,1024]{1,0:T(8,128)S(1)} %collective-permute-done.10.refs_5_), channel_id=1, source_target_pairs={{8,0},{12,4},{16,8},{20,12},{24,16},{28,20},{9,1},{13,5},{17,9},{2... | collective-permute-start | bytes 1572872 | tf_op jit(solution)/shard_map/ppermute | solution.py:337
  116.2 36.5 %collective-permute-start.8 = (f32[128,1024]{1,0:T(8,128)S(1)}, f32[128,1024]{1,0:T(8,128)}, u32[]{:S(2)}, u32[]{:S(2)}) collective-permute-start(f32[128,1024]{1,0:T(8,128)S(1)} %collective-permute-done.7.refs_1_), channel_id=1, source_target_pairs={{0,8},{4,12},{8,16},{12,20},{16,24},{20,28},{1,9},{5,13},{9,17},{1... | collective-permute-start | bytes 1572872 | tf_op jit(solution)/shard_map/ppermute | solution.py:336
  124.2 24.9 %collective-permute-start.14 = (f32[4,1,128,128]{3,2,0,1:T(8,128)S(1)}, f32[4,1,128,128]{3,2,0,1:T(8,128)S(1)}, u32[]{:S(2)}, u32[]{:S(2)}) collective-permute-start(f32[4,1,128,128]{3,2,0,1:T(8,128)S(1)} %get-tuple-element.60), channel_id=1, source_target_pairs={{0,3},{1,2},{2,1},{3,0},{4,7},{5,6},{6,5},{7,4},{8,11},{9,10},{10,... | collective-permute-start | bytes 786440 | tf_op jit(solution)/shard_map/ppermute | solution.py:430
  188.0 40.3 %collective-permute-start.19 = (f32[4,7,128,512]{3,2,1,0:T(8,128)}, f32[4,7,128,512]{3,2,1,0:T(8,128)}, u32[]{:S(2)}, u32[]{:S(2)}) collective-permute-start(f32[4,7,128,512]{3,2,1,0:T(8,128)} %gate.1.rest_4_.refs_5_.refs_6_.refs_4_), channel_id=1, source_target_pairs={{0,4},{4,0},{8,12},{12,8},{16,20},{20,16},{24,28},{28,24},{1,5},{5... | collective-permute-start | bytes 22020104 | tf_op jit(solution)/shard_map/ppermute | solution.py:408
  190.7 20.9 %collective-permute-start.16 = (f32[128,1024]{1,0:T(8,128)S(1)}, f32[128,1024]{1,0:T(8,128)S(1)}, u32[]{:S(2)}, u32[]{:S(2)}) collective-permute-start(f32[128,1024]{1,0:T(8,128)S(1)} %copy-done.42), channel_id=1, source_target_pairs={{0,1},{1,0},{2,3},{3,2},{4,5},{5,4},{6,7},{7,6},{8,9},{9,8},{10,11... | collective-permute-start | bytes 1572872 | tf_op jit(solution)/shard_map/ppermute | solution.py:464
  192.2 22.6 %collective-permute-start.17 = (f32[128,1024]{1,0:T(8,128)S(1)}, f32[128,1024]{1,0:T(8,128)S(1)}, u32[]{:S(2)}, u32[]{:S(2)}) collective-permute-start(f32[128,1024]{1,0:T(8,128)S(1)} %copy-done.41), channel_id=1, source_target_pairs={{0,2},{1,3},{2,0},{3,1},{4,6},{5,7},{6,4},{7,5},{8,10},{9,11},{10,... | collective-permute-start | bytes 1572872 | tf_op jit(solution)/shard_map/ppermute | solution.py:464
  192.8 35.5 %collective-permute-start.18 = (f32[128,1024]{1,0:T(8,128)S(1)}, f32[128,1024]{1,0:T(8,128)S(1)}, u32[]{:S(2)}, u32[]{:S(2)}) collective-permute-start(f32[128,1024]{1,0:T(8,128)S(1)} %copy-done.39), channel_id=1, source_target_pairs={{0,3},{1,2},{2,1},{3,0},{4,7},{5,6},{6,5},{7,4},{8,11},{9,10},{10,... | collective-permute-start | bytes 1572872 | tf_op jit(solution)/shard_map/ppermute | solution.py:464
  242.9 52.8 %all-to-all-start = ((f32[8,128,512]{2,1,0:T(8,128)}), f32[8,128,512]{2,1,0:T(8,128)S(1)}, u32[]{:S(2)}, u32[]{:S(2)}) async-start(f32[8,128,512]{2,1,0:T(8,128)} %reduce_columns.6.rest_4_), calls=%async_computation | async-start | bytes 4194304 | tf_op jit(solution)/shard_map/all_to_all | solution.py:486
  246.7 26.8 %collective-permute-start.20 = (f32[128,1024]{1,0:T(8,128)}, f32[128,1024]{1,0:T(8,128)S(1)}, u32[]{:S(2)}, u32[]{:S(2)}) collective-permute-start(f32[128,1024]{1,0:T(8,128)} %get-tuple-element.40), channel_id=1, source_target_pairs={{0,1},{1,0},{2,3},{3,2},{4,5},{5,4},{6,7},{7,6},{8,9},{9,8},{10,11... | collective-permute-start | bytes 1572872 | tf_op jit(solution)/shard_map/ppermute | solution.py:464
  246.8 26.8 %collective-permute-start.21 = (f32[128,1024]{1,0:T(8,128)}, f32[128,1024]{1,0:T(8,128)S(1)}, u32[]{:S(2)}, u32[]{:S(2)}) collective-permute-start(f32[128,1024]{1,0:T(8,128)} %get-tuple-element.41), channel_id=1, source_target_pairs={{0,2},{1,3},{2,0},{3,1},{4,6},{5,7},{6,4},{7,5},{8,10},{9,11},{10,... | collective-permute-start | bytes 1572872 | tf_op jit(solution)/shard_map/ppermute | solution.py:464
  248.1 32.1 %collective-permute-start.22 = (f32[128,1024]{1,0:T(8,128)}, f32[128,1024]{1,0:T(8,128)}, u32[]{:S(2)}, u32[]{:S(2)}) collective-permute-start(f32[128,1024]{1,0:T(8,128)} %get-tuple-element.42), channel_id=1, source_target_pairs={{0,3},{1,2},{2,1},{3,0},{4,7},{5,6},{6,5},{7,4},{8,11},{9,10},{10,... | collective-permute-start | bytes 1572872 | tf_op jit(solution)/shard_map/ppermute | solution.py:464
  295.7 57.0 %all-to-all-start.1 = ((f32[8,128,512]{2,1,0:T(8,128)}), f32[8,128,512]{2,1,0:T(8,128)}, u32[]{:S(2)}, u32[]{:S(2)}) async-start(f32[8,128,512]{2,1,0:T(8,128)} %reduce_columns.7.rest_4_), calls=%async_computation.1 | async-start | bytes 4194304 | tf_op jit(solution)/shard_map/all_to_all | solution.py:486
  300.1 78.7 %all-gather.11.cloned.1.call-start = ((), (), s32[]{:S(2)}) async-start(), calls=%async_computation.8 | async-start | bytes 5242880 | tf_op jit(solution)/shard_map/all_gather | solution.py:420
  302.4 19.6 %collective-permute-start.23 = (f32[128,1024]{1,0:T(8,128)}, f32[128,1024]{1,0:T(8,128)S(1)}, u32[]{:S(2)}, u32[]{:S(2)}) collective-permute-start(f32[128,1024]{1,0:T(8,128)} %get-tuple-element.44), channel_id=1, source_target_pairs={{0,1},{1,0},{2,3},{3,2},{4,5},{5,4},{6,7},{7,6},{8,9},{9,8},{10,11... | collective-permute-start | bytes 1572872 | tf_op jit(solution)/shard_map/ppermute | solution.py:464
  302.5 20.2 %collective-permute-start.24 = (f32[128,1024]{1,0:T(8,128)S(1)}, f32[128,1024]{1,0:T(8,128)S(1)}, u32[]{:S(2)}, u32[]{:S(2)}) collective-permute-start(f32[128,1024]{1,0:T(8,128)S(1)} %copy-done.36), channel_id=1, source_target_pairs={{0,2},{1,3},{2,0},{3,1},{4,6},{5,7},{6,4},{7,5},{8,10},{9,11},{10,... | collective-permute-start | bytes 1572872 | tf_op jit(solution)/shard_map/ppermute | solution.py:464
  303.9 34.8 %collective-permute-start.25 = (f32[128,1024]{1,0:T(8,128)S(1)}, f32[128,1024]{1,0:T(8,128)S(1)}, u32[]{:S(2)}, u32[]{:S(2)}) collective-permute-start(f32[128,1024]{1,0:T(8,128)S(1)} %copy-done.35), channel_id=1, source_target_pairs={{0,3},{1,2},{2,1},{3,0},{4,7},{5,6},{6,5},{7,4},{8,11},{9,10},{10,... | collective-permute-start | bytes 1572872 | tf_op jit(solution)/shard_map/ppermute | solution.py:464
  352.7 54.1 %all-to-all-start.2 = ((f32[8,128,512]{2,1,0:T(8,128)}), f32[8,128,512]{2,1,0:T(8,128)S(1)}, u32[]{:S(2)}, u32[]{:S(2)}) async-start(f32[8,128,512]{2,1,0:T(8,128)} %reduce_columns.8.rest_4_), calls=%async_computation.2 | async-start | bytes 4194304 | tf_op jit(solution)/shard_map/all_to_all | solution.py:486
  357.8 30.6 %collective-permute-start.26 = (f32[128,1024]{1,0:T(8,128)}, f32[128,1024]{1,0:T(8,128)S(1)}, u32[]{:S(2)}, u32[]{:S(2)}) collective-permute-start(f32[128,1024]{1,0:T(8,128)} %get-tuple-element.48), channel_id=1, source_target_pairs={{0,1},{1,0},{2,3},{3,2},{4,5},{5,4},{6,7},{7,6},{8,9},{9,8},{10,11... | collective-permute-start | bytes 1572872 | tf_op jit(solution)/shard_map/ppermute | solution.py:464
  359.3 29.1 %collective-permute-start.27 = (f32[128,1024]{1,0:T(8,128)}, f32[128,1024]{1,0:T(8,128)S(1)}, u32[]{:S(2)}, u32[]{:S(2)}) collective-permute-start(f32[128,1024]{1,0:T(8,128)} %get-tuple-element.49), channel_id=1, source_target_pairs={{0,2},{1,3},{2,0},{3,1},{4,6},{5,7},{6,4},{7,5},{8,10},{9,11},{10,... | collective-permute-start | bytes 1572872 | tf_op jit(solution)/shard_map/ppermute | solution.py:464
  360.5 32.7 %collective-permute-start.28 = (f32[128,1024]{1,0:T(8,128)}, f32[128,1024]{1,0:T(8,128)}, u32[]{:S(2)}, u32[]{:S(2)}) collective-permute-start(f32[128,1024]{1,0:T(8,128)} %get-tuple-element.50), channel_id=1, source_target_pairs={{0,3},{1,2},{2,1},{3,0},{4,7},{5,6},{6,5},{7,4},{8,11},{9,10},{10,... | collective-permute-start | bytes 1572872 | tf_op jit(solution)/shard_map/ppermute | solution.py:464
  406.8 53.4 %all-to-all-start.3 = ((f32[8,128,512]{2,1,0:T(8,128)}), f32[8,128,512]{2,1,0:T(8,128)}, u32[]{:S(2)}, u32[]{:S(2)}) async-start(f32[8,128,512]{2,1,0:T(8,128)} %reduce_columns.9.rest_4_), calls=%async_computation.3 | async-start | bytes 4194304 | tf_op jit(solution)/shard_map/all_to_all | solution.py:486
  412.7 24.1 %collective-permute-start.30 = (f32[128,1024]{1,0:T(8,128)}, f32[128,1024]{1,0:T(8,128)S(1)}, u32[]{:S(2)}, u32[]{:S(2)}) collective-permute-start(f32[128,1024]{1,0:T(8,128)} %get-tuple-element.53), channel_id=1, source_target_pairs={{0,2},{1,3},{2,0},{3,1},{4,6},{5,7},{6,4},{7,5},{8,10},{9,11},{10,... | collective-permute-start | bytes 1572872 | tf_op jit(solution)/shard_map/ppermute | solution.py:464
  413.9 24.4 %collective-permute-start.31 = (f32[128,1024]{1,0:T(8,128)}, f32[128,1024]{1,0:T(8,128)S(1)}, u32[]{:S(2)}, u32[]{:S(2)}) collective-permute-start(f32[128,1024]{1,0:T(8,128)} %get-tuple-element.54), channel_id=1, source_target_pairs={{0,3},{1,2},{2,1},{3,0},{4,7},{5,6},{6,5},{7,4},{8,11},{9,10},{10,... | collective-permute-start | bytes 1572872 | tf_op jit(solution)/shard_map/ppermute | solution.py:464
  460.2 53.7 %all-to-all-start.4 = ((f32[8,128,512]{2,1,0:T(8,128)}), f32[8,128,512]{2,1,0:T(8,128)}, u32[]{:S(2)}, u32[]{:S(2)}) async-start(f32[8,128,512]{2,1,0:T(8,128)} %reduce_columns.10), calls=%async_computation.4 | async-start | bytes 4194304 | tf_op jit(solution)/shard_map/all_to_all | solution.py:486
  466.4 23.9 %collective-permute-start.33 = (f32[128,1024]{1,0:T(8,128)S(1)}, f32[128,1024]{1,0:T(8,128)S(1)}, u32[]{:S(2)}, u32[]{:S(2)}) collective-permute-start(f32[128,1024]{1,0:T(8,128)S(1)} %copy-done.38), channel_id=1, source_target_pairs={{0,2},{1,3},{2,0},{3,1},{4,6},{5,7},{6,4},{7,5},{8,10},{9,11},{10,... | collective-permute-start | bytes 1572872 | tf_op jit(solution)/shard_map/ppermute | solution.py:464
  467.6 24.3 %collective-permute-start.34 = (f32[128,1024]{1,0:T(8,128)S(1)}, f32[128,1024]{1,0:T(8,128)S(1)}, u32[]{:S(2)}, u32[]{:S(2)}) collective-permute-start(f32[128,1024]{1,0:T(8,128)S(1)} %copy-done.37), channel_id=1, source_target_pairs={{0,3},{1,2},{2,1},{3,0},{4,7},{5,6},{6,5},{7,4},{8,11},{9,10},{10,... | collective-permute-start | bytes 1572872 | tf_op jit(solution)/shard_map/ppermute | solution.py:464
  513.9 53.4 %all-to-all-start.5 = ((f32[8,128,512]{2,1,0:T(8,128)}), f32[8,128,512]{2,1,0:T(8,128)}, u32[]{:S(2)}, u32[]{:S(2)}) async-start(f32[8,128,512]{2,1,0:T(8,128)} %reduce_columns.11), calls=%async_computation.5 | async-start | bytes 4194304 | tf_op jit(solution)/shard_map/all_to_all | solution.py:486
  (56 other events, 770.4 us)
Sparse Core Ops, SparseCore 0:
  9.2 55.3 all-gather.6
  69.9 90.3 all-gather.12
  190.8 73.0 all-gather.8
  302.6 76.1 all-gather.10

commit v3 on v2

--- a/solution.py
+++ b/solution.py
@@ -26,6 +26,13 @@
         return lax.dot_general(a, b, contract, preferred_element_type=jnp.float32)
 
     return one(left[0], right[0]) + (one(left[0], right[1]) + one(left[1], right[0]))
+
+
+def stacked_product(both, high, low):
+    rows = both.shape[0] // 2
+    first = jnp.dot(both[...], high, preferred_element_type=jnp.float32)
+    second = jnp.dot(both[:rows], low, preferred_element_type=jnp.float32)
+    return first[:rows] + (first[rows:] + second)
 
 
 def whole(shape):
@@ -68,7 +75,14 @@
         for p in range(k):
             block = (cor_high[p, rows], cor_low[p, rows])
             current = current - product(block, parts[p])
-        answer = product((inv_high[k], inv_low[k]), split(current))
+        half = width // 2
+        known = split(current)
+        upper = product(
+            (inv_high[k, :half, :half], inv_low[k, :half, :half]),
+            (known[0][:half], known[1][:half]),
+        )
+        lower = product((inv_high[k, half:], inv_low[k, half:]), known)
+        answer = jnp.concatenate([upper, lower], 0)
         parts.append(split(answer))
         solved_ref[rows] = answer
         high_ref[rows] = parts[k][0]
@@ -108,32 +122,24 @@
     )(place, own, other, inverse, corner)
 
 
-def update_kernel(tops, slots, offset, count, place, slab, *rest):
-    factors = rest[:count]
-    high, low, own_top = rest[count : count + 3]
-    outs = rest[-slots - 3 : -3]
-    factor_high, factor_low, total = rest[-3:]
+def update_kernel(tops, slots, offset, place, slab, factor, high, low, own_top, *rest):
+    outs = rest[-slots - 2 : -2]
+    both, total = rest[-2:]
+    rows = both.shape[0] // 2
+    chunk = rows // slots
 
     @pl.when(pl.program_id(0) == 0)
     def _():
-        panels, share, columns = factors[0].shape
-        held = columns // slots
-        chunk = slab.shape[1]
+        held = factor.shape[1] // slots
         for dest in range(slots):
-            rows = slice(dest * chunk, (dest + 1) * chunk)
+            at = dest * chunk
             taken = slice(dest * held + offset, dest * held + offset + chunk)
-            for panel in range(panels):
-                for slot in range(count):
-                    start = pl.multiple_of((place[1] ^ slot) * share, BLOCK)
-                    at = pl.ds(panel * share * count + start, share)
-                    parts = split(factors[slot][panel, :, taken].T)
-                    factor_high[rows, at], factor_low[rows, at] = parts
-
-    answer = product((factor_high[...], factor_low[...]), (high[...], low[...]))
-    total[...] = answer.reshape(total.shape)
-    for dest, first, count, flag in tops:
-
-        @pl.when(place[2 + flag] > 0)
+            both[at : at + chunk], both[rows + at : rows + at + chunk] = split(factor[:, taken].T)
+
+    total[...] = stacked_product(both, high[...], low[...]).reshape(total.shape)
+    for dest, first, count in tops:
+
+        @pl.when(place[2] > 0)
         def _():
             total[dest, :count] = slab[dest, :count] - own_top[first : first + count]
 
@@ -142,7 +148,7 @@
         outs[slot][...] = slab[dest] - total[dest]
 
 
-def update_rows(place, slab, factors, high, low, own_top, begin, chunk, offset, after):
+def update_rows(place, slab, factor, high, low, solved, begin, chunk, offset, after):
     slots, piece, breadth = slab.shape
     depth = high.shape[0]
     tile = min(breadth, 256)
@@ -150,29 +156,25 @@
     tops = []
     for dest in range(slots):
         first = dest * piece + begin
-        for b in range(own_top.shape[0] // BLOCK):
-            start, stop = max(first, b * BLOCK), min(first + chunk, (b + 1) * BLOCK)
-            if start < stop:
-                assert start == first
-                tops.append((dest, start, stop - start, b))
+        if first < BLOCK:
+            tops.append((dest, first, min(chunk, BLOCK - first)))
     columns = pl.BlockSpec((depth, tile), lambda i, _: (0, i))
     return pl.pallas_call(
-        functools.partial(update_kernel, tops, slots, offset, len(factors)),
+        functools.partial(update_kernel, tops, slots, offset),
         grid_spec=pltpu.PrefetchScalarGridSpec(
             num_scalar_prefetch=1,
             grid=(breadth // tile,),
             in_specs=[
                 pl.BlockSpec((slots, chunk, tile), lambda i, _: (0, begin // chunk, i)),
-                *[whole(f.shape) for f in factors],
+                whole(factor.shape),
                 columns,
                 columns,
-                pl.BlockSpec((own_top.shape[0], tile), lambda i, _: (0, i)),
+                pl.BlockSpec((BLOCK, tile), lambda i, place: (place[1], i)),
             ]
             + [ANY] * len(after),
             out_specs=[pl.BlockSpec((chunk, tile), lambda i, _: (0, i))] * slots,
             scratch_shapes=[
-                pltpu.VMEM((slots * chunk, depth), jnp.bfloat16),
-                pltpu.VMEM((slots * chunk, depth), jnp.bfloat16),
+                pltpu.VMEM((2 * slots * chunk, depth), jnp.bfloat16),
                 pltpu.VMEM((slots, chunk, tile), jnp.float32),
             ],
         ),
@@ -180,7 +182,7 @@
         compiler_params=compiler_params(60),
         cost_estimate=cost(12 * slots * chunk * depth * breadth, 12 * depth * breadth),
         name="update_rows",
-    )(place, slab, *factors, high, low, own_top, *after)
+    )(place, slab, factor, high, low, solved, *after)
 
 
 def reduce_kernel(slots, views, extra, place, *refs):
@@ -188,7 +190,7 @@
     inverse = refs[slots]
     own = refs[slots + 1 : slots + 1 + views]
     other = refs[slots + 1 + views : slots + 1 + 2 * views]
-    out, current, high, low, factor_high, factor_low = refs[slots + 1 + 2 * views + extra :]
+    out, current, both, factor_high, factor_low = refs[slots + 1 + 2 * views + extra :]
     step = pl.program_id(0)
     chunk, breadth = pieces[0].shape
     width = inverse.shape[1]
@@ -226,14 +228,14 @@
     def _():
         first = product(split(current[:, :width]), split(inverse[0]), CONTRACT_COLS)
         first_parts = split(first)
-        high[:, :width], low[:, :width] = first_parts
+        both[:chunk, :width], both[chunk:, :width] = first_parts
         store(first, 0)
         for group in range(width // narrow, depth // narrow):
             load(group, 1)
             columns = slice(group * narrow, (group + 1) * narrow)
             current[:, columns] -= product(first_parts, (factor_high[:width], factor_low[:width]))
         second = product(split(current[:, width:]), split(inverse[1]), CONTRACT_COLS)
-        high[:, width:], low[:, width:] = split(second)
+        both[:chunk, width:], both[chunk:, width:] = split(second)
         store(second, width)
 
     @pl.when(step > 0)
@@ -241,7 +243,7 @@
         for group in range(depth // narrow):
             load(group, 2)
             columns = slice(group * narrow, (group + 1) * narrow)
-            part = product((high[...], low[...]), (factor_high[...], factor_low[...]))
+            part = stacked_product(both, factor_high[...], factor_low[...])
             out[group] = current[:, columns] - part
 
 
@@ -273,8 +275,7 @@
             out_specs=pl.BlockSpec((depth // narrow, chunk, narrow), lambda i, _: (i, 0, 0)),
             scratch_shapes=[
                 pltpu.VMEM((chunk, depth), jnp.float32),
-                pltpu.VMEM((chunk, depth), jnp.bfloat16),
-                pltpu.VMEM((chunk, depth), jnp.bfloat16),
+                pltpu.VMEM((2 * chunk, depth), jnp.bfloat16),
                 pltpu.VMEM((depth, narrow), jnp.bfloat16),
                 pltpu.VMEM((depth, narrow), jnp.bfloat16),
             ],
@@ -327,16 +328,20 @@
     )(place, *pieces, *after)
 
 
-def along_line(block, row_count, skipped, after):
+def along_lines(blocks, row_count):
     chips = row_count // 2
     up = [(i, i + 2) for i in range(row_count - 2)]
     down = [(i + 2, i) for i in range(row_count - 2)]
-    below, above = [block], [block]
-    for _ in range(chips - 1):
-        below.append(lax.ppermute(below[-1], "rows", up))
-        above.append(lax.ppermute(above[-1], "rows", down))
-    place = jnp.stack([lax.axis_index("rows") // 2])
-    return in_order(place, below[:0:-1] + above, skipped, after), [below[-1], above[-1]]
+    below, above = [[b] for b in blocks], [[b] for b in blocks]
+    for step in range(chips - 1):
+        for n in range(len(blocks)):
+            below[n].append(lax.ppermute(below[n][-1], "rows", up))
+            above[n].append(lax.ppermute(above[n][-1], "rows", down))
+        if step < chips - 2:
+            brought = [side[n][-1] for n in range(1, len(blocks)) for side in (below, above)]
+            below[0][-1] = gate(below[0][-1], brought)
+            above[0][-1] = gate(above[0][-1], brought)
+    return [below[n][:0:-1] + above[n] for n in range(len(blocks))]
 
 
 def gate_kernel(*refs):
@@ -417,29 +422,32 @@
         else:
             columns = [d * piece + begin for d in range(col_count)]
             part = jnp.concatenate([first_factor[:, :, c : c + extent] for c in columns], 2)
-        return [lax.all_gather(part, "cols", axis=1, tiled=True)]
+        part = lax.all_gather(part, "cols", axis=1, tiled=True)
+        return part.reshape(depth, -1)
 
     factors = [gather_factor(groups[0], [])]
 
-    line, last = along_line(second_factor, row_count, True, factors[0])
+    second_line, head_line = along_lines([second_factor, window_slab[:BLOCK]], row_count)
+    chip = jnp.stack([row_index // 2])
+
+    line = in_order(chip, second_line, True, [factors[0]])
     own_second = lax.all_gather(line, "cols")
 
-    corner = pick_blocks(first_factor[: panels - 1, :, :BLOCK], 2, BLOCK, [0], [line])
+    corner = pick_blocks(first_factor[: panels - 1, :, :BLOCK], 2, BLOCK, [0], second_line[-2:-1])
     corner = lax.all_gather(corner, "rows")[width // BLOCK : depth // BLOCK]
+    own_head = in_order(chip, head_line, False, [corner])
+    other_head = from_sibling(own_head)
     if col_count == 4:
         corner = jnp.stack([corner] + [lax.ppermute(corner, "cols", p) for p in over_cols[1:]])
         corner = corner[jnp.arange(col_count) ^ col_index]
     else:
         corner = lax.all_gather(corner, "cols")
 
-    own_head, _ = along_line(pick_blocks(window_slab, 0, BLOCK, [0], [line]), row_count, False, [corner])
-    other_head = from_sibling(own_head)
     solved, solved_high, solved_low = solve_rows(
         jnp.stack([core]), own_head, other_head, first_inverse, corner
     )
-    start = row_index * BLOCK
-    own_top = lax.dynamic_slice_in_dim(solved, jnp.minimum(start, depth - BLOCK), BLOCK, 0)
-    is_top = (start < depth).astype(jnp.int32)
+    is_top = (row_index * BLOCK < depth).astype(jnp.int32)
+    own_block = jnp.minimum(row_index, depth // BLOCK - 1)
 
     slab = window_slab.reshape(col_count, piece, breadth)
     updated, done, results, ready = [], [], [], []
@@ -448,12 +456,12 @@
         number = next(g for g, group in enumerate(groups) if j in group)
         after = [done[j - AHEAD]] if j >= AHEAD else ready
         out = update_rows(
-            jnp.stack([col_index, jnp.int32(0), is_top]),
+            jnp.stack([col_index, own_block, is_top]),
             slab,
             factors[number],
             solved_high,
             solved_low,
-            own_top,
+            solved,
             begins[j],
             sizes[j],
             begins[j] - begins[groups[number][0]],

time: 582 us -> 568 us (0.976)
  waiting for transfers between devices: 255 us -> 239 us
  local copies, waits for them, and re-layouts: 25.9 us -> 32 us
    unnamed x91 -> x103, local copies, waits for them, and re-layouts: 17.8 us -> 23.8 us
  transfers between devices with their start and end apart: 45 -> 45, of which waited for: 31 -> 30; matrix products, arithmetic and copies ran while one was open for 3% -> 4% of each run, Pallas kernels for 29% -> 28%
where the time goes in v3:
time: 568 us; the launch traced here: 563 us
  waiting for transfers between devices  239 us (42%)
  Pallas kernels  168 us (30%)
  starting transfers between devices  89.8 us (16%)
  local copies, waits for them, and re-layouts  32 us (6%)
  blocking collectives  18.1 us (3%)
  between operations  13.9 us (2%)
    ppermute x18, waiting for transfers between devices, update(): pieces.append(lax.ppermute(out[slot], 'cols', over_cols[slot]))  94.6 us
    pallas_call x6, Pallas kernels, reduce_columns(): pl.pallas_call(functools.partial(reduce_kernel, slots, len(views), len(af...  79.2 us
    pallas_call x6, Pallas kernels, update_rows(): pl.pallas_call(functools.partial(update_kernel, tops, slots, offset), gri...  58.4 us
    all_to_all x6, waiting for transfers between devices, on_device(): lax.all_to_all(done[j], 'rows', split_axis=0, concat_axis=0, tiled=True)  54.1 us
    all_gather x3, waiting for transfers between devices, gather_factor(): part = lax.all_gather(part, 'cols', axis=1, tiled=True)  32.6 us
    ppermute x6, waiting for transfers between devices, along_lines(): above[n].append(lax.ppermute(above[n][-1], 'rows', down))  31.4 us
    ppermute x6, starting transfers between devices, along_lines(): below[n].append(lax.ppermute(below[n][-1], 'rows', up))  28.8 us
    all_to_all x6, starting transfers between devices, on_device(): lax.all_to_all(done[j], 'rows', split_axis=0, concat_axis=0, tiled=True)  28 us
  transfers between devices with their start and end apart: 45, of which 30 were waited for; matrix products, arithmetic and copies ran while one was open for 4% of the time, Pallas kernels for 28%

profile of v3, /device:TPU:0, one launch (start us, length us, event | category | flops | bytes accessed | tf_op | source)
XLA Modules:
  0.0 563.4 jit_solution(16934782877023791910)
XLA Ops:
  11.2 5.6 collective-permute-start
  33.6 5.3 collective-permute-done.6.refs_0_
  51.6 8.9 %collective-permute-done.7.refs_0_ = f32[2,128,512]{2,1,0:T(8,128)S(1)} collective-permute-done((f32[2,128,512]{2,1,0:T(8,128)}, f32[2,128,512]{2,1,0:T(8,128)S(1)}, u32[]{:S(2)}, u32[]{:S(2)}) %collective-permute-start.7) | collective-permute-done | bytes 524320 | tf_op jit(solution)/shard_map/ppermute | solution.py:339
  68.0 8.6 %collective-permute-done.18.refs_6_ = f32[2,128,512]{2,1,0:T(8,128)S(1)} collective-permute-done((f32[2,128,512]{2,1,0:T(8,128)}, f32[2,128,512]{2,1,0:T(8,128)S(1)}, u32[]{:S(2)}, u32[]{:S(2)}) %collective-permute-start.18) | collective-permute-done | bytes 524320 | tf_op jit(solution)/shard_map/ppermute | solution.py:339
  93.9 18.1 %all-gather = f32[8,128,128]{2,1,0:T(8,128)S(1)} all-gather(f32[1,128,128]{2,1,0:T(8,128)} %pick_blocks.5), channel_id=2, replica_groups=mesh['rows'=8,'cols'=4] {'rows'}, dimensions={0}, use_global_device_ids=true | all-gather | bytes 589824 | tf_op jit(solution)/shard_map/all_gather | solution.py:437
  122.3 7.5 %collective-permute-done.11 = f32[4,1,128,128]{3,2,0,1:T(8,128)S(1)} collective-permute-done((f32[4,1,128,128]{3,2,0,1:T(8,128)S(1)}, f32[4,1,128,128]{3,2,0,1:T(8,128)S(1)}, u32[]{:S(2)}, u32[]{:S(2)}) %collective-permute-start.11) | collective-permute-done | bytes 262176 | tf_op jit(solution)/shard_map/ppermute | solution.py:441
  129.8 10.5 %collective-permute-done.9 = f32[4,1,128,128]{3,2,0,1:T(8,128)S(1)} collective-permute-done((f32[4,1,128,128]{3,2,0,1:T(8,128)S(1)}, f32[4,1,128,128]{3,2,0,1:T(8,128)S(1)}, u32[]{:S(2)}, u32[]{:S(2)}) %collective-permute-start.9) | collective-permute-done | bytes 262176 | tf_op jit(solution)/shard_map/ppermute | solution.py:441
  145.4 12.7 %solve_rows.1 = (f32[1024,1024]{1,0:T(8,128)}, bf16[1024,1024]{1,0:T(8,128)(2,1)}, bf16[1024,1024]{1,0:T(8,128)(2,1)}) custom-call(s32[1]{0:T(128)} %bitcast.1.place, f32[4,128,1024]{2,1,0:T(8,128)} %in_order.2.own, f32[4,128,1024]{2,1,0:T(8,128)} %copy-done.15, f32[2,512,512]{2,1,0:T(8,128)} %inverse_ref.1, f32[4,4,1,128,128]{4,3,2,1,0:T(8,128)} %bitcast.40), custom_call_target="tpu_custom_call" | custom-call | flops 4831838 | bytes 16777 | tf_op jit(solution)/shard_map/solve_rows/pallas_call | solution.py:100
  158.0 9.8 %update_rows.6 = (f32[128,1024]{1,0:T(8,128)}, f32[128,1024]{1,0:T(8,128)}, f32[128,1024]{1,0:T(8,128)}, f32[128,1024]{1,0:T(8,128)}) custom-call(s32[3]{0:T(128)} %pad_add_fusion.1.place, f32[4,768,1024]{2,1,0:T(8,128)} %bitcast.27, f32[1024,1024]{1,0:T(8,128)} %bitcast.34, bf16[1024,1024]{1,0:T(8,128)(2,1)} %get-tuple-element.32.high, ...), custom_call_target="tpu_custom_call" | custom-call | flops 6442450 | bytes 12582 | tf_op jit(solution)/shard_map/update_rows/pallas_call | solution.py:162
  179.4 9.8 %update_rows.7 = (f32[128,1024]{1,0:T(8,128)}, f32[128,1024]{1,0:T(8,128)}, f32[128,1024]{1,0:T(8,128)}, f32[128,1024]{1,0:T(8,128)}) custom-call(s32[3]{0:T(128)} %pad_add_fusion.1.place, f32[4,768,1024]{2,1,0:T(8,128)} %bitcast.28, f32[1024,1024]{1,0:T(8,128)} %bitcast.35, bf16[1024,1024]{1,0:T(8,128)(2,1)} %get-tuple-element.32.high, ...), custom_call_target="tpu_custom_call" | custom-call | flops 6442450 | bytes 12582 | tf_op jit(solution)/shard_map/update_rows/pallas_call | solution.py:162
  196.5 16.1 %collective-permute-done.14.refs_3_ = f32[128,1024]{1,0:T(8,128)S(1)} collective-permute-done((f32[128,1024]{1,0:T(8,128)S(1)}, f32[128,1024]{1,0:T(8,128)S(1)}, u32[]{:S(2)}, u32[]{:S(2)}) %collective-permute-start.14) | collective-permute-done | bytes 524320 | tf_op jit(solution)/shard_map/ppermute | solution.py:472
  213.4 13.2 %reduce_columns.6.rest_0_ = f32[8,128,512]{2,1,0:T(8,128)} custom-call(s32[2]{0:T(128)} %pad_add_fusion.place, f32[128,1024]{1,0:T(8,128)} %get-tuple-element.35.refs_1_.refs_0_, f32[128,1024]{1,0:T(8,128)} %copy-done.17, f32[128,1024]{1,0:T(8,128)} %copy-done.19, f32[128,1024]{1,0:T(8,128)} %copy-done.26, f32[2,512,512]{2,1,0:T(8,128)} %refs_4_.11, ...), custom_call_target="tpu_custom_call" | custom-call | flops 3221225 | bytes 16777 | tf_op jit(solution)/shard_map/reduce_columns/pallas_call | solution.py:266
  235.4 16.6 %all-gather.9.cloned.1.call-done = f32[2,512,1024]{2,1,0:T(8,128)} async-done(((f32[2,128,1024]{2,1,0:T(8,128)}), f32[2,512,1024]{2,1,0:T(8,128)}) %all-gather.9.cloned.1.call-update) | async-done | bytes 4194320 | tf_op jit(solution)/shard_map/all_gather | solution.py:425
  252.0 9.7 %update_rows.8 = (f32[128,1024]{1,0:T(8,128)}, f32[128,1024]{1,0:T(8,128)}, f32[128,1024]{1,0:T(8,128)}, f32[128,1024]{1,0:T(8,128)}) custom-call(s32[3]{0:T(128)} %pad_add_fusion.1.place, f32[4,768,1024]{2,1,0:T(8,128)} %bitcast.29, f32[1024,1024]{1,0:T(8,128)} %bitcast.36, bf16[1024,1024]{1,0:T(8,128)(2,1)} %get-tuple-element.32.high, ...), custom_call_target="tpu_custom_call" | custom-call | flops 6442450 | bytes 12582 | tf_op jit(solution)/shard_map/update_rows/pallas_call | solution.py:162
  266.9 13.1 %reduce_columns.7.rest_0_ = f32[8,128,512]{2,1,0:T(8,128)} custom-call(s32[2]{0:T(128)} %pad_add_fusion.place, f32[128,1024]{1,0:T(8,128)} %get-tuple-element.39.refs_9_.refs_0_, f32[128,1024]{1,0:T(8,128)} %copy-done.20, f32[128,1024]{1,0:T(8,128)} %copy-done.23, f32[128,1024]{1,0:T(8,128)} %collective-permute-done.22.refs_3_, f32[2,512,512]{2,1,0:T(8,128)} %refs_4_.11, ...), custom_call_target="tpu_custom_call" | custom-call | flops 3221225 | bytes 16777 | tf_op jit(solution)/shard_map/reduce_columns/pallas_call | solution.py:266
  291.2 9.7 %update_rows.9 = (f32[128,1024]{1,0:T(8,128)}, f32[128,1024]{1,0:T(8,128)}, f32[128,1024]{1,0:T(8,128)}, f32[128,1024]{1,0:T(8,128)}) custom-call(s32[3]{0:T(128)} %pad_add_fusion.1.place, f32[4,768,1024]{2,1,0:T(8,128)} %bitcast.30, f32[1024,1024]{1,0:T(8,128)} %bitcast.37, bf16[1024,1024]{1,0:T(8,128)(2,1)} %get-tuple-element.32.high, ...), custom_call_target="tpu_custom_call" | custom-call | flops 6442450 | bytes 12582 | tf_op jit(solution)/shard_map/update_rows/pallas_call | solution.py:162
  301.0 5.6 collective-permute-done.23.refs_1_
  310.2 14.7 %collective-permute-done.25.refs_3_ = f32[128,1024]{1,0:T(8,128)S(1)} collective-permute-done((f32[128,1024]{1,0:T(8,128)S(1)}, f32[128,1024]{1,0:T(8,128)S(1)}, u32[]{:S(2)}, u32[]{:S(2)}) %collective-permute-start.25) | collective-permute-done | bytes 524320 | tf_op jit(solution)/shard_map/ppermute | solution.py:472
  325.7 13.2 %reduce_columns.8.rest_0_ = f32[8,128,512]{2,1,0:T(8,128)} custom-call(s32[2]{0:T(128)} %pad_add_fusion.place, f32[128,1024]{1,0:T(8,128)} %get-tuple-element.43.refs_9_.refs_0_, f32[128,1024]{1,0:T(8,128)} %copy-done.24, f32[128,1024]{1,0:T(8,128)} %copy-done.27, f32[128,1024]{1,0:T(8,128)} %copy-done.31, f32[2,512,512]{2,1,0:T(8,128)} %refs_4_.11, ...), custom_call_target="tpu_custom_call" | custom-call | flops 3221225 | bytes 16777 | tf_op jit(solution)/shard_map/reduce_columns/pallas_call | solution.py:266
  347.5 16.0 %all-gather.11.cloned.1.call-done = f32[2,512,1024]{2,1,0:T(8,128)} async-done(((f32[2,128,1024]{2,1,0:T(8,128)}), f32[2,512,1024]{2,1,0:T(8,128)}) %all-gather.11.cloned.1.call-update) | async-done | bytes 4194320 | tf_op jit(solution)/shard_map/all_gather | solution.py:425
  363.5 9.7 %update_rows.10 = (f32[128,1024]{1,0:T(8,128)}, f32[128,1024]{1,0:T(8,128)}, f32[128,1024]{1,0:T(8,128)}, f32[128,1024]{1,0:T(8,128)}) custom-call(s32[3]{0:T(128)} %pad_add_fusion.1.place, f32[4,768,1024]{2,1,0:T(8,128)} %bitcast.31, f32[1024,1024]{1,0:T(8,128)} %bitcast.38, bf16[1024,1024]{1,0:T(8,128)(2,1)} %get-tuple-element.32.high, ...), custom_call_target="tpu_custom_call" | custom-call | flops 6442450 | bytes 12582 | tf_op jit(solution)/shard_map/update_rows/pallas_call | solution.py:162
  373.2 5.5 collective-permute-done.28.refs_3_
  378.7 13.2 %reduce_columns.9.rest_0_ = f32[8,128,512]{2,1,0:T(8,128)} custom-call(s32[2]{0:T(128)} %pad_add_fusion.place, f32[128,1024]{1,0:T(8,128)} %get-tuple-element.47.refs_9_.refs_0_, f32[128,1024]{1,0:T(8,128)} %copy-done.21, f32[128,1024]{1,0:T(8,128)} %copy-done.25, f32[128,1024]{1,0:T(8,128)} %collective-permute-done.28.refs_3_, f32[2,512,512]{2,1,0:T(8,128)} %refs_4_.11, ...), custom_call_target="tpu_custom_call" | custom-call | flops 3221225 | bytes 16777 | tf_op jit(solution)/shard_map/reduce_columns/pallas_call | solution.py:266
  400.9 9.7 %update_rows.11 = (f32[128,1024]{1,0:T(8,128)}, f32[128,1024]{1,0:T(8,128)}, f32[128,1024]{1,0:T(8,128)}, f32[128,1024]{1,0:T(8,128)}) custom-call(s32[3]{0:T(128)} %pad_add_fusion.1.place, f32[4,768,1024]{2,1,0:T(8,128)} %bitcast.32, f32[1024,1024]{1,0:T(8,128)} %bitcast.39, bf16[1024,1024]{1,0:T(8,128)(2,1)} %get-tuple-element.32.high, ...), custom_call_target="tpu_custom_call" | custom-call | flops 6442450 | bytes 12582 | tf_op jit(solution)/shard_map/update_rows/pallas_call | solution.py:162
  412.4 11.8 %collective-permute-done.30.refs_2_ = f32[128,1024]{1,0:T(8,128)S(1)} collective-permute-done((f32[128,1024]{1,0:T(8,128)}, f32[128,1024]{1,0:T(8,128)S(1)}, u32[]{:S(2)}, u32[]{:S(2)}) %collective-permute-start.30) | collective-permute-done | bytes 524320 | tf_op jit(solution)/shard_map/ppermute | solution.py:472
  425.1 13.2 %reduce_columns.10 = f32[8,128,512]{2,1,0:T(8,128)} custom-call(s32[2]{0:T(128)} %pad_add_fusion.place, f32[128,1024]{1,0:T(8,128)} %get-tuple-element.51.refs_9_.refs_0_, f32[128,1024]{1,0:T(8,128)} %copy-done.18, f32[128,1024]{1,0:T(8,128)} %copy-done.22, f32[128,1024]{1,0:T(8,128)} %copy-done.28, f32[2,512,512]{2,1,0:T(8,128)} %refs_4_.11, ...), custom_call_target="tpu_custom_call" | custom-call | flops 3221225 | bytes 16777 | tf_op jit(solution)/shard_map/reduce_columns/pallas_call | solution.py:266
  438.3 8.1 %all-to-all-done.3.refs_9_ = f32[8,128,512]{2,1,0:T(8,128)} async-done(((f32[8,128,512]{2,1,0:T(8,128)}), f32[8,128,512]{2,1,0:T(8,128)}, u32[]{:S(2)}, u32[]{:S(2)}) %all-to-all-start.3) | async-done | bytes 2097184 | tf_op jit(solution)/shard_map/all_to_all | solution.py:494
  454.6 11.2 %collective-permute-done.32.refs_1_ = f32[128,1024]{1,0:T(8,128)S(1)} collective-permute-done((f32[128,1024]{1,0:T(8,128)S(1)}, f32[128,1024]{1,0:T(8,128)S(1)}, u32[]{:S(2)}, u32[]{:S(2)}) %collective-permute-start.32) | collective-permute-done | bytes 524320 | tf_op jit(solution)/shard_map/ppermute | solution.py:472
  465.9 11.9 %collective-permute-done.33.refs_2_ = f32[128,1024]{1,0:T(8,128)S(1)} collective-permute-done((f32[128,1024]{1,0:T(8,128)S(1)}, f32[128,1024]{1,0:T(8,128)S(1)}, u32[]{:S(2)}, u32[]{:S(2)}) %collective-permute-start.33) | collective-permute-done | bytes 524320 | tf_op jit(solution)/shard_map/ppermute | solution.py:472
  479.4 13.2 %reduce_columns.11 = f32[8,128,512]{2,1,0:T(8,128)} custom-call(s32[2]{0:T(128)} %pad_add_fusion.place, f32[128,1024]{1,0:T(8,128)} %get-tuple-element.55.refs_9_.refs_0_, f32[128,1024]{1,0:T(8,128)} %copy-done.29, f32[128,1024]{1,0:T(8,128)} %copy-done.30, f32[128,1024]{1,0:T(8,128)} %copy-done.32, f32[2,512,512]{2,1,0:T(8,128)} %refs_4_.11, ...), custom_call_target="tpu_custom_call" | custom-call | flops 3221225 | bytes 16777 | tf_op jit(solution)/shard_map/reduce_columns/pallas_call | solution.py:266
  492.7 7.5 %all-to-all-done.4 = f32[8,128,512]{2,1,0:T(8,128)} async-done(((f32[8,128,512]{2,1,0:T(8,128)}), f32[8,128,512]{2,1,0:T(8,128)}, u32[]{:S(2)}, u32[]{:S(2)}) %all-to-all-start.4) | async-done | bytes 2097184 | tf_op jit(solution)/shard_map/all_to_all | solution.py:494
  516.9 36.6 %all-to-all-done.5 = f32[8,128,512]{2,1,0:T(8,128)} async-done(((f32[8,128,512]{2,1,0:T(8,128)}), f32[8,128,512]{2,1,0:T(8,128)}, u32[]{:S(2)}, u32[]{:S(2)}) %all-to-all-start.5) | async-done | bytes 2097184 | tf_op jit(solution)/shard_map/all_to_all | solution.py:494
  (200 shorter events, 173.5 us)
Async XLA Ops:
  6.5 72.2 %all-gather.7.cloned.1.call-start = ((), (), s32[]{:S(2)}) async-start(), calls=%async_computation.6 | async-start | bytes 5242880 | tf_op jit(solution)/shard_map/all_gather | solution.py:425
  8.8 163.9 %all-gather.13.cloned.1.call-start = ((), (), s32[]{:S(2)}) async-start(), calls=%async_computation.9 | async-start | bytes 9175040 | tf_op jit(solution)/shard_map/all_gather | solution.py:434
  16.8 22.0 %collective-permute-start.6 = (f32[2,128,512]{2,1,0:T(8,128)}, f32[2,128,512]{2,1,0:T(8,128)S(1)}, u32[]{:S(2)}, u32[]{:S(2)}) collective-permute-start(f32[2,128,512]{2,1,0:T(8,128)} %refs_3_.5), channel_id=1, source_target_pairs={{8,0},{12,4},{16,8},{20,12},{24,16},{28,20},{9,1},{13,5},{17,9},{2... | collective-permute-start | bytes 1572872 | tf_op jit(solution)/shard_map/ppermute | solution.py:339
  18.1 22.8 %collective-permute-start.15 = (f32[2,128,512]{2,1,0:T(8,128)}, f32[2,128,512]{2,1,0:T(8,128)S(1)}, u32[]{:S(2)}, u32[]{:S(2)}) collective-permute-start(f32[2,128,512]{2,1,0:T(8,128)} %refs_3_.5), channel_id=1, source_target_pairs={{0,8},{4,12},{8,16},{12,20},{16,24},{20,28},{1,9},{5,13},{9,17},{1... | collective-permute-start | bytes 1572872 | tf_op jit(solution)/shard_map/ppermute | solution.py:338
  27.6 22.5 %collective-permute-start.4 = (f32[128,1024]{1,0:T(8,128)S(1)}, f32[128,1024]{1,0:T(8,128)S(1)}, u32[]{:S(2)}, u32[]{:S(2)}) collective-permute-start(f32[128,1024]{1,0:T(8,128)S(1)} %collective-permute-done.3.refs_2_.refs_4_), channel_id=1, source_target_pairs={{8,0},{12,4},{16,8},{20,12},{24,16},{28,20},{9,1},{13,5},{17,9},{2... | collective-permute-start | bytes 1572872 | tf_op jit(solution)/shard_map/ppermute | solution.py:339
  29.1 22.5 %collective-permute-start.1 = (f32[128,1024]{1,0:T(8,128)S(1)}, f32[128,1024]{1,0:T(8,128)S(1)}, u32[]{:S(2)}, u32[]{:S(2)}) collective-permute-start(f32[128,1024]{1,0:T(8,128)S(1)} %collective-permute-done.refs_1_.refs_2_), channel_id=1, source_target_pairs={{0,8},{4,12},{8,16},{12,20},{16,24},{20,28},{1,9},{5,13},{9,17},{1... | collective-permute-start | bytes 1572872 | tf_op jit(solution)/shard_map/ppermute | solution.py:338
  39.6 20.9 %collective-permute-start.7 = (f32[2,128,512]{2,1,0:T(8,128)}, f32[2,128,512]{2,1,0:T(8,128)S(1)}, u32[]{:S(2)}, u32[]{:S(2)}) collective-permute-start(f32[2,128,512]{2,1,0:T(8,128)} %gate.5.refs_4_), channel_id=1, source_target_pairs={{8,0},{12,4},{16,8},{20,12},{24,16},{28,20},{9,1},{13,5},{17,9},{2... | collective-permute-start | bytes 1572872 | tf_op jit(solution)/shard_map/ppermute | solution.py:339
  84.6 167.4 %all-gather.9.cloned.1.call-start = ((), (), s32[]{:S(2)}) async-start(), calls=%async_computation.7 | async-start | bytes 5242880 | tf_op jit(solution)/shard_map/all_gather | solution.py:425
  84.6 28.4 %collective-permute-start.5 = (f32[128,1024]{1,0:T(8,128)S(1)}, f32[128,1024]{1,0:T(8,128)S(1)}, u32[]{:S(2)}, u32[]{:S(2)}) collective-permute-start(f32[128,1024]{1,0:T(8,128)S(1)} %copy-done.8), channel_id=1, source_target_pairs={{8,0},{12,4},{16,8},{20,12},{24,16},{28,20},{9,1},{13,5},{17,9},{2... | collective-permute-start | bytes 1572872 | tf_op jit(solution)/shard_map/ppermute | solution.py:339
  86.0 27.1 %collective-permute-start.2 = (f32[128,1024]{1,0:T(8,128)S(1)}, f32[128,1024]{1,0:T(8,128)S(1)}, u32[]{:S(2)}, u32[]{:S(2)}) collective-permute-start(f32[128,1024]{1,0:T(8,128)S(1)} %copy-done.10), channel_id=1, source_target_pairs={{0,8},{4,12},{8,16},{12,20},{16,24},{20,28},{1,9},{5,13},{9,17},{1... | collective-permute-start | bytes 1572872 | tf_op jit(solution)/shard_map/ppermute | solution.py:338
  117.8 26.2 %collective-permute-start.8 = (f32[4,128,1024]{2,1,0:T(8,128)}, f32[4,128,1024]{2,1,0:T(8,128)S(1)}, u32[]{:S(2)}, u32[]{:S(2)}) collective-permute-start(f32[4,128,1024]{2,1,0:T(8,128)} %in_order.2.own), channel_id=1, source_target_pairs={{0,4},{4,0},{8,12},{12,8},{16,20},{20,16},{24,28},{28,24},{1,5},{5... | collective-permute-start | bytes 6291464 | tf_op jit(solution)/shard_map/ppermute | solution.py:413
  172.7 39.9 %collective-permute-start.19 = (f32[4,7,128,512]{3,2,1,0:T(8,128)}, f32[4,7,128,512]{3,2,1,0:T(8,128)}, u32[]{:S(2)}, u32[]{:S(2)}) collective-permute-start(f32[4,7,128,512]{3,2,1,0:T(8,128)} %gate.9.rest_0_.refs_5_.refs_6_.refs_4_), channel_id=1, source_target_pairs={{0,4},{4,0},{8,12},{12,8},{16,20},{20,16},{24,28},{28,24},{1,5},{5... | collective-permute-start | bytes 22020104 | tf_op jit(solution)/shard_map/ppermute | solution.py:413
  177.9 34.7 %collective-permute-start.14 = (f32[128,1024]{1,0:T(8,128)S(1)}, f32[128,1024]{1,0:T(8,128)S(1)}, u32[]{:S(2)}, u32[]{:S(2)}) collective-permute-start(f32[128,1024]{1,0:T(8,128)S(1)} %copy-done.45), channel_id=1, source_target_pairs={{0,3},{1,2},{2,1},{3,0},{4,7},{5,6},{6,5},{7,4},{8,11},{9,10},{10,... | collective-permute-start | bytes 1572872 | tf_op jit(solution)/shard_map/ppermute | solution.py:472
  226.6 54.3 %all-to-all-start = ((f32[8,128,512]{2,1,0:T(8,128)}), f32[8,128,512]{2,1,0:T(8,128)S(1)}, u32[]{:S(2)}, u32[]{:S(2)}) async-start(f32[8,128,512]{2,1,0:T(8,128)} %reduce_columns.6.rest_0_), calls=%async_computation | async-start | bytes 4194304 | tf_op jit(solution)/shard_map/all_to_all | solution.py:494
  231.8 29.8 %collective-permute-start.20 = (f32[128,1024]{1,0:T(8,128)}, f32[128,1024]{1,0:T(8,128)S(1)}, u32[]{:S(2)}, u32[]{:S(2)}) collective-permute-start(f32[128,1024]{1,0:T(8,128)} %get-tuple-element.40), channel_id=1, source_target_pairs={{0,1},{1,0},{2,3},{3,2},{4,5},{5,4},{6,7},{7,6},{8,9},{9,8},{10,11... | collective-permute-start | bytes 1572872 | tf_op jit(solution)/shard_map/ppermute | solution.py:472
  233.3 28.3 %collective-permute-start.21 = (f32[128,1024]{1,0:T(8,128)}, f32[128,1024]{1,0:T(8,128)S(1)}, u32[]{:S(2)}, u32[]{:S(2)}) collective-permute-start(f32[128,1024]{1,0:T(8,128)} %get-tuple-element.41), channel_id=1, source_target_pairs={{0,2},{1,3},{2,0},{3,1},{4,6},{5,7},{6,4},{7,5},{8,10},{9,11},{10,... | collective-permute-start | bytes 1572872 | tf_op jit(solution)/shard_map/ppermute | solution.py:472
  234.2 32.7 %collective-permute-start.22 = (f32[128,1024]{1,0:T(8,128)}, f32[128,1024]{1,0:T(8,128)}, u32[]{:S(2)}, u32[]{:S(2)}) collective-permute-start(f32[128,1024]{1,0:T(8,128)} %get-tuple-element.42), channel_id=1, source_target_pairs={{0,3},{1,2},{2,1},{3,0},{4,7},{5,6},{6,5},{7,4},{8,11},{9,10},{10,... | collective-permute-start | bytes 1572872 | tf_op jit(solution)/shard_map/ppermute | solution.py:472
  280.9 58.0 %all-to-all-start.1 = ((f32[8,128,512]{2,1,0:T(8,128)}), f32[8,128,512]{2,1,0:T(8,128)}, u32[]{:S(2)}, u32[]{:S(2)}) async-start(f32[8,128,512]{2,1,0:T(8,128)} %reduce_columns.7.rest_0_), calls=%async_computation.1 | async-start | bytes 4194304 | tf_op jit(solution)/shard_map/all_to_all | solution.py:494
  285.2 78.2 %all-gather.11.cloned.1.call-start = ((), (), s32[]{:S(2)}) async-start(), calls=%async_computation.8 | async-start | bytes 5242880 | tf_op jit(solution)/shard_map/all_gather | solution.py:425
  289.2 21.0 %collective-permute-start.24 = (f32[128,1024]{1,0:T(8,128)S(1)}, f32[128,1024]{1,0:T(8,128)S(1)}, u32[]{:S(2)}, u32[]{:S(2)}) collective-permute-start(f32[128,1024]{1,0:T(8,128)S(1)} %copy-done.42), channel_id=1, source_target_pairs={{0,2},{1,3},{2,0},{3,1},{4,6},{5,7},{6,4},{7,5},{8,10},{9,11},{10,... | collective-permute-start | bytes 1572872 | tf_op jit(solution)/shard_map/ppermute | solution.py:472
  290.0 34.9 %collective-permute-start.25 = (f32[128,1024]{1,0:T(8,128)S(1)}, f32[128,1024]{1,0:T(8,128)S(1)}, u32[]{:S(2)}, u32[]{:S(2)}) collective-permute-start(f32[128,1024]{1,0:T(8,128)S(1)} %copy-done.41), channel_id=1, source_target_pairs={{0,3},{1,2},{2,1},{3,0},{4,7},{5,6},{6,5},{7,4},{8,11},{9,10},{10,... | collective-permute-start | bytes 1572872 | tf_op jit(solution)/shard_map/ppermute | solution.py:472
  338.9 54.1 %all-to-all-start.2 = ((f32[8,128,512]{2,1,0:T(8,128)}), f32[8,128,512]{2,1,0:T(8,128)S(1)}, u32[]{:S(2)}, u32[]{:S(2)}) async-start(f32[8,128,512]{2,1,0:T(8,128)} %reduce_columns.8.rest_0_), calls=%async_computation.2 | async-start | bytes 4194304 | tf_op jit(solution)/shard_map/all_to_all | solution.py:494
  343.9 29.2 %collective-permute-start.26 = (f32[128,1024]{1,0:T(8,128)}, f32[128,1024]{1,0:T(8,128)S(1)}, u32[]{:S(2)}, u32[]{:S(2)}) collective-permute-start(f32[128,1024]{1,0:T(8,128)} %get-tuple-element.48), channel_id=1, source_target_pairs={{0,1},{1,0},{2,3},{3,2},{4,5},{5,4},{6,7},{7,6},{8,9},{9,8},{10,11... | collective-permute-start | bytes 1572872 | tf_op jit(solution)/shard_map/ppermute | solution.py:472
  345.4 27.8 %collective-permute-start.27 = (f32[128,1024]{1,0:T(8,128)}, f32[128,1024]{1,0:T(8,128)S(1)}, u32[]{:S(2)}, u32[]{:S(2)}) collective-permute-start(f32[128,1024]{1,0:T(8,128)} %get-tuple-element.49), channel_id=1, source_target_pairs={{0,2},{1,3},{2,0},{3,1},{4,6},{5,7},{6,4},{7,5},{8,10},{9,11},{10,... | collective-permute-start | bytes 1572872 | tf_op jit(solution)/shard_map/ppermute | solution.py:472
  346.6 32.0 %collective-permute-start.28 = (f32[128,1024]{1,0:T(8,128)}, f32[128,1024]{1,0:T(8,128)}, u32[]{:S(2)}, u32[]{:S(2)}) collective-permute-start(f32[128,1024]{1,0:T(8,128)} %get-tuple-element.50), channel_id=1, source_target_pairs={{0,3},{1,2},{2,1},{3,0},{4,7},{5,6},{6,5},{7,4},{8,11},{9,10},{10,... | collective-permute-start | bytes 1572872 | tf_op jit(solution)/shard_map/ppermute | solution.py:472
  393.0 53.5 %all-to-all-start.3 = ((f32[8,128,512]{2,1,0:T(8,128)}), f32[8,128,512]{2,1,0:T(8,128)}, u32[]{:S(2)}, u32[]{:S(2)}) async-start(f32[8,128,512]{2,1,0:T(8,128)} %reduce_columns.9.rest_0_), calls=%async_computation.3 | async-start | bytes 4194304 | tf_op jit(solution)/shard_map/all_to_all | solution.py:494
  398.9 25.3 %collective-permute-start.30 = (f32[128,1024]{1,0:T(8,128)}, f32[128,1024]{1,0:T(8,128)S(1)}, u32[]{:S(2)}, u32[]{:S(2)}) collective-permute-start(f32[128,1024]{1,0:T(8,128)} %get-tuple-element.53), channel_id=1, source_target_pairs={{0,2},{1,3},{2,0},{3,1},{4,6},{5,7},{6,4},{7,5},{8,10},{9,11},{10,... | collective-permute-start | bytes 1572872 | tf_op jit(solution)/shard_map/ppermute | solution.py:472
  400.1 24.1 %collective-permute-start.31 = (f32[128,1024]{1,0:T(8,128)}, f32[128,1024]{1,0:T(8,128)S(1)}, u32[]{:S(2)}, u32[]{:S(2)}) collective-permute-start(f32[128,1024]{1,0:T(8,128)} %get-tuple-element.54), channel_id=1, source_target_pairs={{0,3},{1,2},{2,1},{3,0},{4,7},{5,6},{6,5},{7,4},{8,11},{9,10},{10,... | collective-permute-start | bytes 1572872 | tf_op jit(solution)/shard_map/ppermute | solution.py:472
  446.4 53.7 %all-to-all-start.4 = ((f32[8,128,512]{2,1,0:T(8,128)}), f32[8,128,512]{2,1,0:T(8,128)}, u32[]{:S(2)}, u32[]{:S(2)}) async-start(f32[8,128,512]{2,1,0:T(8,128)} %reduce_columns.10), calls=%async_computation.4 | async-start | bytes 4194304 | tf_op jit(solution)/shard_map/all_to_all | solution.py:494
  452.6 25.2 %collective-permute-start.33 = (f32[128,1024]{1,0:T(8,128)S(1)}, f32[128,1024]{1,0:T(8,128)S(1)}, u32[]{:S(2)}, u32[]{:S(2)}) collective-permute-start(f32[128,1024]{1,0:T(8,128)S(1)} %copy-done.44), channel_id=1, source_target_pairs={{0,2},{1,3},{2,0},{3,1},{4,6},{5,7},{6,4},{7,5},{8,10},{9,11},{10,... | collective-permute-start | bytes 1572872 | tf_op jit(solution)/shard_map/ppermute | solution.py:472
  453.8 24.0 %collective-permute-start.34 = (f32[128,1024]{1,0:T(8,128)S(1)}, f32[128,1024]{1,0:T(8,128)S(1)}, u32[]{:S(2)}, u32[]{:S(2)}) collective-permute-start(f32[128,1024]{1,0:T(8,128)S(1)} %copy-done.43), channel_id=1, source_target_pairs={{0,3},{1,2},{2,1},{3,0},{4,7},{5,6},{6,5},{7,4},{8,11},{9,10},{10,... | collective-permute-start | bytes 1572872 | tf_op jit(solution)/shard_map/ppermute | solution.py:472
  500.1 53.4 %all-to-all-start.5 = ((f32[8,128,512]{2,1,0:T(8,128)}), f32[8,128,512]{2,1,0:T(8,128)}, u32[]{:S(2)}, u32[]{:S(2)}) async-start(f32[8,128,512]{2,1,0:T(8,128)} %reduce_columns.11), calls=%async_computation.5 | async-start | bytes 4194304 | tf_op jit(solution)/shard_map/all_to_all | solution.py:494
  (62 other events, 636.3 us)
Sparse Core Ops, SparseCore 0:
  9.2 55.3 all-gather.6
  84.7 87.9 all-gather.12
  175.4 76.5 all-gather.8
  287.8 75.6 all-gather.10

commit v4 on v3

--- a/solution.py
+++ b/solution.py
@@ -454,7 +454,8 @@
 
     def update(j):
         number = next(g for g, group in enumerate(groups) if j in group)
-        after = [done[j - AHEAD]] if j >= AHEAD else ready
+        after = [done[j - 1 if j == 4 else j - AHEAD]] if j >= AHEAD else ready
+        after = after + (updated[2][1][1:2] if j == 3 else [])
         out = update_rows(
             jnp.stack([col_index, own_block, is_top]),
             slab,
@@ -486,14 +487,18 @@
         pieces = updated[j][1]
         after = [updated[j + 1][0][0]] if j + 1 < len(updated) else []
         after += [results[j - 2]] if j >= 2 else []
+        after += factors[2:] if j == 3 else []
         done.append(
             reduce_columns(
                 place_cores, pieces, second_inverse, own_second, other_second, row_count, after
             )
         )
         results.append(lax.all_to_all(done[j], "rows", split_axis=0, concat_axis=0, tiled=True))
-        if j + AHEAD < chunks:
-            update(j + AHEAD)
+        stop = j + AHEAD + (1 if j != 2 else 0)
+        for later in range(len(updated), min(stop if j else AHEAD + 1, chunks)):
+            update(later)
+            if later == 2:
+                factors[2] = gather_factor(groups[2], updated[2][1][1:2])
     turned = jnp.concatenate(results, 1)
     return turned.reshape(row_count * piece, narrow)
 

time: 568 us -> 584 us (1.028)
  waiting for transfers between devices: 239 us -> 253 us
    ppermute x18, waiting for transfers between devices: 94.6 us -> 132 us  [update(): pieces.append(lax.ppermute(out[slot], 'cols', over_cols[slot]))]
    all_gather x3, waiting for transfers between devices: 32.6 us -> 16.4 us  [gather_factor(): part = lax.all_gather(part, 'cols', axis=1, tiled=True)]
    all_to_all x6, waiting for transfers between devices: 54.1 us -> 46.7 us  [on_device(): lax.all_to_all(done[j], 'rows', split_axis=0, concat_axis=0, tiled=True)]
    unnamed x103 -> x101, local copies, waits for them, and re-layouts: 23.8 us -> 24.8 us
  transfers between devices with their start and end apart: 45 -> 45, of which waited for: 30 -> 28; matrix products, arithmetic and copies ran while one was open for 4% -> 3% of each run, Pallas kernels for 28% -> 28%
where the time goes in v4:
time: 584 us; the launch traced here: 580 us
  waiting for transfers between devices  253 us (43%)
  Pallas kernels  168 us (29%)
  starting transfers between devices  91.2 us (16%)
  local copies, waits for them, and re-layouts  33 us (6%)
  blocking collectives  18.1 us (3%)
  between operations  13.8 us (2%)
    ppermute x18, waiting for transfers between devices, update(): pieces.append(lax.ppermute(out[slot], 'cols', over_cols[slot]))  132 us
    pallas_call x6, Pallas kernels, reduce_columns(): pl.pallas_call(functools.partial(reduce_kernel, slots, len(views), len(af...  79.4 us
    pallas_call x6, Pallas kernels, update_rows(): pl.pallas_call(functools.partial(update_kernel, tops, slots, offset), gri...  58.6 us
    all_to_all x6, waiting for transfers between devices, on_device(): lax.all_to_all(done[j], 'rows', split_axis=0, concat_axis=0, tiled=True)  46.7 us
    ppermute x6, waiting for transfers between devices, along_lines(): above[n].append(lax.ppermute(above[n][-1], 'rows', down))  31.3 us
    ppermute x6, starting transfers between devices, along_lines(): below[n].append(lax.ppermute(below[n][-1], 'rows', up))  28.8 us
    all_to_all x6, starting transfers between devices, on_device(): lax.all_to_all(done[j], 'rows', split_axis=0, concat_axis=0, tiled=True)  28.4 us
    unnamed x101, local copies, waits for them, and re-layouts  24.8 us
  transfers between devices with their start and end apart: 45, of which 28 were waited for; matrix products, arithmetic and copies ran while one was open for 3% of the time, Pallas kernels for 28%

profile of v4, /device:TPU:0, one launch (start us, length us, event | category | flops | bytes accessed | tf_op | source)
XLA Modules:
  0.0 579.9 jit_solution(13889424219421882460)
XLA Ops:
  11.2 5.6 collective-permute-start
  33.6 5.3 collective-permute-done.6.refs_0_
  51.6 8.9 %collective-permute-done.7.refs_0_ = f32[2,128,512]{2,1,0:T(8,128)S(1)} collective-permute-done((f32[2,128,512]{2,1,0:T(8,128)}, f32[2,128,512]{2,1,0:T(8,128)S(1)}, u32[]{:S(2)}, u32[]{:S(2)}) %collective-permute-start.7) | collective-permute-done | bytes 524320 | tf_op jit(solution)/shard_map/ppermute | solution.py:339
  68.1 8.6 %collective-permute-done.18.refs_6_ = f32[2,128,512]{2,1,0:T(8,128)S(1)} collective-permute-done((f32[2,128,512]{2,1,0:T(8,128)}, f32[2,128,512]{2,1,0:T(8,128)S(1)}, u32[]{:S(2)}, u32[]{:S(2)}) %collective-permute-start.18) | collective-permute-done | bytes 524320 | tf_op jit(solution)/shard_map/ppermute | solution.py:339
  94.1 18.1 %all-gather = f32[8,128,128]{2,1,0:T(8,128)S(1)} all-gather(f32[1,128,128]{2,1,0:T(8,128)} %pick_blocks.5), channel_id=2, replica_groups=mesh['rows'=8,'cols'=4] {'rows'}, dimensions={0}, use_global_device_ids=true | all-gather | bytes 589824 | tf_op jit(solution)/shard_map/all_gather | solution.py:437
  122.4 7.6 %collective-permute-done.11 = f32[4,1,128,128]{3,2,0,1:T(8,128)S(1)} collective-permute-done((f32[4,1,128,128]{3,2,0,1:T(8,128)S(1)}, f32[4,1,128,128]{3,2,0,1:T(8,128)S(1)}, u32[]{:S(2)}, u32[]{:S(2)}) %collective-permute-start.11) | collective-permute-done | bytes 262176 | tf_op jit(solution)/shard_map/ppermute | solution.py:441
  129.9 10.5 %collective-permute-done.9 = f32[4,1,128,128]{3,2,0,1:T(8,128)S(1)} collective-permute-done((f32[4,1,128,128]{3,2,0,1:T(8,128)S(1)}, f32[4,1,128,128]{3,2,0,1:T(8,128)S(1)}, u32[]{:S(2)}, u32[]{:S(2)}) %collective-permute-start.9) | collective-permute-done | bytes 262176 | tf_op jit(solution)/shard_map/ppermute | solution.py:441
  145.4 12.6 %solve_rows.1 = (f32[1024,1024]{1,0:T(8,128)}, bf16[1024,1024]{1,0:T(8,128)(2,1)}, bf16[1024,1024]{1,0:T(8,128)(2,1)}) custom-call(s32[1]{0:T(128)} %bitcast.1.place, f32[4,128,1024]{2,1,0:T(8,128)} %in_order.2.own, f32[4,128,1024]{2,1,0:T(8,128)} %copy-done.16, f32[2,512,512]{2,1,0:T(8,128)} %inverse_ref.1, f32[4,4,1,128,128]{4,3,2,1,0:T(8,128)} %bitcast.41), custom_call_target="tpu_custom_call" | custom-call | flops 4831838 | bytes 16777 | tf_op jit(solution)/shard_map/solve_rows/pallas_call | solution.py:100
  158.0 9.8 %update_rows.6 = (f32[128,1024]{1,0:T(8,128)}, f32[128,1024]{1,0:T(8,128)}, f32[128,1024]{1,0:T(8,128)}, f32[128,1024]{1,0:T(8,128)}) custom-call(s32[3]{0:T(128)} %pad_add_fusion.1.place, f32[4,768,1024]{2,1,0:T(8,128)} %bitcast.27, f32[1024,1024]{1,0:T(8,128)} %bitcast.34, bf16[1024,1024]{1,0:T(8,128)(2,1)} %get-tuple-element.32.high, ...), custom_call_target="tpu_custom_call" | custom-call | flops 6442450 | bytes 12582 | tf_op jit(solution)/shard_map/update_rows/pallas_call | solution.py:162
  179.6 9.8 %update_rows.7 = (f32[128,1024]{1,0:T(8,128)}, f32[128,1024]{1,0:T(8,128)}, f32[128,1024]{1,0:T(8,128)}, f32[128,1024]{1,0:T(8,128)}) custom-call(s32[3]{0:T(128)} %pad_add_fusion.1.place, f32[4,768,1024]{2,1,0:T(8,128)} %bitcast.28, f32[1024,1024]{1,0:T(8,128)} %bitcast.35, bf16[1024,1024]{1,0:T(8,128)(2,1)} %get-tuple-element.32.high, ...), custom_call_target="tpu_custom_call" | custom-call | flops 6442450 | bytes 12582 | tf_op jit(solution)/shard_map/update_rows/pallas_call | solution.py:162
  196.7 16.0 %collective-permute-done.14.refs_3_ = f32[128,1024]{1,0:T(8,128)S(1)} collective-permute-done((f32[128,1024]{1,0:T(8,128)S(1)}, f32[128,1024]{1,0:T(8,128)S(1)}, u32[]{:S(2)}, u32[]{:S(2)}) %collective-permute-start.14) | collective-permute-done | bytes 524320 | tf_op jit(solution)/shard_map/ppermute | solution.py:473
  213.5 13.3 %reduce_columns.6.rest_0_ = f32[8,128,512]{2,1,0:T(8,128)} custom-call(s32[2]{0:T(128)} %pad_add_fusion.place, f32[128,1024]{1,0:T(8,128)} %get-tuple-element.35.refs_1_.refs_0_, f32[128,1024]{1,0:T(8,128)} %copy-done.18, f32[128,1024]{1,0:T(8,128)} %copy-done.20, f32[128,1024]{1,0:T(8,128)} %copy-done.24, f32[2,512,512]{2,1,0:T(8,128)} %refs_4_.11, ...), custom_call_target="tpu_custom_call" | custom-call | flops 3221225 | bytes 16777 | tf_op jit(solution)/shard_map/reduce_columns/pallas_call | solution.py:266
  226.8 5.3 all-to-all-start
  235.6 16.4 %all-gather.9.cloned.1.call-done = f32[2,512,1024]{2,1,0:T(8,128)} async-done(((f32[2,128,1024]{2,1,0:T(8,128)}), f32[2,512,1024]{2,1,0:T(8,128)}) %all-gather.9.cloned.1.call-update) | async-done | bytes 4194320 | tf_op jit(solution)/shard_map/all_gather | solution.py:425
  252.0 9.7 %update_rows.8 = (f32[128,1024]{1,0:T(8,128)}, f32[128,1024]{1,0:T(8,128)}, f32[128,1024]{1,0:T(8,128)}, f32[128,1024]{1,0:T(8,128)}) custom-call(s32[3]{0:T(128)} %pad_add_fusion.1.place, f32[4,768,1024]{2,1,0:T(8,128)} %bitcast.29, f32[1024,1024]{1,0:T(8,128)} %bitcast.39, bf16[1024,1024]{1,0:T(8,128)(2,1)} %get-tuple-element.32.high, ...), custom_call_target="tpu_custom_call" | custom-call | flops 6442450 | bytes 12582 | tf_op jit(solution)/shard_map/update_rows/pallas_call | solution.py:162
  267.0 13.3 %reduce_columns.7.rest_0_ = f32[8,128,512]{2,1,0:T(8,128)} custom-call(s32[2]{0:T(128)} %pad_add_fusion.place, f32[128,1024]{1,0:T(8,128)} %get-tuple-element.39.refs_9_.refs_0_, f32[128,1024]{1,0:T(8,128)} %copy-done.21, f32[128,1024]{1,0:T(8,128)} %copy-done.23, f32[128,1024]{1,0:T(8,128)} %collective-permute-done.22.refs_3_, f32[2,512,512]{2,1,0:T(8,128)} %refs_4_.11, ...), custom_call_target="tpu_custom_call" | custom-call | flops 3221225 | bytes 16777 | tf_op jit(solution)/shard_map/reduce_columns/pallas_call | solution.py:266
  287.0 12.9 %collective-permute-done.23.rest_1_.refs_1_.refs_4_ = f32[128,1024]{1,0:T(8,128)S(1)} collective-permute-done((f32[128,1024]{1,0:T(8,128)}, f32[128,1024]{1,0:T(8,128)S(1)}, u32[]{:S(2)}, u32[]{:S(2)}) %collective-permute-start.23) | collective-permute-done | bytes 524320 | tf_op jit(solution)/shard_map/ppermute | solution.py:473
  306.0 9.9 %update_rows.9 = (f32[128,1024]{1,0:T(8,128)}, f32[128,1024]{1,0:T(8,128)}, f32[128,1024]{1,0:T(8,128)}, f32[128,1024]{1,0:T(8,128)}) custom-call(s32[3]{0:T(128)} %pad_add_fusion.1.place, f32[4,768,1024]{2,1,0:T(8,128)} %bitcast.30, f32[1024,1024]{1,0:T(8,128)} %bitcast.40, bf16[1024,1024]{1,0:T(8,128)(2,1)} %get-tuple-element.32.high, ...), custom_call_target="tpu_custom_call" | custom-call | flops 6442450 | bytes 12582 | tf_op jit(solution)/shard_map/update_rows/pallas_call | solution.py:162
  315.8 23.3 %collective-permute-done.24.refs_2_ = f32[128,1024]{1,0:T(8,128)S(1)} collective-permute-done((f32[128,1024]{1,0:T(8,128)}, f32[128,1024]{1,0:T(8,128)S(1)}, u32[]{:S(2)}, u32[]{:S(2)}) %collective-permute-start.24) | collective-permute-done | bytes 524320 | tf_op jit(solution)/shard_map/ppermute | solution.py:473
  340.1 13.2 %reduce_columns.8 = f32[8,128,512]{2,1,0:T(8,128)} custom-call(s32[2]{0:T(128)} %pad_add_fusion.place, f32[128,1024]{1,0:T(8,128)} %get-tuple-element.43.refs_9_.refs_0_, f32[128,1024]{1,0:T(8,128)} %copy-done.4, f32[128,1024]{1,0:T(8,128)} %copy-done.30, f32[128,1024]{1,0:T(8,128)} %copy-done.32, f32[2,512,512]{2,1,0:T(8,128)} %refs_4_.11, ...), custom_call_target="tpu_custom_call" | custom-call | flops 3221225 | bytes 16777 | tf_op jit(solution)/shard_map/reduce_columns/pallas_call | solution.py:266
  361.7 19.1 %collective-permute-done.26.refs_1_ = f32[128,1024]{1,0:T(8,128)S(1)} collective-permute-done((f32[128,1024]{1,0:T(8,128)}, f32[128,1024]{1,0:T(8,128)S(1)}, u32[]{:S(2)}, u32[]{:S(2)}) %collective-permute-start.26) | collective-permute-done | bytes 524320 | tf_op jit(solution)/shard_map/ppermute | solution.py:473
  380.8 12.1 %collective-permute-done.28.refs_3_ = f32[128,1024]{1,0:T(8,128)} collective-permute-done((f32[128,1024]{1,0:T(8,128)}, f32[128,1024]{1,0:T(8,128)}, u32[]{:S(2)}, u32[]{:S(2)}) %collective-permute-start.28) | collective-permute-done | bytes 524320 | tf_op jit(solution)/shard_map/ppermute | solution.py:473
  392.9 13.2 %reduce_columns.9.rest_0_ = f32[8,128,512]{2,1,0:T(8,128)} custom-call(s32[2]{0:T(128)} %pad_add_fusion.place, f32[128,1024]{1,0:T(8,128)} %get-tuple-element.47.refs_9_.refs_0_, f32[128,1024]{1,0:T(8,128)} %copy-done.25, f32[128,1024]{1,0:T(8,128)} %copy-done.28, f32[128,1024]{1,0:T(8,128)} %collective-permute-done.28.refs_3_, f32[2,512,512]{2,1,0:T(8,128)} %refs_4_.11, ...), custom_call_target="tpu_custom_call" | custom-call | flops 3221225 | bytes 16777 | tf_op jit(solution)/shard_map/reduce_columns/pallas_call | solution.py:266
  411.5 9.7 %update_rows.10 = (f32[128,1024]{1,0:T(8,128)}, f32[128,1024]{1,0:T(8,128)}, f32[128,1024]{1,0:T(8,128)}, f32[128,1024]{1,0:T(8,128)}) custom-call(s32[3]{0:T(128)} %pad_add_fusion.1.place, f32[4,768,1024]{2,1,0:T(8,128)} %bitcast.31, f32[1024,1024]{1,0:T(8,128)} %bitcast.37, bf16[1024,1024]{1,0:T(8,128)(2,1)} %get-tuple-element.32.high, ...), custom_call_target="tpu_custom_call" | custom-call | flops 6442450 | bytes 12582 | tf_op jit(solution)/shard_map/update_rows/pallas_call | solution.py:162
  424.8 9.7 %update_rows.11 = (f32[128,1024]{1,0:T(8,128)}, f32[128,1024]{1,0:T(8,128)}, f32[128,1024]{1,0:T(8,128)}, f32[128,1024]{1,0:T(8,128)}) custom-call(s32[3]{0:T(128)} %pad_add_fusion.1.place, f32[4,768,1024]{2,1,0:T(8,128)} %bitcast.32, f32[1024,1024]{1,0:T(8,128)} %bitcast.38, bf16[1024,1024]{1,0:T(8,128)(2,1)} %get-tuple-element.32.high, ...), custom_call_target="tpu_custom_call" | custom-call | flops 6442450 | bytes 12582 | tf_op jit(solution)/shard_map/update_rows/pallas_call | solution.py:162
  436.3 11.7 %collective-permute-done.30.refs_2_ = f32[128,1024]{1,0:T(8,128)S(1)} collective-permute-done((f32[128,1024]{1,0:T(8,128)}, f32[128,1024]{1,0:T(8,128)S(1)}, u32[]{:S(2)}, u32[]{:S(2)}) %collective-permute-start.30) | collective-permute-done | bytes 524320 | tf_op jit(solution)/shard_map/ppermute | solution.py:473
  449.0 13.2 %reduce_columns.10 = f32[8,128,512]{2,1,0:T(8,128)} custom-call(s32[2]{0:T(128)} %pad_add_fusion.place, f32[128,1024]{1,0:T(8,128)} %get-tuple-element.51.refs_0_, f32[128,1024]{1,0:T(8,128)} %copy-done.19, f32[128,1024]{1,0:T(8,128)} %copy-done.22, f32[128,1024]{1,0:T(8,128)} %copy-done.26, f32[2,512,512]{2,1,0:T(8,128)} %refs_4_.11, ...), custom_call_target="tpu_custom_call" | custom-call | flops 3221225 | bytes 16777 | tf_op jit(solution)/shard_map/reduce_columns/pallas_call | solution.py:266
  471.1 11.2 %collective-permute-done.32.refs_1_ = f32[128,1024]{1,0:T(8,128)S(1)} collective-permute-done((f32[128,1024]{1,0:T(8,128)S(1)}, f32[128,1024]{1,0:T(8,128)S(1)}, u32[]{:S(2)}, u32[]{:S(2)}) %collective-permute-start.32) | collective-permute-done | bytes 524320 | tf_op jit(solution)/shard_map/ppermute | solution.py:473
  482.3 11.2 %collective-permute-done.33.refs_2_ = f32[128,1024]{1,0:T(8,128)S(1)} collective-permute-done((f32[128,1024]{1,0:T(8,128)S(1)}, f32[128,1024]{1,0:T(8,128)S(1)}, u32[]{:S(2)}, u32[]{:S(2)}) %collective-permute-start.33) | collective-permute-done | bytes 524320 | tf_op jit(solution)/shard_map/ppermute | solution.py:473
  495.1 13.3 %reduce_columns.11 = f32[8,128,512]{2,1,0:T(8,128)} custom-call(s32[2]{0:T(128)} %pad_add_fusion.place, f32[128,1024]{1,0:T(8,128)} %get-tuple-element.55.refs_9_.refs_0_, f32[128,1024]{1,0:T(8,128)} %copy-done.27, f32[128,1024]{1,0:T(8,128)} %copy-done.29, f32[128,1024]{1,0:T(8,128)} %copy-done.31, f32[2,512,512]{2,1,0:T(8,128)} %refs_4_.11, ...), custom_call_target="tpu_custom_call" | custom-call | flops 3221225 | bytes 16777 | tf_op jit(solution)/shard_map/reduce_columns/pallas_call | solution.py:266
  508.4 8.2 %all-to-all-done.4 = f32[8,128,512]{2,1,0:T(8,128)} async-done(((f32[8,128,512]{2,1,0:T(8,128)}), f32[8,128,512]{2,1,0:T(8,128)}, u32[]{:S(2)}, u32[]{:S(2)}) %all-to-all-start.4) | async-done | bytes 2097184 | tf_op jit(solution)/shard_map/all_to_all | solution.py:496
  533.4 36.6 %all-to-all-done.5 = f32[8,128,512]{2,1,0:T(8,128)} async-done(((f32[8,128,512]{2,1,0:T(8,128)}), f32[8,128,512]{2,1,0:T(8,128)}, u32[]{:S(2)}, u32[]{:S(2)}) %all-to-all-start.5) | async-done | bytes 2097184 | tf_op jit(solution)/shard_map/all_to_all | solution.py:496
  (198 shorter events, 166.9 us)
Async XLA Ops:
  6.5 72.2 %all-gather.7.cloned.1.call-start = ((), (), s32[]{:S(2)}) async-start(), calls=%async_computation.6 | async-start | bytes 5242880 | tf_op jit(solution)/shard_map/all_gather | solution.py:425
  8.8 164.1 %all-gather.13.cloned.1.call-start = ((), (), s32[]{:S(2)}) async-start(), calls=%async_computation.9 | async-start | bytes 9175040 | tf_op jit(solution)/shard_map/all_gather | solution.py:434
  16.8 22.0 %collective-permute-start.6 = (f32[2,128,512]{2,1,0:T(8,128)}, f32[2,128,512]{2,1,0:T(8,128)S(1)}, u32[]{:S(2)}, u32[]{:S(2)}) collective-permute-start(f32[2,128,512]{2,1,0:T(8,128)} %refs_3_.5), channel_id=1, source_target_pairs={{8,0},{12,4},{16,8},{20,12},{24,16},{28,20},{9,1},{13,5},{17,9},{2... | collective-permute-start | bytes 1572872 | tf_op jit(solution)/shard_map/ppermute | solution.py:339
  18.1 22.8 %collective-permute-start.15 = (f32[2,128,512]{2,1,0:T(8,128)}, f32[2,128,512]{2,1,0:T(8,128)S(1)}, u32[]{:S(2)}, u32[]{:S(2)}) collective-permute-start(f32[2,128,512]{2,1,0:T(8,128)} %refs_3_.5), channel_id=1, source_target_pairs={{0,8},{4,12},{8,16},{12,20},{16,24},{20,28},{1,9},{5,13},{9,17},{1... | collective-permute-start | bytes 1572872 | tf_op jit(solution)/shard_map/ppermute | solution.py:338
  27.6 22.5 %collective-permute-start.4 = (f32[128,1024]{1,0:T(8,128)S(1)}, f32[128,1024]{1,0:T(8,128)S(1)}, u32[]{:S(2)}, u32[]{:S(2)}) collective-permute-start(f32[128,1024]{1,0:T(8,128)S(1)} %collective-permute-done.3.refs_2_.refs_4_), channel_id=1, source_target_pairs={{8,0},{12,4},{16,8},{20,12},{24,16},{28,20},{9,1},{13,5},{17,9},{2... | collective-permute-start | bytes 1572872 | tf_op jit(solution)/shard_map/ppermute | solution.py:339
  29.1 22.5 %collective-permute-start.1 = (f32[128,1024]{1,0:T(8,128)S(1)}, f32[128,1024]{1,0:T(8,128)S(1)}, u32[]{:S(2)}, u32[]{:S(2)}) collective-permute-start(f32[128,1024]{1,0:T(8,128)S(1)} %collective-permute-done.refs_1_.refs_2_), channel_id=1, source_target_pairs={{0,8},{4,12},{8,16},{12,20},{16,24},{20,28},{1,9},{5,13},{9,17},{1... | collective-permute-start | bytes 1572872 | tf_op jit(solution)/shard_map/ppermute | solution.py:338
  39.6 20.8 %collective-permute-start.7 = (f32[2,128,512]{2,1,0:T(8,128)}, f32[2,128,512]{2,1,0:T(8,128)S(1)}, u32[]{:S(2)}, u32[]{:S(2)}) collective-permute-start(f32[2,128,512]{2,1,0:T(8,128)} %gate.5.refs_4_), channel_id=1, source_target_pairs={{8,0},{12,4},{16,8},{20,12},{24,16},{28,20},{9,1},{13,5},{17,9},{2... | collective-permute-start | bytes 1572872 | tf_op jit(solution)/shard_map/ppermute | solution.py:339
  84.7 167.3 %all-gather.9.cloned.1.call-start = ((), (), s32[]{:S(2)}) async-start(), calls=%async_computation.7 | async-start | bytes 5242880 | tf_op jit(solution)/shard_map/all_gather | solution.py:425
  84.8 28.3 %collective-permute-start.5 = (f32[128,1024]{1,0:T(8,128)S(1)}, f32[128,1024]{1,0:T(8,128)S(1)}, u32[]{:S(2)}, u32[]{:S(2)}) collective-permute-start(f32[128,1024]{1,0:T(8,128)S(1)} %copy-done.9), channel_id=1, source_target_pairs={{8,0},{12,4},{16,8},{20,12},{24,16},{28,20},{9,1},{13,5},{17,9},{2... | collective-permute-start | bytes 1572872 | tf_op jit(solution)/shard_map/ppermute | solution.py:339
  86.1 27.0 %collective-permute-start.2 = (f32[128,1024]{1,0:T(8,128)S(1)}, f32[128,1024]{1,0:T(8,128)S(1)}, u32[]{:S(2)}, u32[]{:S(2)}) collective-permute-start(f32[128,1024]{1,0:T(8,128)S(1)} %copy-done.11), channel_id=1, source_target_pairs={{0,8},{4,12},{8,16},{12,20},{16,24},{20,28},{1,9},{5,13},{9,17},{1... | collective-permute-start | bytes 1572872 | tf_op jit(solution)/shard_map/ppermute | solution.py:338
  118.0 26.1 %collective-permute-start.8 = (f32[4,128,1024]{2,1,0:T(8,128)}, f32[4,128,1024]{2,1,0:T(8,128)S(1)}, u32[]{:S(2)}, u32[]{:S(2)}) collective-permute-start(f32[4,128,1024]{2,1,0:T(8,128)} %in_order.2.own), channel_id=1, source_target_pairs={{0,4},{4,0},{8,12},{12,8},{16,20},{20,16},{24,28},{28,24},{1,5},{5... | collective-permute-start | bytes 6291464 | tf_op jit(solution)/shard_map/ppermute | solution.py:413
  172.9 39.8 %collective-permute-start.19 = (f32[4,7,128,512]{3,2,1,0:T(8,128)}, f32[4,7,128,512]{3,2,1,0:T(8,128)}, u32[]{:S(2)}, u32[]{:S(2)}) collective-permute-start(f32[4,7,128,512]{3,2,1,0:T(8,128)} %gate.9.rest_0_.refs_5_.refs_6_.refs_4_), channel_id=1, source_target_pairs={{0,4},{4,0},{8,12},{12,8},{16,20},{20,16},{24,28},{28,24},{1,5},{5... | collective-permute-start | bytes 22020104 | tf_op jit(solution)/shard_map/ppermute | solution.py:413
  178.1 34.6 %collective-permute-start.14 = (f32[128,1024]{1,0:T(8,128)S(1)}, f32[128,1024]{1,0:T(8,128)S(1)}, u32[]{:S(2)}, u32[]{:S(2)}) collective-permute-start(f32[128,1024]{1,0:T(8,128)S(1)} %copy-done.44), channel_id=1, source_target_pairs={{0,3},{1,2},{2,1},{3,0},{4,7},{5,6},{6,5},{7,4},{8,11},{9,10},{10,... | collective-permute-start | bytes 1572872 | tf_op jit(solution)/shard_map/ppermute | solution.py:473
  226.8 54.3 %all-to-all-start = ((f32[8,128,512]{2,1,0:T(8,128)}), f32[8,128,512]{2,1,0:T(8,128)S(1)}, u32[]{:S(2)}, u32[]{:S(2)}) async-start(f32[8,128,512]{2,1,0:T(8,128)} %reduce_columns.6.rest_0_), calls=%async_computation | async-start | bytes 4194304 | tf_op jit(solution)/shard_map/all_to_all | solution.py:496
  232.1 29.7 %collective-permute-start.20 = (f32[128,1024]{1,0:T(8,128)}, f32[128,1024]{1,0:T(8,128)S(1)}, u32[]{:S(2)}, u32[]{:S(2)}) collective-permute-start(f32[128,1024]{1,0:T(8,128)} %get-tuple-element.40), channel_id=1, source_target_pairs={{0,1},{1,0},{2,3},{3,2},{4,5},{5,4},{6,7},{7,6},{8,9},{9,8},{10,11... | collective-permute-start | bytes 1572872 | tf_op jit(solution)/shard_map/ppermute | solution.py:473
  233.6 28.2 %collective-permute-start.21 = (f32[128,1024]{1,0:T(8,128)}, f32[128,1024]{1,0:T(8,128)S(1)}, u32[]{:S(2)}, u32[]{:S(2)}) collective-permute-start(f32[128,1024]{1,0:T(8,128)} %get-tuple-element.41), channel_id=1, source_target_pairs={{0,2},{1,3},{2,0},{3,1},{4,6},{5,7},{6,4},{7,5},{8,10},{9,11},{10,... | collective-permute-start | bytes 1572872 | tf_op jit(solution)/shard_map/ppermute | solution.py:473
  234.3 32.7 %collective-permute-start.22 = (f32[128,1024]{1,0:T(8,128)}, f32[128,1024]{1,0:T(8,128)}, u32[]{:S(2)}, u32[]{:S(2)}) collective-permute-start(f32[128,1024]{1,0:T(8,128)} %get-tuple-element.42), channel_id=1, source_target_pairs={{0,3},{1,2},{2,1},{3,0},{4,7},{5,6},{6,5},{7,4},{8,11},{9,10},{10,... | collective-permute-start | bytes 1572872 | tf_op jit(solution)/shard_map/ppermute | solution.py:473
  281.1 72.2 %all-to-all-start.1 = ((f32[8,128,512]{2,1,0:T(8,128)}), f32[8,128,512]{2,1,0:T(8,128)}, u32[]{:S(2)}, u32[]{:S(2)}) async-start(f32[8,128,512]{2,1,0:T(8,128)} %reduce_columns.7.rest_0_), calls=%async_computation.1 | async-start | bytes 4194304 | tf_op jit(solution)/shard_map/all_to_all | solution.py:496
  285.4 107.5 %all-gather.11.cloned.1.call-start = ((), (), s32[]{:S(2)}) async-start(), calls=%async_computation.8 | async-start | bytes 5242880 | tf_op jit(solution)/shard_map/all_gather | solution.py:425
  303.0 36.2 %collective-permute-start.24 = (f32[128,1024]{1,0:T(8,128)}, f32[128,1024]{1,0:T(8,128)S(1)}, u32[]{:S(2)}, u32[]{:S(2)}) collective-permute-start(f32[128,1024]{1,0:T(8,128)} %get-tuple-element.45), channel_id=1, source_target_pairs={{0,2},{1,3},{2,0},{3,1},{4,6},{5,7},{6,4},{7,5},{8,10},{9,11},{10,... | collective-permute-start | bytes 1572872 | tf_op jit(solution)/shard_map/ppermute | solution.py:473
  303.8 35.4 %collective-permute-start.25 = (f32[128,1024]{1,0:T(8,128)S(1)}, f32[128,1024]{1,0:T(8,128)S(1)}, u32[]{:S(2)}, u32[]{:S(2)}) collective-permute-start(f32[128,1024]{1,0:T(8,128)S(1)} %copy-done.41), channel_id=1, source_target_pairs={{0,3},{1,2},{2,1},{3,0},{4,7},{5,6},{6,5},{7,4},{8,11},{9,10},{10,... | collective-permute-start | bytes 1572872 | tf_op jit(solution)/shard_map/ppermute | solution.py:473
  353.3 53.9 %all-to-all-start.2 = ((f32[8,128,512]{2,1,0:T(8,128)}), f32[8,128,512]{2,1,0:T(8,128)S(1)}, u32[]{:S(2)}, u32[]{:S(2)}) async-start(f32[8,128,512]{2,1,0:T(8,128)} %reduce_columns.8), calls=%async_computation.2 | async-start | bytes 4194304 | tf_op jit(solution)/shard_map/all_to_all | solution.py:496
  358.1 22.7 %collective-permute-start.26 = (f32[128,1024]{1,0:T(8,128)}, f32[128,1024]{1,0:T(8,128)S(1)}, u32[]{:S(2)}, u32[]{:S(2)}) collective-permute-start(f32[128,1024]{1,0:T(8,128)} %get-tuple-element.48), channel_id=1, source_target_pairs={{0,1},{1,0},{2,3},{3,2},{4,5},{5,4},{6,7},{7,6},{8,9},{9,8},{10,11... | collective-permute-start | bytes 1572872 | tf_op jit(solution)/shard_map/ppermute | solution.py:473
  359.6 21.3 %collective-permute-start.27 = (f32[128,1024]{1,0:T(8,128)}, f32[128,1024]{1,0:T(8,128)S(1)}, u32[]{:S(2)}, u32[]{:S(2)}) collective-permute-start(f32[128,1024]{1,0:T(8,128)} %get-tuple-element.49), channel_id=1, source_target_pairs={{0,2},{1,3},{2,0},{3,1},{4,6},{5,7},{6,4},{7,5},{8,10},{9,11},{10,... | collective-permute-start | bytes 1572872 | tf_op jit(solution)/shard_map/ppermute | solution.py:473
  360.2 32.7 %collective-permute-start.28 = (f32[128,1024]{1,0:T(8,128)}, f32[128,1024]{1,0:T(8,128)}, u32[]{:S(2)}, u32[]{:S(2)}) collective-permute-start(f32[128,1024]{1,0:T(8,128)} %get-tuple-element.50), channel_id=1, source_target_pairs={{0,3},{1,2},{2,1},{3,0},{4,7},{5,6},{6,5},{7,4},{8,11},{9,10},{10,... | collective-permute-start | bytes 1572872 | tf_op jit(solution)/shard_map/ppermute | solution.py:473
  407.2 55.1 %all-to-all-start.3 = ((f32[8,128,512]{2,1,0:T(8,128)}), f32[8,128,512]{2,1,0:T(8,128)}, u32[]{:S(2)}, u32[]{:S(2)}) async-start(f32[8,128,512]{2,1,0:T(8,128)} %reduce_columns.9.rest_0_), calls=%async_computation.3 | async-start | bytes 4194304 | tf_op jit(solution)/shard_map/all_to_all | solution.py:496
  422.7 25.3 %collective-permute-start.30 = (f32[128,1024]{1,0:T(8,128)}, f32[128,1024]{1,0:T(8,128)S(1)}, u32[]{:S(2)}, u32[]{:S(2)}) collective-permute-start(f32[128,1024]{1,0:T(8,128)} %get-tuple-element.53), channel_id=1, source_target_pairs={{0,2},{1,3},{2,0},{3,1},{4,6},{5,7},{6,4},{7,5},{8,10},{9,11},{10,... | collective-permute-start | bytes 1572872 | tf_op jit(solution)/shard_map/ppermute | solution.py:473
  423.3 24.7 %collective-permute-start.31 = (f32[128,1024]{1,0:T(8,128)}, f32[128,1024]{1,0:T(8,128)S(1)}, u32[]{:S(2)}, u32[]{:S(2)}) collective-permute-start(f32[128,1024]{1,0:T(8,128)} %get-tuple-element.54), channel_id=1, source_target_pairs={{0,3},{1,2},{2,1},{3,0},{4,7},{5,6},{6,5},{7,4},{8,11},{9,10},{10,... | collective-permute-start | bytes 1572872 | tf_op jit(solution)/shard_map/ppermute | solution.py:473
  462.3 54.3 %all-to-all-start.4 = ((f32[8,128,512]{2,1,0:T(8,128)}), f32[8,128,512]{2,1,0:T(8,128)}, u32[]{:S(2)}, u32[]{:S(2)}) async-start(f32[8,128,512]{2,1,0:T(8,128)} %reduce_columns.10), calls=%async_computation.4 | async-start | bytes 4194304 | tf_op jit(solution)/shard_map/all_to_all | solution.py:496
  468.2 25.3 %collective-permute-start.33 = (f32[128,1024]{1,0:T(8,128)S(1)}, f32[128,1024]{1,0:T(8,128)S(1)}, u32[]{:S(2)}, u32[]{:S(2)}) collective-permute-start(f32[128,1024]{1,0:T(8,128)S(1)} %copy-done.43), channel_id=1, source_target_pairs={{0,2},{1,3},{2,0},{3,1},{4,6},{5,7},{6,4},{7,5},{8,10},{9,11},{10,... | collective-permute-start | bytes 1572872 | tf_op jit(solution)/shard_map/ppermute | solution.py:473
  469.1 24.4 %collective-permute-start.34 = (f32[128,1024]{1,0:T(8,128)S(1)}, f32[128,1024]{1,0:T(8,128)S(1)}, u32[]{:S(2)}, u32[]{:S(2)}) collective-permute-start(f32[128,1024]{1,0:T(8,128)S(1)} %copy-done.42), channel_id=1, source_target_pairs={{0,3},{1,2},{2,1},{3,0},{4,7},{5,6},{6,5},{7,4},{8,11},{9,10},{10,... | collective-permute-start | bytes 1572872 | tf_op jit(solution)/shard_map/ppermute | solution.py:473
  516.6 53.4 %all-to-all-start.5 = ((f32[8,128,512]{2,1,0:T(8,128)}), f32[8,128,512]{2,1,0:T(8,128)}, u32[]{:S(2)}, u32[]{:S(2)}) async-start(f32[8,128,512]{2,1,0:T(8,128)} %reduce_columns.11), calls=%async_computation.5 | async-start | bytes 4194304 | tf_op jit(solution)/shard_map/all_to_all | solution.py:496
  (61 other events, 610.9 us)
Sparse Core Ops, SparseCore 0:
  9.2 55.3 all-gather.6
  84.8 87.9 all-gather.12
  175.5 76.4 all-gather.8
  303.1 74.5 all-gather.10
